TPU v7x, 256 devices: a whole 4x4x8 slice. The times are simulated.
256 devices in a mesh: look: 32 (over y_lo, z, core), swath: 8 (over y_hi, x).
Axes of the slice: x: 4, y: 4 (y_hi: 2, y_lo: 2; y = y_hi * 2 + y_lo), z: 8, core: 2. Of those that a mesh axis runs over, the one named last changes fastest.
Arguments:
- images: bfloat16 [64, 32, 2, 512, 512], P('look', 'swath'), may hold values from -6 to 6
- patch_weight: float32 [32], P('swath'), may hold values from 1 to 10
- pair_mask: int32 [64, 4], P('look'), may hold values 0 or 1
Outputs:
- drift: float32 [64, 4, 256, 256], P('look', None, 'swath')
All inputs are finite; a program needn't handle non-finite values. No bound on the sum of `pair_mask` on one device may be relied on, other than what follows from the above.
Results may differ from a plain program's by a relative error of at most 0.015.
Values may be sent and summed in bfloat16 or wider, within the bound.
No kernel may reach another device: no remote copies, remote signals or barrier semaphores. Data moves between devices by JAX's collectives and lax.ppermute only.
A program may use at most 128 MiB of HBM per device.

v0:
```python
import functools
import math

import jax
import jax.numpy as jnp
import numpy as np
from jax import lax
from jax.experimental import pallas as pl
from jax.experimental.pallas import tpu as pltpu
from jax.sharding import PartitionSpec as P

PIX = 512
BAND = 256
WIN = 256
HALF = 256
CHUNK = 2
EROWS = 16
TABLES = 32
REST_LIMIT = 52
BF = jnp.bfloat16
F32 = jnp.float32


def phases(rows, cols):
    phase = (rows[:, None] * cols[None, :]) % PIX
    angle = (2.0 * math.pi / PIX * phase.astype(np.float32)).astype(np.float32)
    return np.cos(angle), np.sin(angle)


def make_tables():
    order = np.concatenate([np.arange(0, BAND, 2), np.arange(1, BAND, 2)])
    n0 = np.arange(HALF)
    left = []
    for parity in range(2):
        ks = np.arange(parity, BAND, 2) - BAND // 2
        re, im = phases(ks, n0)
        im = -im
        left.append(np.block([[re, -im], [im, re]]))
    ts = np.arange(WIN) - WIN // 2
    gre, gim = phases(ts, order - BAND // 2)
    first = np.block([[gre, -gim], [gim, gre]])
    second = np.concatenate([gre, -gim], axis=1)
    cast = lambda a: jnp.asarray(np.asarray(a, np.float32).astype(jnp.bfloat16))
    room = np.zeros((TABLES - 2, 256, 512))
    return cast(np.concatenate([np.stack(left), room])), cast(np.stack([first[:256], first[256:], second]))


def place():
    look = lax.axis_index("look")
    swath = lax.axis_index("swath")
    nlook = lax.axis_size("look")
    return dict(
        lo=(look >= nlook // 2).astype(jnp.int32),
        zero=look == 0,
        last=look == nlook - 1,
        x=lax.rem(swath, 4),
        yh=swath // 4,
    )


def dot(a, b):
    return jnp.dot(a, b, preferred_element_type=F32)


def dot_nt(a, b):
    return lax.dot_general(a, b, (((1,), (1,)), ((), ())), preferred_element_type=F32)


def butterflies(x):
    x00 = x[:HALF, :HALF].astype(F32)
    x01 = x[:HALF, HALF:].astype(F32)
    x10 = x[HALF:, :HALF].astype(F32)
    x11 = x[HALF:, HALF:].astype(F32)
    a, b = x00 + x10, x01 + x11
    c, d = x00 - x10, x01 - x11
    return [v.astype(BF) for v in (a + b, a - b, c + d, c - d)]


def image_pair(xbuf, at, tab, hbuf, ybuf, store):
    for k in range(2):
        for part in range(2):
            for q, h in enumerate(butterflies(xbuf.at[at + k, part])):
                kp, lp = q // 2, q % 2
                row = 512 * k + 256 * kp
                hbuf[lp, row : row + 256, 256 * part : 256 * part + 256] = h
    for lp in range(2):
        y = dot_nt(hbuf[lp], tab[lp]).astype(BF)
        for k in range(2):
            for kp in range(2):
                block = y[512 * k + 256 * kp : 512 * k + 256 * kp + 256]
                lane = 256 * k + 128 * lp
                ybuf[kp, :256, lane : lane + 128] = block[:, :128]
                ybuf[kp, 256:, lane : lane + 128] = block[:, 128:]
    for kp in range(2):
        spec = dot(tab[kp], ybuf[kp]).astype(BF)
        for k in range(2):
            for part in range(2):
                store(k, part, kp, spec[128 * part : 128 * part + 128, 256 * k : 256 * k + 256])


def image_copies(img, look, patches, xbuf, sems):
    return [
        pltpu.make_async_copy(img.at[look, p], xbuf.at[i], sems.at[i]) for i, p in enumerate(patches)
    ]


def send_kernel(patches, img, tables, out, xbuf, tab, hbuf, ybuf, sems):
    copies = image_copies(img, 1 - place()["lo"], patches, xbuf, sems)
    load = pltpu.make_async_copy(tables.at[pl.ds(0, 2)], tab, sems.at[len(patches)])
    for c in copies[:1] + [load] + copies[1:]:
        c.start()
    for c in copies + [load]:
        c.wait()

    def store(k, part, kp, value):
        out[k, part, 128 * kp : 128 * kp + 128, :] = value

    image_pair(xbuf, 0, tab, hbuf, ybuf, store)


def rest_kernel(
    img, tables, sent_a, sent_b, e0_a, e0_b, e1_a, e1_b, wrapped_a, wrapped_b, xbuf, tab, hbuf, ybuf, sems
):
    at = place()
    copies = image_copies(img, 1 - at["lo"], (2, 3), xbuf, sems)
    copies += image_copies(img, at["lo"], range(4), xbuf.at[pl.ds(2, 4)], sems.at[pl.ds(2, 4)])
    load = pltpu.make_async_copy(tables.at[pl.ds(0, 2)], tab, sems.at[6])
    for c in copies[:1] + [load] + copies[1:]:
        c.start()
    lo = at["lo"] > 0
    zero = at["zero"]
    load.wait()

    def keep(k, part, kp, value):
        sent_b[k, part, 128 * kp : 128 * kp + 128, :] = value

    for pair in range(3):
        for c in copies[2 * pair : 2 * pair + 2]:
            c.wait()

        def store(k, part, kp, value):
            rows = slice(128 * kp, 128 * kp + 128)
            sent, e0, e1, wrapped = ((sent_a, e0_a, e1_a, wrapped_a), (sent_b, e0_b, e1_b, wrapped_b))[pair - 1]
            other = sent[k, part, rows, :]
            v0 = jnp.where(lo, other, value)
            v1 = jnp.where(lo, value, other)
            e0[k, part, rows, :] = v0
            e1[k, part, rows, :] = v1
            wrapped[k, part, rows, :] = jnp.where(zero, v0, v1)

        image_pair(xbuf, 2 * pair, tab, hbuf.at[pair], ybuf.at[pair], store if pair else keep)


VM = pl.BlockSpec(memory_space=pltpu.VMEM)
SM = pl.BlockSpec(memory_space=pltpu.SMEM)
ANY = pl.BlockSpec(memory_space=pl.ANY)


def call(kernel, outs, ins, scratch, limit, flops, name):
    specs = []
    for kind, _ in ins:
        specs.append({"s": SM, "v": VM, "a": ANY}[kind])
    return pl.pallas_call(
        kernel,
        out_shape=[jax.ShapeDtypeStruct(s, t) for s, t in outs],
        in_specs=specs,
        out_specs=[VM] * len(outs),
        scratch_shapes=scratch,
        compiler_params=pltpu.CompilerParams(vmem_limit_bytes=limit * 2**20),
        cost_estimate=pl.CostEstimate(flops=flops * 10**6, bytes_accessed=2**20, transcendentals=0),
        name=name,
    )(*[a for _, a in ins])


def forward_send(patches, images, tables):
    return call(
        functools.partial(send_kernel, patches),
        [((2, 2, BAND, BAND), BF)],
        [("a", images), ("a", tables)],
        [
            pltpu.VMEM((2, 2, PIX, PIX), BF),
            pltpu.VMEM((2, 256, 512), BF),
            pltpu.VMEM((2, 1024, 512), BF),
            pltpu.VMEM((2, 512, 512), BF),
            pltpu.SemaphoreType.DMA((3,)),
        ],
        57,
        1200,
        "forward_send",
    )[0]


def forward_rest(images, tables, sent_a):
    return call(
        rest_kernel,
        [((2, 2, BAND, BAND), BF)] * 7,
        [("a", images), ("a", tables), ("v", sent_a)],
        [
            pltpu.VMEM((6, 2, PIX, PIX), BF),
            pltpu.VMEM((2, 256, 512), BF),
            pltpu.VMEM((3, 2, 1024, 512), BF),
            pltpu.VMEM((3, 2, 512, 512), BF),
            pltpu.SemaphoreType.DMA((7,)),
        ],
        REST_LIMIT,
        3600,
        "forward_rest",
    )


def load_block(ref, p, row, lane):
    return [ref[p, part, pl.ds(row, 16), lane].astype(F32) for part in range(2)]


def accumulate(acc, i, l, m):
    acc[2 * i] = acc[2 * i] + (l[0] * m[0] + l[1] * m[1])
    acc[2 * i + 1] = acc[2 * i + 1] + (l[1] * m[0] - l[0] * m[1])


def add_energy(energy, i, w, s):
    energy[i] = energy[i] + w * (s[0] * s[0] + s[1] * s[1])


def pick(cond, a, b):
    return [jnp.where(cond, u, v) for u, v in zip(a, b)]


def inverse(tab, cross, surf, pairs):
    for i in range(pairs):
        shifted = dot(tab[0], cross[i]).astype(BF)
        low = dot(tab[1], cross[i]).astype(BF)
        surf[i] = (dot_nt(shifted, tab[2, :, :BAND]) + dot_nt(low, tab[2, :, BAND:])).astype(BF)


def emit(surf, pairs, outs, erows):
    x = place()["x"]
    for slot, out in enumerate(outs):
        dest = lax.rem(x + slot, 4)
        for yh in range(2):
            start = pl.multiple_of((4 * yh + dest) * 32, 32)
            for i in range(pairs):
                out[yh, 32 * i : 32 * i + 32, :] = surf[i, pl.ds(start, 32), :]
            out[yh, 32 * pairs :, :] = erows


def split(value):
    hi = value.astype(BF).astype(F32)
    return hi, (value - hi).astype(BF).astype(F32)


def energy_rows(values):
    his, los = zip(*[split(v) for v in values])
    pad = [jnp.zeros_like(values[0])] * (EROWS - 2 * len(values))
    return jnp.concatenate(list(his) + list(los) + pad, axis=0).astype(BF)


def total_rows(energy_sum, count):
    totals = []
    for i in range(count):
        total = jnp.sum(jnp.sum(energy_sum[i], axis=1, keepdims=True), axis=0, keepdims=True)
        totals.append(jnp.broadcast_to(total, (1, WIN)))
    return energy_rows(totals)


def blocks(body):
    @pl.loop(0, BAND // 16)
    def _(block):
        row = pl.multiple_of(block * 16, 16)
        rowi = pl.multiple_of(block * 16 + BAND, 16)
        for half in range(2):
            body(row, rowi, slice(128 * half, 128 * half + 128))


def zeros(count):
    return [jnp.zeros((16, 128), F32)] * count


def early_kernel(
    weight, tab, e0_a, e0_b, e1_a, e1_b, op_a, op_b, s0, s1, s2, s3, energy_out, cross, surf
):
    lo = place()["lo"] > 0
    energy_out[...] = jnp.zeros_like(energy_out)

    def body(row, rowi, lane):
        acc, energy = zeros(4), zeros(3)
        for p in range(4):
            w = weight[p]
            own0 = load_block((e0_a, e0_b)[p // 2], p % 2, row, lane)
            own1 = load_block((e1_a, e1_b)[p // 2], p % 2, row, lane)
            opp = load_block((op_a, op_b)[p // 2], p % 2, row, lane)
            for i, v in enumerate((own0, own1, opp)):
                add_energy(energy, i, w, v)
            accumulate(acc, 0, [w * v for v in own0], own1)
            accumulate(acc, 1, [w * v for v in pick(lo, own1, own0)], opp)
        for i in range(2):
            cross[i, pl.ds(row, 16), lane] = acc[2 * i].astype(BF)
            cross[i, pl.ds(rowi, 16), lane] = acc[2 * i + 1].astype(BF)
        cross[2, pl.ds(row, 16), lane] = acc[2].astype(BF)
        cross[2, pl.ds(rowi, 16), lane] = (-acc[3]).astype(BF)
        for i in range(3):
            energy_out[i] += energy[i][:8] + energy[i][8:]

    blocks(body)
    inverse(tab, cross, surf, 3)
    emit(surf, 3, (s0, s1, s2, s3), total_rows(energy_out, 3))


def late_kernel(
    weight, tab, energy_in, e0_a, e0_b, e1_a, e1_b, q1_a, q1_b, pl0_a, pl0_b, pl1_a, pl1_b,
    s0, s1, s2, s3, cross, surf, energy_sum,
):
    swapped = place()["last"]
    energy_sum[0:2] = energy_in[0:2]
    energy_sum[2:5] = jnp.zeros((3, 8, 128), F32)

    def body(row, rowi, lane):
        acc, energy = zeros(10), zeros(3)
        for p in range(4):
            w = weight[p]
            own0, own1, prev, a, b = [
                load_block(pair[p // 2], p % 2, row, lane)
                for pair in ((e0_a, e0_b), (e1_a, e1_b), (q1_a, q1_b), (pl0_a, pl0_b), (pl1_a, pl1_b))
            ]
            next0, next1 = pick(swapped, b, a), pick(swapped, a, b)
            for i, v in enumerate((prev, next0, next1)):
                add_energy(energy, i, w, v)
            w0 = [w * v for v in own0]
            wq = [w * v for v in prev]
            for i, (l, m) in enumerate(
                ((w0, next0), (w0, next1), (wq, own0), (wq, own1), (wq, next0))
            ):
                accumulate(acc, i, l, m)
        for i in range(5):
            cross[i, pl.ds(row, 16), lane] = acc[2 * i].astype(BF)
            cross[i, pl.ds(rowi, 16), lane] = acc[2 * i + 1].astype(BF)
        for i in range(3):
            energy_sum[2 + i] += energy[i][:8] + energy[i][8:]

    blocks(body)
    inverse(tab, cross, surf, 5)
    emit(surf, 5, (s0, s1, s2, s3), total_rows(energy_sum, 5))


def surfaces(kernel, pairs, ins, more, scratch, name):
    return call(
        kernel,
        [((2, 32 * pairs + EROWS, WIN), BF)] * 4 + more,
        ins,
        [pltpu.VMEM((pairs, 2 * BAND, BAND), BF), pltpu.VMEM((pairs, WIN, WIN), BF)] + scratch,
        24,
        250 * pairs,
        name,
    )


def sum_energy(block, count):
    return [block[i : i + 1] + block[count + i : count + i + 1] for i in range(count)]


def add_parts(parts, h):
    a, b, c, d = [r[h].astype(F32) for r in parts]
    return (a + b) + (c + d)


def gather_early_kernel(a, b, c, d, keep, near, opp_same, opp_other):
    yh = place()["yh"]
    for h, (near_out, opp_out) in ((yh, (keep, opp_same)), (1 - yh, (near, opp_other))):
        total = add_parts((a, b, c, d), h)
        erows = energy_rows(sum_energy(total[96:], 3))
        near_out[0:64] = total[0:64].astype(near_out.dtype)
        near_out[64:] = erows.astype(near_out.dtype)
        opp_out[0:32] = total[64:96].astype(BF)
        opp_out[32:] = erows


def gather_late_kernel(a, b, c, d, keep, near, back_same, back_other):
    yh = place()["yh"]
    for h, (near_out, back_out) in ((yh, (keep, back_same)), (1 - yh, (near, back_other))):
        total = add_parts((a, b, c, d), h)
        erows = energy_rows(sum_energy(total[160:], 5))
        near_out[0:64] = total[0:64].astype(near_out.dtype)
        near_out[64:] = erows.astype(near_out.dtype)
        back_out[0:96] = total[64:160].astype(BF)
        back_out[96:] = erows


def final_kernel(scale, mask, keep, near, opp_a, opp_b, keep2, near2, back_a, back_b, out):
    lo = place()["lo"] > 0
    mine = keep[...] + near[...].astype(F32)
    other = opp_a[...].astype(F32) + opp_b[...].astype(F32)
    mine2 = keep2[...] + near2[...].astype(F32)
    back = back_a[...].astype(F32) + back_b[...].astype(F32)

    def factor(el, em):
        return scale / jnp.sqrt(el * em)

    def put(look, lag, value):
        out[look, lag] = value * mask[look, lag].astype(F32)

    own0, own1, opp = sum_energy(mine[64:], 3)
    _, _, _, next0, next1 = sum_energy(mine2[64:], 5)
    put(0, 0, mine[:32] * factor(own0, own1))
    put(0, 1, mine2[:32] * factor(own0, next0))
    put(0, 2, mine2[32:64] * factor(own0, next1))
    b0, b1, bq, bn0, _ = sum_energy(back[96:], 5)
    put(1, 0, back[:32] * factor(bq, b0))
    put(1, 1, back[32:64] * factor(bq, b1))
    put(1, 2, back[64:96] * factor(bq, bn0))
    o0, o1, oo = sum_energy(other[32:], 3)
    own_opp = mine[32:64] * factor(jnp.where(lo, own1, own0), opp)
    other_opp = other[:32] * factor(jnp.where(lo, o0, o1), oo)
    put(0, 3, jnp.where(lo, other_opp, own_opp))
    put(1, 3, jnp.where(lo, own_opp, other_opp))


def after(array, *others):
    return lax.optimization_barrier((array,) + others)[0]


def per_device(images, patch_weight, pair_mask):
    nlook = lax.axis_size("look")
    nswath = lax.axis_size("swath")
    ring = nlook // 2
    edge = lax.axis_index("look") % ring == 0
    tables, inverse_tables = make_tables()

    def over_look(array, to):
        return lax.ppermute(array, "look", [(i, to(i)) for i in range(nlook)])

    def over_x(parts):
        moved = [parts[0]]
        for by in range(1, 4):
            perm = [(i, i // 4 * 4 + (i + by) % 4) for i in range(nswath)]
            moved.append(lax.ppermute(parts[by], "swath", perm))
        return moved

    def over_both(array, to_look, flip):
        perm = [
            (i * nswath + s, to_look(i) * nswath + ((s + nswath // 2) % nswath if flip else s))
            for i in range(nlook)
            for s in range(nswath)
        ]
        return lax.ppermute(array, ("look", "swath"), perm)

    stay = lambda i: i
    ahead = lambda i: (i + 1) % nlook
    behind = lambda i: (i - 1) % nlook
    across = lambda i: (i + ring) % nlook
    turn = lambda i: i // ring * ring + (i - 1) % ring

    sent_a = forward_send((0, 1), images, tables)
    op_a = over_look(sent_a, across)
    sent_b, e0_a, e0_b, e1_a, e1_b, wrapped_a, wrapped_b = forward_rest(images, tables, sent_a)
    op_b = over_look(sent_b, across)
    pl1_a = over_look(wrapped_a, behind)
    q1_a = over_look(e1_a, ahead)
    pl0_a = over_look(jnp.where(edge, op_a, e0_a), turn)
    op_b = after(op_b, pl0_a)
    turn_b = jnp.where(edge, op_b, e0_b)
    pl0_b = over_look(turn_b, turn)
    pl1_b = over_look(after(wrapped_b, turn_b), behind)
    q1_b = over_look(after(e1_b, turn_b), ahead)

    vm = lambda *arrays: [("v", a) for a in arrays]
    common = [("s", patch_weight), ("v", inverse_tables)]
    *early, energy = surfaces(
        early_kernel,
        3,
        common + vm(e0_a, e0_b, e1_a, e1_b, op_a, after(op_b, turn_b, pl1_a, q1_a)),
        [((3, 8, 128), F32)],
        [],
        "surfaces_early",
    )
    early = over_x(early)
    energy = after(energy, *early[1:])
    late = surfaces(
        late_kernel,
        5,
        common + vm(energy, e0_a, e0_b, e1_a, e1_b, q1_a, q1_b, pl0_a, pl0_b, pl1_a, pl1_b),
        [],
        [pltpu.VMEM((5, 8, 128), F32)],
        "surfaces_late",
    )
    late = over_x(late)
    rows = lambda n, t: ((n + EROWS, WIN), t)
    keep, near, opp_same, opp_other = call(
        gather_early_kernel,
        [rows(64, F32), rows(64, BF), rows(32, BF), rows(32, BF)],
        vm(*early),
        [],
        16,
        10,
        "gather_early",
    )
    got = [
        keep,
        over_both(near, stay, True),
        over_both(opp_same, across, False),
        over_both(opp_other, across, True),
    ]
    late[0] = after(late[0], *got)
    keep, near, back_same, back_other = call(
        gather_late_kernel,
        [rows(64, F32), rows(64, BF), rows(96, BF), rows(96, BF)],
        vm(*late),
        [],
        16,
        10,
        "gather_late",
    )
    got += [
        keep,
        over_both(near, stay, True),
        over_both(back_same, behind, False),
        over_both(back_other, behind, True),
    ]
    scale = BAND * math.sqrt(patch_weight.shape[0] * nswath)
    return call(
        functools.partial(final_kernel, scale),
        [((2, 4, 32, WIN), F32)],
        [("s", pair_mask)] + vm(*got),
        [],
        16,
        10,
        "final",
    )[0]


def solution(mesh):
    return jax.shard_map(
        per_device,
        mesh=mesh,
        in_specs=(P("look", "swath", None, None, None), P("swath"), P("look", None)),
        out_specs=P("look", None, "swath", None),
        check_vma=False,
    )
```

profile of v0, /device:TPU:2, one launch (start us, length us, event | category | flops | bytes accessed | tf_op | source)
XLA Modules:
  0.0 88.4 jit_solution(12172427268918252813)
XLA Ops:
  0.0 3.7 %forward_send.1.sent_a = bf16[2,2,256,256]{3,2,1,0:T(8,128)(2,1)} custom-call(bf16[2,4,2,512,512]{4,3,2,1,0:T(8,128)(2,1)} %img.3, bf16[32,256,512]{2,1,0:T(8,128)(2,1)} %constant.24.clone.tables), custom_call_target="tpu_custom_call" | custom-call | flops 1200000000 | bytes 1048576 | tf_op jit(solution)/shard_map/forward_send/pallas_call | solution.py:163
  3.7 1.7 %collective-permute-start = (bf16[2,2,256,256]{3,2,1,0:T(8,128)(2,1)}, bf16[2,2,256,256]{3,2,1,0:T(8,128)(2,1)S(1)}, u32[]{:S(2)}, u32[]{:S(2)}) collective-permute-start(bf16[2,2,256,256]{3,2,1,0:T(8,128)(2,1)} %forward_send.1.sent_a), channel_id=1, source_target_pairs={{0,128},{8,136},{16,144},{24,152},{32,160},{40,168},{48,176},{56,1... | collective-permute-start | bytes 1572872 | tf_op jit(solution)/shard_map/ppermute | solution.py:428
  5.4 7.4 %forward_rest.1 = (bf16[2,2,256,256]{3,2,1,0:T(8,128)(2,1)S(1)}, bf16[2,2,256,256]{3,2,1,0:T(8,128)(2,1)S(1)}, bf16[2,2,256,256]{3,2,1,0:T(8,128)(2,1)S(1)}, bf1...) custom-call(bf16[2,4,2,512,512]{4,3,2,1,0:T(8,128)(2,1)} %img.3, ...), custom_call_target="tpu_custom_call" | custom-call | flops 3600000000 | bytes 1048576 | tf_op jit(solution)/shard_map/forward_rest/pallas_call | solution.py:163
  12.8 0.5 collective-permute-start.1
  13.4 5.4 %collective-permute-done.op_a = bf16[2,2,256,256]{3,2,1,0:T(8,128)(2,1)S(1)} collective-permute-done((bf16[2,2,256,256]{3,2,1,0:T(8,128)(2,1)}, bf16[2,2,256,256]{3,2,1,0:T(8,128)(2,1)S(1)}, u32[]{:S(2)}, u32[]{:S(2)}) %collective-permute-start) | collective-permute-done | bytes 524320 | tf_op jit(solution)/shard_map/ppermute | solution.py:428
  18.9 3.3 %collective-permute-start.2 = (bf16[2,2,256,256]{3,2,1,0:T(8,128)(2,1)S(1)}, bf16[2,2,256,256]{3,2,1,0:T(8,128)(2,1)S(1)}, u32[]{:S(2)}, u32[]{:S(2)}) collective-permute-start(bf16[2,2,256,256]{3,2,1,0:T(8,128)(2,1)S(1)} %broadcast_select_fusion.1), channel_id=1, source_target_pairs={{0,120},{8,0},{16,8},{24,16},{32,24},{40,32},{48,40},{56,48},{64,5... | collective-permute-start | bytes 1572872 | tf_op jit(solution)/shard_map/ppermute | solution.py:428
  22.2 3.7 %collective-permute-start.3 = (bf16[2,2,256,256]{3,2,1,0:T(8,128)(2,1)}, bf16[2,2,256,256]{3,2,1,0:T(8,128)(2,1)S(1)}, u32[]{:S(2)}, u32[]{:S(2)}) collective-permute-start(bf16[2,2,256,256]{3,2,1,0:T(8,128)(2,1)} %get-tuple-element.41), channel_id=1, source_target_pairs={{0,248},{8,0},{16,8},{24,16},{32,24},{40,32},{48,40},{56,48},{64,5... | collective-permute-start | bytes 1572872 | tf_op jit(solution)/shard_map/ppermute | solution.py:428
  25.9 3.0 %collective-permute-done.1.op_b = bf16[2,2,256,256]{3,2,1,0:T(8,128)(2,1)S(1)} collective-permute-done((bf16[2,2,256,256]{3,2,1,0:T(8,128)(2,1)S(1)}, bf16[2,2,256,256]{3,2,1,0:T(8,128)(2,1)S(1)}, u32[]{:S(2)}, u32[]{:S(2)}) %collective-permute-start.1) | collective-permute-done | bytes 524320 | tf_op jit(solution)/shard_map/ppermute | solution.py:428
  29.0 9.2 %collective-permute-start.12 = (bf16[2,2,256,256]{3,2,1,0:T(8,128)(2,1)S(1)}, bf16[2,2,256,256]{3,2,1,0:T(8,128)(2,1)S(1)}, u32[]{:S(2)}, u32[]{:S(2)}) collective-permute-start(bf16[2,2,256,256]{3,2,1,0:T(8,128)(2,1)S(1)} %broadcast_select_fusion), channel_id=1, source_target_pairs={{0,120},{8,0},{16,8},{24,16},{32,24},{40,32},{48,40},{56,48},{64,5... | collective-permute-start | bytes 1572872 | tf_op jit(solution)/shard_map/ppermute | solution.py:428
  38.1 3.9 %collective-permute-start.13 = (bf16[2,2,256,256]{3,2,1,0:T(8,128)(2,1)}, bf16[2,2,256,256]{3,2,1,0:T(8,128)(2,1)S(1)}, u32[]{:S(2)}, u32[]{:S(2)}) collective-permute-start(bf16[2,2,256,256]{3,2,1,0:T(8,128)(2,1)} %get-tuple-element.55), channel_id=1, source_target_pairs={{0,248},{8,0},{16,8},{24,16},{32,24},{40,32},{48,40},{56,48},{64,5... | collective-permute-start | bytes 1572872 | tf_op jit(solution)/shard_map/ppermute | solution.py:428
  42.0 1.0 %copy-done.1 = bf16[2,2,256,256]{3,2,1,0:T(8,128)(2,1)S(1)} copy-done((bf16[2,2,256,256]{3,2,1,0:T(8,128)(2,1)S(1)}, bf16[2,2,256,256]{3,2,1,0:T(8,128)(2,1)}, u32[]{:S(2)}) %copy-start.1) | copy-done | bytes 524312
  43.0 1.0 %copy-done.2 = bf16[2,2,256,256]{3,2,1,0:T(8,128)(2,1)S(1)} copy-done((bf16[2,2,256,256]{3,2,1,0:T(8,128)(2,1)S(1)}, bf16[2,2,256,256]{3,2,1,0:T(8,128)(2,1)}, u32[]{:S(2)}) %copy-start.2) | copy-done | bytes 524312
  44.1 3.3 %surfaces_early.1 = (bf16[2,112,256]{2,1,0:T(8,128)(2,1)S(1)}, bf16[2,112,256]{2,1,0:T(8,128)(2,1)S(1)}, bf16[2,112,256]{2,1,0:T(8,128)(2,1)S(1)}, bf16[2,112,256]{2,1,0:T(8,128)(2,1)S(1)}, f32[3,8,128]{2,1,0:T(8,128)S(1)}) custom-call(f32[4]{0:T(128)S(1)} %copy-done.3, bf16[3,256,512]{2,1,0:T(8,128)(2,1)S(1)} %copy-done, ...), custom_call_target="tpu_custom_call" | custom-call | flops 750000000 | bytes 1048576 | tf_op jit(solution)/shard_map/surfaces_early/pallas_call | solution.py:163
  47.4 1.6 %collective-permute-start.5 = (bf16[2,112,256]{2,1,0:T(8,128)(2,1)S(1)}, bf16[2,112,256]{2,1,0:T(8,128)(2,1)S(1)}, u32[]{:S(2)}, u32[]{:S(2)}) collective-permute-start(bf16[2,112,256]{2,1,0:T(8,128)(2,1)S(1)} %get-tuple-element.44), channel_id=1, source_target_pairs={{0,1},{1,2},{2,3},{3,0},{4,5},{5,6},{6,7},{7,4},{8,9},{9,10},{10,1... | collective-permute-start | bytes 344072 | tf_op jit(solution)/shard_map/ppermute | solution.py:434
  49.0 1.1 %collective-permute-start.6 = (bf16[2,112,256]{2,1,0:T(8,128)(2,1)S(1)}, bf16[2,112,256]{2,1,0:T(8,128)(2,1)S(1)}, u32[]{:S(2)}, u32[]{:S(2)}) collective-permute-start(bf16[2,112,256]{2,1,0:T(8,128)(2,1)S(1)} %get-tuple-element.45), channel_id=1, source_target_pairs={{0,2},{1,3},{2,0},{3,1},{4,6},{5,7},{6,4},{7,5},{8,10},{9,11},{10,... | collective-permute-start | bytes 344072 | tf_op jit(solution)/shard_map/ppermute | solution.py:434
  50.1 2.2 %collective-permute-done.5.b = bf16[2,112,256]{2,1,0:T(8,128)(2,1)S(1)} collective-permute-done((bf16[2,112,256]{2,1,0:T(8,128)(2,1)S(1)}, bf16[2,112,256]{2,1,0:T(8,128)(2,1)S(1)}, u32[]{:S(2)}, u32[]{:S(2)}) %collective-permute-start.5) | collective-permute-done | bytes 114720 | tf_op jit(solution)/shard_map/ppermute | solution.py:434
  52.3 1.7 %collective-permute-start.7 = (bf16[2,112,256]{2,1,0:T(8,128)(2,1)S(1)}, bf16[2,112,256]{2,1,0:T(8,128)(2,1)S(1)}, u32[]{:S(2)}, u32[]{:S(2)}) collective-permute-start(bf16[2,112,256]{2,1,0:T(8,128)(2,1)S(1)} %get-tuple-element.46), channel_id=1, source_target_pairs={{0,3},{1,0},{2,1},{3,2},{4,7},{5,4},{6,5},{7,6},{8,11},{9,8},{10,9... | collective-permute-start | bytes 344072 | tf_op jit(solution)/shard_map/ppermute | solution.py:434
  54.0 1.3 %collective-permute-done.6.c = bf16[2,112,256]{2,1,0:T(8,128)(2,1)S(1)} collective-permute-done((bf16[2,112,256]{2,1,0:T(8,128)(2,1)S(1)}, bf16[2,112,256]{2,1,0:T(8,128)(2,1)S(1)}, u32[]{:S(2)}, u32[]{:S(2)}) %collective-permute-start.6) | collective-permute-done | bytes 114720 | tf_op jit(solution)/shard_map/ppermute | solution.py:434
  55.3 1.8 %collective-permute-done.7.d = bf16[2,112,256]{2,1,0:T(8,128)(2,1)S(1)} collective-permute-done((bf16[2,112,256]{2,1,0:T(8,128)(2,1)S(1)}, bf16[2,112,256]{2,1,0:T(8,128)(2,1)S(1)}, u32[]{:S(2)}, u32[]{:S(2)}) %collective-permute-start.7) | collective-permute-done | bytes 114720 | tf_op jit(solution)/shard_map/ppermute | solution.py:434
  57.1 5.1 %surfaces_late.1 = (bf16[2,176,256]{2,1,0:T(8,128)(2,1)S(1)}, bf16[2,176,256]{2,1,0:T(8,128)(2,1)S(1)}, bf16[2,176,256]{2,1,0:T(8,128)(2,1)S(1)}, bf16[2,176,256]{2,1,0:T(8,128)(2,1)S(1)}) custom-call(f32[4]{0:T(128)S(1)} %copy-done.3, bf16[3,256,512]{2,1,0:T(8,128)(2,1)S(1)} %copy-done, f32[3,8,128]{2,1,0:T(8,128)S(1)} %get-tuple-element.52.energy_in, ...), custom_call_target="tpu_custom_call" | custom-call | flops 1250000000 | bytes 1048576 | tf_op jit(solution)/shard_map/surfaces_late/pallas_call | solution.py:163
  62.2 1.6 %collective-permute-start.14 = (bf16[2,176,256]{2,1,0:T(8,128)(2,1)S(1)}, bf16[2,176,256]{2,1,0:T(8,128)(2,1)S(1)}, u32[]{:S(2)}, u32[]{:S(2)}) collective-permute-start(bf16[2,176,256]{2,1,0:T(8,128)(2,1)S(1)} %get-tuple-element.58), channel_id=1, source_target_pairs={{0,1},{1,2},{2,3},{3,0},{4,5},{5,6},{6,7},{7,4},{8,9},{9,10},{10,1... | collective-permute-start | bytes 540680 | tf_op jit(solution)/shard_map/ppermute | solution.py:434
  63.8 2.3 %collective-permute-start.15 = (bf16[2,176,256]{2,1,0:T(8,128)(2,1)S(1)}, bf16[2,176,256]{2,1,0:T(8,128)(2,1)S(1)}, u32[]{:S(2)}, u32[]{:S(2)}) collective-permute-start(bf16[2,176,256]{2,1,0:T(8,128)(2,1)S(1)} %get-tuple-element.59), channel_id=1, source_target_pairs={{0,2},{1,3},{2,0},{3,1},{4,6},{5,7},{6,4},{7,5},{8,10},{9,11},{10,... | collective-permute-start | bytes 540680 | tf_op jit(solution)/shard_map/ppermute | solution.py:434
  66.1 2.2 %collective-permute-start.16 = (bf16[2,176,256]{2,1,0:T(8,128)(2,1)S(1)}, bf16[2,176,256]{2,1,0:T(8,128)(2,1)S(1)}, u32[]{:S(2)}, u32[]{:S(2)}) collective-permute-start(bf16[2,176,256]{2,1,0:T(8,128)(2,1)S(1)} %get-tuple-element.60), channel_id=1, source_target_pairs={{0,3},{1,0},{2,1},{3,2},{4,7},{5,4},{6,5},{7,6},{8,11},{9,8},{10,9... | collective-permute-start | bytes 540680 | tf_op jit(solution)/shard_map/ppermute | solution.py:434
  68.4 2.6 %collective-permute-start.9 = (bf16[48,256]{1,0:T(8,128)(2,1)S(1)}, bf16[48,256]{1,0:T(8,128)(2,1)S(1)}, u32[]{:S(2)}, u32[]{:S(2)}) collective-permute-start(bf16[48,256]{1,0:T(8,128)(2,1)S(1)} %get-tuple-element.49), channel_id=1, source_target_pairs={{0,128},{1,129},{2,130},{3,131},{4,132},{5,133},{6,134},{7,135},{8... | collective-permute-start | bytes 73736 | tf_op jit(solution)/shard_map/ppermute | solution.py:443
  70.9 2.9 %collective-permute-start.8 = (bf16[80,256]{1,0:T(8,128)(2,1)S(1)}, bf16[80,256]{1,0:T(8,128)(2,1)S(1)}, u32[]{:S(2)}, u32[]{:S(2)}) collective-permute-start(bf16[80,256]{1,0:T(8,128)(2,1)S(1)} %get-tuple-element.48), channel_id=1, source_target_pairs={{0,4},{1,5},{2,6},{3,7},{4,0},{5,1},{6,2},{7,3},{8,12},{9,13},{10,... | collective-permute-start | bytes 122888 | tf_op jit(solution)/shard_map/ppermute | solution.py:443
  73.8 2.4 %collective-permute-start.10 = (bf16[48,256]{1,0:T(8,128)(2,1)S(1)}, bf16[48,256]{1,0:T(8,128)(2,1)S(1)}, u32[]{:S(2)}, u32[]{:S(2)}) collective-permute-start(bf16[48,256]{1,0:T(8,128)(2,1)S(1)} %get-tuple-element.50), channel_id=1, source_target_pairs={{0,132},{1,133},{2,134},{3,135},{4,128},{5,129},{6,130},{7,131},{8... | collective-permute-start | bytes 73736 | tf_op jit(solution)/shard_map/ppermute | solution.py:443
  76.2 2.7 %collective-permute-done.10.opp_b = bf16[48,256]{1,0:T(8,128)(2,1)S(1)} collective-permute-done((bf16[48,256]{1,0:T(8,128)(2,1)S(1)}, bf16[48,256]{1,0:T(8,128)(2,1)S(1)}, u32[]{:S(2)}, u32[]{:S(2)}) %collective-permute-start.10) | collective-permute-done | bytes 24608 | tf_op jit(solution)/shard_map/ppermute | solution.py:443
  78.9 0.1 gather_late.1
  79.0 0.1 collective-permute-start.18
  79.1 2.5 %collective-permute-start.19 = (bf16[112,256]{1,0:T(8,128)(2,1)S(1)}, bf16[112,256]{1,0:T(8,128)(2,1)S(1)}, u32[]{:S(2)}, u32[]{:S(2)}) collective-permute-start(bf16[112,256]{1,0:T(8,128)(2,1)S(1)} %get-tuple-element.64), channel_id=1, source_target_pairs={{0,252},{1,253},{2,254},{3,255},{4,248},{5,249},{6,250},{7,251},{8... | collective-permute-start | bytes 172040 | tf_op jit(solution)/shard_map/ppermute | solution.py:443
  81.6 5.5 %collective-permute-done.17.near2 = bf16[80,256]{1,0:T(8,128)(2,1)S(1)} collective-permute-done((bf16[80,256]{1,0:T(8,128)(2,1)S(1)}, bf16[80,256]{1,0:T(8,128)(2,1)S(1)}, u32[]{:S(2)}, u32[]{:S(2)}) %collective-permute-start.17) | collective-permute-done | bytes 40992 | tf_op jit(solution)/shard_map/ppermute | solution.py:443
  87.1 1.3 %final.1 = f32[2,4,32,256]{3,2,1,0:T(8,128)} custom-call(s32[2,4]{1,0:T(2,128)S(1)} %copy-done.4, f32[80,256]{1,0:T(8,128)S(1)} %get-tuple-element.47.keep, bf16[80,256]{1,0:T(8,128)(2,1)S(1)} %collective-permute-done.8.near, bf16[48,256]{1,0:T(8,128)(2,1)S(1)} %collective-permute-done.9.opp_a, bf16[48,256]{1,0:T(8,128)(2,1)S(1)} %collective-permute-done.10.opp_b, ...), custom_call_target="tpu_custom_call" | custom-call | flops 10000000 | bytes 1048576 | tf_op jit(solution)/shard_map/final/pallas_call | solution.py:163
  (27 shorter events, 0.2 us)
Async XLA Ops:
  3.7 38.3 %copy-start = (bf16[3,256,512]{2,1,0:T(8,128)(2,1)S(1)}, bf16[3,256,512]{2,1,0:T(8,128)(2,1)}, u32[]{:S(2)}) copy-start(bf16[3,256,512]{2,1,0:T(8,128)(2,1)} %constant.25.clone.tab) | copy-start | bytes 2359300
  3.7 38.3 %copy-start.3 = (f32[4]{0:T(128)S(1)}, f32[4]{0:T(128)}, u32[]{:S(2)}) copy-start(f32[4]{0:T(128)} %weight.3) | copy-start | bytes 52
  3.7 15.1 %collective-permute-start = (bf16[2,2,256,256]{3,2,1,0:T(8,128)(2,1)}, bf16[2,2,256,256]{3,2,1,0:T(8,128)(2,1)S(1)}, u32[]{:S(2)}, u32[]{:S(2)}) collective-permute-start(bf16[2,2,256,256]{3,2,1,0:T(8,128)(2,1)} %forward_send.1.sent_a), channel_id=1, source_target_pairs={{0,128},{8,136},{16,144},{24,152},{32,160},{40,168},{48,176},{56,1... | collective-permute-start | bytes 1572872 | tf_op jit(solution)/shard_map/ppermute | solution.py:428
  12.8 74.3 %copy-start.4 = (s32[2,4]{1,0:T(2,128)S(1)}, s32[2,4]{1,0:T(2,128)}, u32[]{:S(2)}) copy-start(s32[2,4]{1,0:T(2,128)} %mask.1) | copy-start | bytes 100
  12.8 16.1 %collective-permute-start.1 = (bf16[2,2,256,256]{3,2,1,0:T(8,128)(2,1)S(1)}, bf16[2,2,256,256]{3,2,1,0:T(8,128)(2,1)S(1)}, u32[]{:S(2)}, u32[]{:S(2)}) collective-permute-start(bf16[2,2,256,256]{3,2,1,0:T(8,128)(2,1)S(1)} %get-tuple-element.39), channel_id=1, source_target_pairs={{0,128},{8,136},{16,144},{24,152},{32,160},{40,168},{48,176},{56,1... | collective-permute-start | bytes 1572872 | tf_op jit(solution)/shard_map/ppermute | solution.py:428
  18.9 10.0 %collective-permute-start.2 = (bf16[2,2,256,256]{3,2,1,0:T(8,128)(2,1)S(1)}, bf16[2,2,256,256]{3,2,1,0:T(8,128)(2,1)S(1)}, u32[]{:S(2)}, u32[]{:S(2)}) collective-permute-start(bf16[2,2,256,256]{3,2,1,0:T(8,128)(2,1)S(1)} %broadcast_select_fusion.1), channel_id=1, source_target_pairs={{0,120},{8,0},{16,8},{24,16},{32,24},{40,32},{48,40},{56,48},{64,5... | collective-permute-start | bytes 1572872 | tf_op jit(solution)/shard_map/ppermute | solution.py:428
  22.2 19.8 %collective-permute-start.3 = (bf16[2,2,256,256]{3,2,1,0:T(8,128)(2,1)}, bf16[2,2,256,256]{3,2,1,0:T(8,128)(2,1)S(1)}, u32[]{:S(2)}, u32[]{:S(2)}) collective-permute-start(bf16[2,2,256,256]{3,2,1,0:T(8,128)(2,1)} %get-tuple-element.41), channel_id=1, source_target_pairs={{0,248},{8,0},{16,8},{24,16},{32,24},{40,32},{48,40},{56,48},{64,5... | collective-permute-start | bytes 1572872 | tf_op jit(solution)/shard_map/ppermute | solution.py:428
  25.9 16.1 %collective-permute-start.4 = (bf16[2,2,256,256]{3,2,1,0:T(8,128)(2,1)}, bf16[2,2,256,256]{3,2,1,0:T(8,128)(2,1)S(1)}, u32[]{:S(2)}, u32[]{:S(2)}) collective-permute-start(bf16[2,2,256,256]{3,2,1,0:T(8,128)(2,1)} %get-tuple-element.37.e1_a), channel_id=1, source_target_pairs={{0,8},{8,16},{16,24},{24,32},{32,40},{40,48},{48,56},{56,64},{64,7... | collective-permute-start | bytes 1572872 | tf_op jit(solution)/shard_map/ppermute | solution.py:428
  29.0 28.1 %collective-permute-start.12 = (bf16[2,2,256,256]{3,2,1,0:T(8,128)(2,1)S(1)}, bf16[2,2,256,256]{3,2,1,0:T(8,128)(2,1)S(1)}, u32[]{:S(2)}, u32[]{:S(2)}) collective-permute-start(bf16[2,2,256,256]{3,2,1,0:T(8,128)(2,1)S(1)} %broadcast_select_fusion), channel_id=1, source_target_pairs={{0,120},{8,0},{16,8},{24,16},{32,24},{40,32},{48,40},{56,48},{64,5... | collective-permute-start | bytes 1572872 | tf_op jit(solution)/shard_map/ppermute | solution.py:428
  38.1 19.0 %collective-permute-start.11 = (bf16[2,2,256,256]{3,2,1,0:T(8,128)(2,1)}, bf16[2,2,256,256]{3,2,1,0:T(8,128)(2,1)S(1)}, u32[]{:S(2)}, u32[]{:S(2)}) collective-permute-start(bf16[2,2,256,256]{3,2,1,0:T(8,128)(2,1)} %get-tuple-element.53.e1_b), channel_id=1, source_target_pairs={{0,8},{8,16},{16,24},{24,32},{32,40},{40,48},{48,56},{56,64},{64,7... | collective-permute-start | bytes 1572872 | tf_op jit(solution)/shard_map/ppermute | solution.py:428
  38.1 19.0 %collective-permute-start.13 = (bf16[2,2,256,256]{3,2,1,0:T(8,128)(2,1)}, bf16[2,2,256,256]{3,2,1,0:T(8,128)(2,1)S(1)}, u32[]{:S(2)}, u32[]{:S(2)}) collective-permute-start(bf16[2,2,256,256]{3,2,1,0:T(8,128)(2,1)} %get-tuple-element.55), channel_id=1, source_target_pairs={{0,248},{8,0},{16,8},{24,16},{32,24},{40,32},{48,40},{56,48},{64,5... | collective-permute-start | bytes 1572872 | tf_op jit(solution)/shard_map/ppermute | solution.py:428
  42.0 1.0 %copy-start.1 = (bf16[2,2,256,256]{3,2,1,0:T(8,128)(2,1)S(1)}, bf16[2,2,256,256]{3,2,1,0:T(8,128)(2,1)}, u32[]{:S(2)}) copy-start(bf16[2,2,256,256]{3,2,1,0:T(8,128)(2,1)} %get-tuple-element.37.e1_a) | copy-start | bytes 1572868
  43.0 1.0 %copy-start.2 = (bf16[2,2,256,256]{3,2,1,0:T(8,128)(2,1)S(1)}, bf16[2,2,256,256]{3,2,1,0:T(8,128)(2,1)}, u32[]{:S(2)}) copy-start(bf16[2,2,256,256]{3,2,1,0:T(8,128)(2,1)} %get-tuple-element.53.e1_b) | copy-start | bytes 1572868
  47.4 4.9 %collective-permute-start.5 = (bf16[2,112,256]{2,1,0:T(8,128)(2,1)S(1)}, bf16[2,112,256]{2,1,0:T(8,128)(2,1)S(1)}, u32[]{:S(2)}, u32[]{:S(2)}) collective-permute-start(bf16[2,112,256]{2,1,0:T(8,128)(2,1)S(1)} %get-tuple-element.44), channel_id=1, source_target_pairs={{0,1},{1,2},{2,3},{3,0},{4,5},{5,6},{6,7},{7,4},{8,9},{9,10},{10,1... | collective-permute-start | bytes 344072 | tf_op jit(solution)/shard_map/ppermute | solution.py:434
  49.0 6.3 %collective-permute-start.6 = (bf16[2,112,256]{2,1,0:T(8,128)(2,1)S(1)}, bf16[2,112,256]{2,1,0:T(8,128)(2,1)S(1)}, u32[]{:S(2)}, u32[]{:S(2)}) collective-permute-start(bf16[2,112,256]{2,1,0:T(8,128)(2,1)S(1)} %get-tuple-element.45), channel_id=1, source_target_pairs={{0,2},{1,3},{2,0},{3,1},{4,6},{5,7},{6,4},{7,5},{8,10},{9,11},{10,... | collective-permute-start | bytes 344072 | tf_op jit(solution)/shard_map/ppermute | solution.py:434
  52.3 4.8 %collective-permute-start.7 = (bf16[2,112,256]{2,1,0:T(8,128)(2,1)S(1)}, bf16[2,112,256]{2,1,0:T(8,128)(2,1)S(1)}, u32[]{:S(2)}, u32[]{:S(2)}) collective-permute-start(bf16[2,112,256]{2,1,0:T(8,128)(2,1)S(1)} %get-tuple-element.46), channel_id=1, source_target_pairs={{0,3},{1,0},{2,1},{3,2},{4,7},{5,4},{6,5},{7,6},{8,11},{9,8},{10,9... | collective-permute-start | bytes 344072 | tf_op jit(solution)/shard_map/ppermute | solution.py:434
  62.2 16.6 %collective-permute-start.14 = (bf16[2,176,256]{2,1,0:T(8,128)(2,1)S(1)}, bf16[2,176,256]{2,1,0:T(8,128)(2,1)S(1)}, u32[]{:S(2)}, u32[]{:S(2)}) collective-permute-start(bf16[2,176,256]{2,1,0:T(8,128)(2,1)S(1)} %get-tuple-element.58), channel_id=1, source_target_pairs={{0,1},{1,2},{2,3},{3,0},{4,5},{5,6},{6,7},{7,4},{8,9},{9,10},{10,1... | collective-permute-start | bytes 540680 | tf_op jit(solution)/shard_map/ppermute | solution.py:434
  63.8 15.1 %collective-permute-start.15 = (bf16[2,176,256]{2,1,0:T(8,128)(2,1)S(1)}, bf16[2,176,256]{2,1,0:T(8,128)(2,1)S(1)}, u32[]{:S(2)}, u32[]{:S(2)}) collective-permute-start(bf16[2,176,256]{2,1,0:T(8,128)(2,1)S(1)} %get-tuple-element.59), channel_id=1, source_target_pairs={{0,2},{1,3},{2,0},{3,1},{4,6},{5,7},{6,4},{7,5},{8,10},{9,11},{10,... | collective-permute-start | bytes 540680 | tf_op jit(solution)/shard_map/ppermute | solution.py:434
  66.1 12.7 %collective-permute-start.16 = (bf16[2,176,256]{2,1,0:T(8,128)(2,1)S(1)}, bf16[2,176,256]{2,1,0:T(8,128)(2,1)S(1)}, u32[]{:S(2)}, u32[]{:S(2)}) collective-permute-start(bf16[2,176,256]{2,1,0:T(8,128)(2,1)S(1)} %get-tuple-element.60), channel_id=1, source_target_pairs={{0,3},{1,0},{2,1},{3,2},{4,7},{5,4},{6,5},{7,6},{8,11},{9,8},{10,9... | collective-permute-start | bytes 540680 | tf_op jit(solution)/shard_map/ppermute | solution.py:434
  68.4 5.4 %collective-permute-start.9 = (bf16[48,256]{1,0:T(8,128)(2,1)S(1)}, bf16[48,256]{1,0:T(8,128)(2,1)S(1)}, u32[]{:S(2)}, u32[]{:S(2)}) collective-permute-start(bf16[48,256]{1,0:T(8,128)(2,1)S(1)} %get-tuple-element.49), channel_id=1, source_target_pairs={{0,128},{1,129},{2,130},{3,131},{4,132},{5,133},{6,134},{7,135},{8... | collective-permute-start | bytes 73736 | tf_op jit(solution)/shard_map/ppermute | solution.py:443
  70.9 7.9 %collective-permute-start.8 = (bf16[80,256]{1,0:T(8,128)(2,1)S(1)}, bf16[80,256]{1,0:T(8,128)(2,1)S(1)}, u32[]{:S(2)}, u32[]{:S(2)}) collective-permute-start(bf16[80,256]{1,0:T(8,128)(2,1)S(1)} %get-tuple-element.48), channel_id=1, source_target_pairs={{0,4},{1,5},{2,6},{3,7},{4,0},{5,1},{6,2},{7,3},{8,12},{9,13},{10,... | collective-permute-start | bytes 122888 | tf_op jit(solution)/shard_map/ppermute | solution.py:443
  73.8 5.0 %collective-permute-start.10 = (bf16[48,256]{1,0:T(8,128)(2,1)S(1)}, bf16[48,256]{1,0:T(8,128)(2,1)S(1)}, u32[]{:S(2)}, u32[]{:S(2)}) collective-permute-start(bf16[48,256]{1,0:T(8,128)(2,1)S(1)} %get-tuple-element.50), channel_id=1, source_target_pairs={{0,132},{1,133},{2,134},{3,135},{4,128},{5,129},{6,130},{7,131},{8... | collective-permute-start | bytes 73736 | tf_op jit(solution)/shard_map/ppermute | solution.py:443
  79.0 8.1 %collective-permute-start.18 = (bf16[112,256]{1,0:T(8,128)(2,1)S(1)}, bf16[112,256]{1,0:T(8,128)(2,1)S(1)}, u32[]{:S(2)}, u32[]{:S(2)}) collective-permute-start(bf16[112,256]{1,0:T(8,128)(2,1)S(1)} %get-tuple-element.63), channel_id=1, source_target_pairs={{0,248},{1,249},{2,250},{3,251},{4,252},{5,253},{6,254},{7,255},{8... | collective-permute-start | bytes 172040 | tf_op jit(solution)/shard_map/ppermute | solution.py:443
  79.1 8.0 %collective-permute-start.19 = (bf16[112,256]{1,0:T(8,128)(2,1)S(1)}, bf16[112,256]{1,0:T(8,128)(2,1)S(1)}, u32[]{:S(2)}, u32[]{:S(2)}) collective-permute-start(bf16[112,256]{1,0:T(8,128)(2,1)S(1)} %get-tuple-element.64), channel_id=1, source_target_pairs={{0,252},{1,253},{2,254},{3,255},{4,248},{5,249},{6,250},{7,251},{8... | collective-permute-start | bytes 172040 | tf_op jit(solution)/shard_map/ppermute | solution.py:443
  81.6 5.5 %collective-permute-start.17 = (bf16[80,256]{1,0:T(8,128)(2,1)S(1)}, bf16[80,256]{1,0:T(8,128)(2,1)S(1)}, u32[]{:S(2)}, u32[]{:S(2)}) collective-permute-start(bf16[80,256]{1,0:T(8,128)(2,1)S(1)} %get-tuple-element.62), channel_id=1, source_target_pairs={{0,4},{1,5},{2,6},{3,7},{4,0},{5,1},{6,2},{7,3},{8,12},{9,13},{10,... | collective-permute-start | bytes 122888 | tf_op jit(solution)/shard_map/ppermute | solution.py:443
where the time goes:
time: 88.7 us; the launch traced here: 88.4 us
  starting transfers between devices  43.1 us (49%)
  waiting for transfers between devices  21.9 us (25%)
  Pallas kernels  21.1 us (24%)
  local copies, waits for them, and re-layouts  2.1 us (2%)
    ppermute x8, starting transfers between devices, over_look(): return lax.ppermute(array, 'look', [(i, to(i)) for i in range(nlook)])  22.2 us
    pallas_call x7, Pallas kernels, call(): pl.pallas_call(kernel, out_shape=[jax.ShapeDtypeStruct(s, t) for s, t in...  21.1 us
    ppermute x6, starting transfers between devices, over_x(): moved.append(lax.ppermute(parts[by], 'swath', perm))  10.5 us
    ppermute x6, starting transfers between devices, over_both(): return lax.ppermute(array, ('look', 'swath'), perm)  10.4 us
    ppermute x8, waiting for transfers between devices, over_look(): return lax.ppermute(array, 'look', [(i, to(i)) for i in range(nlook)])  8.48 us
    ppermute x6, waiting for transfers between devices, over_both(): return lax.ppermute(array, ('look', 'swath'), perm)  8.19 us
    ppermute x6, waiting for transfers between devices, over_x(): moved.append(lax.ppermute(parts[by], 'swath', perm))  5.25 us
    unnamed x10, local copies, waits for them, and re-layouts  2.1 us
  transfers between devices with their start and end apart: 20, of which 7 were waited for; matrix products, arithmetic and copies ran while one was open for 0% of the time, Pallas kernels for 12%

commit v1 on v0

--- a/solution.py
+++ b/solution.py
@@ -53,6 +53,7 @@
         lo=(look >= nlook // 2).astype(jnp.int32),
         zero=look == 0,
         last=look == nlook - 1,
+        end=lax.rem(look, nlook // 2) == nlook // 2 - 1,
         x=lax.rem(swath, 4),
         yh=swath // 4,
     )
@@ -119,7 +120,7 @@
 
 
 def rest_kernel(
-    img, tables, sent_a, sent_b, e0_a, e0_b, e1_a, e1_b, wrapped_a, wrapped_b, xbuf, tab, hbuf, ybuf, sems
+    img, tables, sent_a, e0, e1, wrapped, sent_b, xbuf, tab, hbuf, ybuf, sems
 ):
     at = place()
     copies = image_copies(img, 1 - at["lo"], (2, 3), xbuf, sems)
@@ -140,13 +141,14 @@
 
         def store(k, part, kp, value):
             rows = slice(128 * kp, 128 * kp + 128)
-            sent, e0, e1, wrapped = ((sent_a, e0_a, e1_a, wrapped_a), (sent_b, e0_b, e1_b, wrapped_b))[pair - 1]
+            sent = (sent_a, sent_b)[pair - 1]
             other = sent[k, part, rows, :]
             v0 = jnp.where(lo, other, value)
             v1 = jnp.where(lo, value, other)
-            e0[k, part, rows, :] = v0
-            e1[k, part, rows, :] = v1
-            wrapped[k, part, rows, :] = jnp.where(zero, v0, v1)
+            p = 2 * (pair - 1) + k
+            e0[p, part, rows, :] = v0
+            e1[p, part, rows, :] = v1
+            wrapped[p, part, rows, :] = jnp.where(zero, v0, v1)
 
         image_pair(xbuf, 2 * pair, tab, hbuf.at[pair], ybuf.at[pair], store if pair else keep)
 
@@ -193,7 +195,7 @@
 def forward_rest(images, tables, sent_a):
     return call(
         rest_kernel,
-        [((2, 2, BAND, BAND), BF)] * 7,
+        [((4, 2, BAND, BAND), BF)] * 3 + [((2, 2, BAND, BAND), BF)],
         [("a", images), ("a", tables), ("v", sent_a)],
         [
             pltpu.VMEM((6, 2, PIX, PIX), BF),
@@ -225,11 +227,11 @@
     return [jnp.where(cond, u, v) for u, v in zip(a, b)]
 
 
-def inverse(tab, cross, surf, pairs):
+def inverse(tab, cross, surf, pairs, at):
     for i in range(pairs):
         shifted = dot(tab[0], cross[i]).astype(BF)
         low = dot(tab[1], cross[i]).astype(BF)
-        surf[i] = (dot_nt(shifted, tab[2, :, :BAND]) + dot_nt(low, tab[2, :, BAND:])).astype(BF)
+        surf[at + i] = (dot_nt(shifted, tab[2, :, :BAND]) + dot_nt(low, tab[2, :, BAND:])).astype(BF)
 
 
 def emit(surf, pairs, outs, erows):
@@ -275,9 +277,7 @@
     return [jnp.zeros((16, 128), F32)] * count
 
 
-def early_kernel(
-    weight, tab, e0_a, e0_b, e1_a, e1_b, op_a, op_b, s0, s1, s2, s3, energy_out, cross, surf
-):
+def early_kernel(weight, tab, e0, e1, op_a, op_b, surf, energy_out, cross):
     lo = place()["lo"] > 0
     energy_out[...] = jnp.zeros_like(energy_out)
 
@@ -285,8 +285,7 @@
         acc, energy = zeros(4), zeros(3)
         for p in range(4):
             w = weight[p]
-            own0 = load_block((e0_a, e0_b)[p // 2], p % 2, row, lane)
-            own1 = load_block((e1_a, e1_b)[p // 2], p % 2, row, lane)
+            own0, own1 = load_block(e0, p, row, lane), load_block(e1, p, row, lane)
             opp = load_block((op_a, op_b)[p // 2], p % 2, row, lane)
             for i, v in enumerate((own0, own1, opp)):
                 add_energy(energy, i, w, v)
@@ -301,26 +300,29 @@
             energy_out[i] += energy[i][:8] + energy[i][8:]
 
     blocks(body)
-    inverse(tab, cross, surf, 3)
-    emit(surf, 3, (s0, s1, s2, s3), total_rows(energy_out, 3))
+    inverse(tab, cross, surf, 3, 0)
 
 
 def late_kernel(
-    weight, tab, energy_in, e0_a, e0_b, e1_a, e1_b, q1_a, q1_b, pl0_a, pl0_b, pl1_a, pl1_b,
-    s0, s1, s2, s3, cross, surf, energy_sum,
+    weight, tab, early, energy_in, e0, e1, q1, pl0, pl1, turn_a, turn_b, s0, s1, s2, s3, cross, surf, energy_sum
 ):
-    swapped = place()["last"]
-    energy_sum[0:2] = energy_in[0:2]
-    energy_sum[2:5] = jnp.zeros((3, 8, 128), F32)
+    at = place()
+    swapped, end = at["last"], at["end"]
+    energy_sum[0:3] = energy_in[...]
+    energy_sum[3:6] = jnp.zeros((3, 8, 128), F32)
 
     def body(row, rowi, lane):
         acc, energy = zeros(10), zeros(3)
         for p in range(4):
             w = weight[p]
-            own0, own1, prev, a, b = [
-                load_block(pair[p // 2], p % 2, row, lane)
-                for pair in ((e0_a, e0_b), (e1_a, e1_b), (q1_a, q1_b), (pl0_a, pl0_b), (pl1_a, pl1_b))
+            own0, own1 = load_block(e0, p, row, lane), load_block(e1, p, row, lane)
+            prev = load_block(q1, p, row, lane)
+            turned = (turn_a, turn_b)[p // 2]
+            a = [
+                jnp.where(end, turned[p % 2, part, pl.ds(row, 16), lane], pl0[p, part, pl.ds(row, 16), lane]).astype(F32)
+                for part in range(2)
             ]
+            b = load_block(pl1, p, row, lane)
             next0, next1 = pick(swapped, b, a), pick(swapped, a, b)
             for i, v in enumerate((prev, next0, next1)):
                 add_energy(energy, i, w, v)
@@ -334,20 +336,21 @@
             cross[i, pl.ds(row, 16), lane] = acc[2 * i].astype(BF)
             cross[i, pl.ds(rowi, 16), lane] = acc[2 * i + 1].astype(BF)
         for i in range(3):
-            energy_sum[2 + i] += energy[i][:8] + energy[i][8:]
+            energy_sum[3 + i] += energy[i][:8] + energy[i][8:]
 
     blocks(body)
-    inverse(tab, cross, surf, 5)
-    emit(surf, 5, (s0, s1, s2, s3), total_rows(energy_sum, 5))
-
-
-def surfaces(kernel, pairs, ins, more, scratch, name):
+    surf[0:3] = early[...]
+    inverse(tab, cross, surf, 5, 3)
+    emit(surf, 8, (s0, s1, s2, s3), total_rows(energy_sum, 6))
+
+
+def surfaces(kernel, pairs, outs, ins, scratch, name):
     return call(
         kernel,
-        [((2, 32 * pairs + EROWS, WIN), BF)] * 4 + more,
+        outs,
         ins,
-        [pltpu.VMEM((pairs, 2 * BAND, BAND), BF), pltpu.VMEM((pairs, WIN, WIN), BF)] + scratch,
-        24,
+        [pltpu.VMEM((pairs, 2 * BAND, BAND), BF)] + scratch,
+        28,
         250 * pairs,
         name,
     )
@@ -362,34 +365,28 @@
     return (a + b) + (c + d)
 
 
-def gather_early_kernel(a, b, c, d, keep, near, opp_same, opp_other):
+def gather_kernel(a, b, c, d, keep, near, back_same, back_other, opp_same, opp_other):
     yh = place()["yh"]
-    for h, (near_out, opp_out) in ((yh, (keep, opp_same)), (1 - yh, (near, opp_other))):
+    for h, (near_out, back_out, opp_out) in (
+        (yh, (keep, back_same, opp_same)),
+        (1 - yh, (near, back_other, opp_other)),
+    ):
         total = add_parts((a, b, c, d), h)
-        erows = energy_rows(sum_energy(total[96:], 3))
+        erows = energy_rows(sum_energy(total[256:], 6))
         near_out[0:64] = total[0:64].astype(near_out.dtype)
-        near_out[64:] = erows.astype(near_out.dtype)
+        near_out[64:128] = total[96:160].astype(near_out.dtype)
+        near_out[128:] = erows.astype(near_out.dtype)
+        back_out[0:96] = total[160:256].astype(BF)
+        back_out[96:] = erows
         opp_out[0:32] = total[64:96].astype(BF)
         opp_out[32:] = erows
 
 
-def gather_late_kernel(a, b, c, d, keep, near, back_same, back_other):
-    yh = place()["yh"]
-    for h, (near_out, back_out) in ((yh, (keep, back_same)), (1 - yh, (near, back_other))):
-        total = add_parts((a, b, c, d), h)
-        erows = energy_rows(sum_energy(total[160:], 5))
-        near_out[0:64] = total[0:64].astype(near_out.dtype)
-        near_out[64:] = erows.astype(near_out.dtype)
-        back_out[0:96] = total[64:160].astype(BF)
-        back_out[96:] = erows
-
-
-def final_kernel(scale, mask, keep, near, opp_a, opp_b, keep2, near2, back_a, back_b, out):
+def final_kernel(scale, mask, keep, near, back_a, back_b, opp_a, opp_b, out):
     lo = place()["lo"] > 0
     mine = keep[...] + near[...].astype(F32)
+    back = back_a[...].astype(F32) + back_b[...].astype(F32)
     other = opp_a[...].astype(F32) + opp_b[...].astype(F32)
-    mine2 = keep2[...] + near2[...].astype(F32)
-    back = back_a[...].astype(F32) + back_b[...].astype(F32)
 
     def factor(el, em):
         return scale / jnp.sqrt(el * em)
@@ -397,16 +394,15 @@
     def put(look, lag, value):
         out[look, lag] = value * mask[look, lag].astype(F32)
 
-    own0, own1, opp = sum_energy(mine[64:], 3)
-    _, _, _, next0, next1 = sum_energy(mine2[64:], 5)
+    own0, own1, opp, _, next0, next1 = sum_energy(mine[128:], 6)
     put(0, 0, mine[:32] * factor(own0, own1))
-    put(0, 1, mine2[:32] * factor(own0, next0))
-    put(0, 2, mine2[32:64] * factor(own0, next1))
-    b0, b1, bq, bn0, _ = sum_energy(back[96:], 5)
+    put(0, 1, mine[64:96] * factor(own0, next0))
+    put(0, 2, mine[96:128] * factor(own0, next1))
+    b0, b1, _, bq, bn0, _ = sum_energy(back[96:], 6)
     put(1, 0, back[:32] * factor(bq, b0))
     put(1, 1, back[32:64] * factor(bq, b1))
     put(1, 2, back[64:96] * factor(bq, bn0))
-    o0, o1, oo = sum_energy(other[32:], 3)
+    o0, o1, oo, _, _, _ = sum_energy(other[32:], 6)
     own_opp = mine[32:64] * factor(jnp.where(lo, own1, own0), opp)
     other_opp = other[:32] * factor(jnp.where(lo, o0, o1), oo)
     put(0, 3, jnp.where(lo, other_opp, own_opp))
@@ -421,7 +417,6 @@
     nlook = lax.axis_size("look")
     nswath = lax.axis_size("swath")
     ring = nlook // 2
-    edge = lax.axis_index("look") % ring == 0
     tables, inverse_tables = make_tables()
 
     def over_look(array, to):
@@ -450,70 +445,52 @@
 
     sent_a = forward_send((0, 1), images, tables)
     op_a = over_look(sent_a, across)
-    sent_b, e0_a, e0_b, e1_a, e1_b, wrapped_a, wrapped_b = forward_rest(images, tables, sent_a)
+    e0, e1, wrapped, sent_b = forward_rest(images, tables, sent_a)
     op_b = over_look(sent_b, across)
-    pl1_a = over_look(wrapped_a, behind)
-    q1_a = over_look(e1_a, ahead)
-    pl0_a = over_look(jnp.where(edge, op_a, e0_a), turn)
-    op_b = after(op_b, pl0_a)
-    turn_b = jnp.where(edge, op_b, e0_b)
-    pl0_b = over_look(turn_b, turn)
-    pl1_b = over_look(after(wrapped_b, turn_b), behind)
-    q1_b = over_look(after(e1_b, turn_b), ahead)
+    pl0 = lax.ppermute(e0, "look", [(i, turn(i)) for i in range(nlook) if i % ring])
+    edges = [(i, turn(i)) for i in range(nlook) if i % ring == 0]
+    turn_a = lax.ppermute(op_a, "look", edges)
+    op_b = after(op_b, pl0, turn_a)
+    turn_b = lax.ppermute(op_b, "look", edges)
+    pl1 = over_look(after(wrapped, op_b), behind)
+    q1 = over_look(after(e1, op_b), ahead)
 
     vm = lambda *arrays: [("v", a) for a in arrays]
     common = [("s", patch_weight), ("v", inverse_tables)]
-    *early, energy = surfaces(
+    surf, energy = surfaces(
         early_kernel,
         3,
-        common + vm(e0_a, e0_b, e1_a, e1_b, op_a, after(op_b, turn_b, pl1_a, q1_a)),
-        [((3, 8, 128), F32)],
+        [((3, WIN, WIN), BF), ((3, 8, 128), F32)],
+        common + vm(e0, e1, op_a, op_b),
         [],
         "surfaces_early",
     )
-    early = over_x(early)
-    energy = after(energy, *early[1:])
-    late = surfaces(
+    parts = surfaces(
         late_kernel,
         5,
-        common + vm(energy, e0_a, e0_b, e1_a, e1_b, q1_a, q1_b, pl0_a, pl0_b, pl1_a, pl1_b),
-        [],
-        [pltpu.VMEM((5, 8, 128), F32)],
+        [((2, 8 * 32 + EROWS, WIN), BF)] * 4,
+        common + vm(surf, energy, e0, e1, q1, pl0, pl1, turn_a, turn_b),
+        [pltpu.VMEM((8, WIN, WIN), BF), pltpu.VMEM((6, 8, 128), F32)],
         "surfaces_late",
     )
-    late = over_x(late)
     rows = lambda n, t: ((n + EROWS, WIN), t)
-    keep, near, opp_same, opp_other = call(
-        gather_early_kernel,
-        [rows(64, F32), rows(64, BF), rows(32, BF), rows(32, BF)],
-        vm(*early),
+    keep, near, back_same, back_other, opp_same, opp_other = call(
+        gather_kernel,
+        [rows(128, F32), rows(128, BF), rows(96, BF), rows(96, BF), rows(32, BF), rows(32, BF)],
+        vm(*over_x(parts)),
         [],
         16,
         10,
-        "gather_early",
-    )
-    got = [
-        keep,
-        over_both(near, stay, True),
-        over_both(opp_same, across, False),
-        over_both(opp_other, across, True),
-    ]
-    late[0] = after(late[0], *got)
-    keep, near, back_same, back_other = call(
-        gather_late_kernel,
-        [rows(64, F32), rows(64, BF), rows(96, BF), rows(96, BF)],
-        vm(*late),
-        [],
-        16,
-        10,
-        "gather_late",
-    )
-    got += [
+        "gather",
+    )
+    got = (
         keep,
         over_both(near, stay, True),
         over_both(back_same, behind, False),
         over_both(back_other, behind, True),
-    ]
+        over_both(opp_same, across, False),
+        over_both(opp_other, across, True),
+    )
     scale = BAND * math.sqrt(patch_weight.shape[0] * nswath)
     return call(
         functools.partial(final_kernel, scale),

time: 88.7 us -> 83.9 us (0.946)
  starting transfers between devices: 43.1 us -> 29.2 us
  waiting for transfers between devices: 21.9 us -> 30.2 us
  local copies, waits for them, and re-layouts: 2.1 us -> 3.53 us
    ppermute x8 -> x4, starting transfers between devices: 22.2 us -> 6.83 us  [over_look(): return lax.ppermute(array, 'look', [(i, to(i)) for i in range(nlook)])]
    ppermute x0 -> x3, waiting for transfers between devices: none -> 11.2 us  [the longest x1 9.9 us: per_device(): turn_b = lax.ppermute(op_b, 'look', edges)]
    ppermute x0 -> x3, starting transfers between devices: none -> 10.1 us  [the longest x1 6.35 us: per_device(): turn_a = lax.ppermute(op_a, 'look', edges)]
    ppermute x6 -> x3, starting transfers between devices: 10.5 us -> 4.85 us  [over_x(): moved.append(lax.ppermute(parts[by], 'swath', perm))]
    ppermute x6 -> x5, waiting for transfers between devices: 8.19 us -> 3.83 us  [over_both(): return lax.ppermute(array, ('look', 'swath'), perm)]
    ppermute x6 -> x5, starting transfers between devices: 10.4 us -> 7.4 us  [over_both(): return lax.ppermute(array, ('look', 'swath'), perm)]
    ppermute x6 -> x3, waiting for transfers between devices: 5.25 us -> 7.36 us  [over_x(): moved.append(lax.ppermute(parts[by], 'swath', perm))]
    unnamed x10 -> x12, local copies, waits for them, and re-layouts: 2.1 us -> 3.53 us
  transfers between devices with their start and end apart: 20 -> 15, of which waited for: 7 -> 9; matrix products, arithmetic and copies ran while one was open for 0% -> 0% of each run, Pallas kernels for 12% -> 12%
where the time goes in v1:
time: 83.9 us; the launch traced here: 83.6 us
  waiting for transfers between devices  30.2 us (36%)
  starting transfers between devices  29.2 us (35%)
  Pallas kernels  20.6 us (25%)
  local copies, waits for them, and re-layouts  3.53 us (4%)
    pallas_call x6, Pallas kernels, call(): pl.pallas_call(kernel, out_shape=[jax.ShapeDtypeStruct(s, t) for s, t in...  20.6 us
    ppermute x1, waiting for transfers between devices, per_device(): turn_b = lax.ppermute(op_b, 'look', edges)  9.9 us
    ppermute x4, waiting for transfers between devices, over_look(): return lax.ppermute(array, 'look', [(i, to(i)) for i in range(nlook)])  7.84 us
    ppermute x5, starting transfers between devices, over_both(): return lax.ppermute(array, ('look', 'swath'), perm)  7.4 us
    ppermute x3, waiting for transfers between devices, over_x(): moved.append(lax.ppermute(parts[by], 'swath', perm))  7.36 us
    ppermute x4, starting transfers between devices, over_look(): return lax.ppermute(array, 'look', [(i, to(i)) for i in range(nlook)])  6.83 us
    ppermute x1, starting transfers between devices, per_device(): turn_a = lax.ppermute(op_a, 'look', edges)  6.35 us
    ppermute x3, starting transfers between devices, over_x(): moved.append(lax.ppermute(parts[by], 'swath', perm))  4.85 us
  transfers between devices with their start and end apart: 15, of which 9 were waited for; matrix products, arithmetic and copies ran while one was open for 0% of the time, Pallas kernels for 12%

profile of v1, /device:TPU:2, one launch (start us, length us, event | category | flops | bytes accessed | tf_op | source)
XLA Modules:
  0.0 83.6 jit_solution(434248049813763619)
XLA Ops:
  0.0 3.7 %forward_send.1.sent_a = bf16[2,2,256,256]{3,2,1,0:T(8,128)(2,1)} custom-call(bf16[2,4,2,512,512]{4,3,2,1,0:T(8,128)(2,1)} %img.3, bf16[32,256,512]{2,1,0:T(8,128)(2,1)} %constant.4.clone.tables), custom_call_target="tpu_custom_call" | custom-call | flops 1200000000 | bytes 1048576 | tf_op jit(solution)/shard_map/forward_send/pallas_call | solution.py:165
  3.7 1.7 %collective-permute-start = (bf16[2,2,256,256]{3,2,1,0:T(8,128)(2,1)}, bf16[2,2,256,256]{3,2,1,0:T(8,128)(2,1)S(1)}, u32[]{:S(2)}, u32[]{:S(2)}) collective-permute-start(bf16[2,2,256,256]{3,2,1,0:T(8,128)(2,1)} %forward_send.1.sent_a), channel_id=1, source_target_pairs={{0,128},{8,136},{16,144},{24,152},{32,160},{40,168},{48,176},{56,1... | collective-permute-start | bytes 1572872 | tf_op jit(solution)/shard_map/ppermute | solution.py:423
  5.4 1.1 %copy-done.3 = bf16[2,2,256,256]{3,2,1,0:T(8,128)(2,1)S(1)} copy-done((bf16[2,2,256,256]{3,2,1,0:T(8,128)(2,1)S(1)}, bf16[2,2,256,256]{3,2,1,0:T(8,128)(2,1)}, u32[]{:S(2)}) %copy-start.3) | copy-done | bytes 524312
  6.4 6.9 %forward_rest.1 = (bf16[4,2,256,256]{3,2,1,0:T(8,128)(2,1)}, bf16[4,2,256,256]{3,2,1,0:T(8,128)(2,1)}, bf16[4,2,256,256]{3,2,1,0:T(8,128)(2,1)}, bf16[2,2,256,256]{3,2,1,0:T(8,128)(2,1)S(1)}) custom-call(bf16[2,4,2,512,512]{4,3,2,1,0:T(8,128)(2,1)} %img.3, bf16[32,256,512]{2,1,0:T(8,128)(2,1)} %constant.4.clone.tables, bf16[2,2,256,256]{3,2,1,0:T(8,128)(2,1)S(1)} %copy-done.3), custom_call_target="tpu_custom_call" | custom-call | flops 3600000000 | bytes 1048576 | tf_op jit(solution)/shard_map/forward_rest/pallas_call | solution.py:165
  13.3 1.3 %collective-permute-start.2 = (bf16[4,2,256,256]{3,2,1,0:T(8,128)(2,1)}, bf16[4,2,256,256]{3,2,1,0:T(8,128)(2,1)S(1)}, u32[]{:S(2)}, u32[]{:S(2)}) collective-permute-start(bf16[4,2,256,256]{3,2,1,0:T(8,128)(2,1)} %get-tuple-element.24.e0), channel_id=1, source_target_pairs={{8,0},{16,8},{24,16},{32,24},{40,32},{48,40},{56,48},{64,56},{72,6... | collective-permute-start | bytes 3145736 | tf_op jit(solution)/shard_map/ppermute | solution.py:450
  14.6 0.5 collective-permute-start.1
  15.2 2.5 %collective-permute-done.op_a = bf16[2,2,256,256]{3,2,1,0:T(8,128)(2,1)S(1)} collective-permute-done((bf16[2,2,256,256]{3,2,1,0:T(8,128)(2,1)}, bf16[2,2,256,256]{3,2,1,0:T(8,128)(2,1)S(1)}, u32[]{:S(2)}, u32[]{:S(2)}) %collective-permute-start) | collective-permute-done | bytes 524320 | tf_op jit(solution)/shard_map/ppermute | solution.py:423
  17.7 6.4 %collective-permute-start.3 = (bf16[2,2,256,256]{3,2,1,0:T(8,128)(2,1)S(1)}, bf16[2,2,256,256]{3,2,1,0:T(8,128)(2,1)S(1)}, u32[]{:S(2)}, u32[]{:S(2)}) collective-permute-start(bf16[2,2,256,256]{3,2,1,0:T(8,128)(2,1)S(1)} %collective-permute-done.op_a), channel_id=1, source_target_pairs={{0,120},{128,248},{1,121},{129,249},{2,122},{130,250},{3,123},{131... | collective-permute-start | bytes 1572872 | tf_op jit(solution)/shard_map/ppermute | solution.py:452
  24.0 5.3 %collective-permute-done.1.op_b = bf16[2,2,256,256]{3,2,1,0:T(8,128)(2,1)S(1)} collective-permute-done((bf16[2,2,256,256]{3,2,1,0:T(8,128)(2,1)S(1)}, bf16[2,2,256,256]{3,2,1,0:T(8,128)(2,1)S(1)}, u32[]{:S(2)}, u32[]{:S(2)}) %collective-permute-start.1) | collective-permute-done | bytes 524320 | tf_op jit(solution)/shard_map/ppermute | solution.py:423
  29.4 1.3 %collective-permute-done.3.turn_a = bf16[2,2,256,256]{3,2,1,0:T(8,128)(2,1)S(1)} collective-permute-done((bf16[2,2,256,256]{3,2,1,0:T(8,128)(2,1)S(1)}, bf16[2,2,256,256]{3,2,1,0:T(8,128)(2,1)S(1)}, u32[]{:S(2)}, u32[]{:S(2)}) %collective-permute-start.3) | collective-permute-done | bytes 524320 | tf_op jit(solution)/shard_map/ppermute | solution.py:452
  30.7 4.6 %collective-permute-start.5 = (bf16[4,2,256,256]{3,2,1,0:T(8,128)(2,1)}, bf16[4,2,256,256]{3,2,1,0:T(8,128)(2,1)S(1)}, u32[]{:S(2)}, u32[]{:S(2)}) collective-permute-start(bf16[4,2,256,256]{3,2,1,0:T(8,128)(2,1)} %get-tuple-element.32), channel_id=1, source_target_pairs={{0,248},{8,0},{16,8},{24,16},{32,24},{40,32},{48,40},{56,48},{64,5... | collective-permute-start | bytes 3145736 | tf_op jit(solution)/shard_map/ppermute | solution.py:423
  35.3 2.4 %collective-permute-start.6 = (bf16[2,2,256,256]{3,2,1,0:T(8,128)(2,1)S(1)}, bf16[2,2,256,256]{3,2,1,0:T(8,128)(2,1)S(1)}, u32[]{:S(2)}, u32[]{:S(2)}) collective-permute-start(bf16[2,2,256,256]{3,2,1,0:T(8,128)(2,1)S(1)} %collective-permute-done.1.op_b), channel_id=1, source_target_pairs={{0,120},{128,248},{1,121},{129,249},{2,122},{130,250},{3,123},{131... | collective-permute-start | bytes 1572872 | tf_op jit(solution)/shard_map/ppermute | solution.py:454
  37.8 1.2 %copy-done = bf16[4,2,256,256]{3,2,1,0:T(8,128)(2,1)S(1)} copy-done((bf16[4,2,256,256]{3,2,1,0:T(8,128)(2,1)S(1)}, bf16[4,2,256,256]{3,2,1,0:T(8,128)(2,1)}, u32[]{:S(2)}) %copy-start) | copy-done | bytes 1048600
  39.0 1.2 %copy-done.1 = bf16[4,2,256,256]{3,2,1,0:T(8,128)(2,1)S(1)} copy-done((bf16[4,2,256,256]{3,2,1,0:T(8,128)(2,1)S(1)}, bf16[4,2,256,256]{3,2,1,0:T(8,128)(2,1)}, u32[]{:S(2)}) %copy-start.1) | copy-done | bytes 1048600
  40.2 3.3 %surfaces_early.1 = (bf16[3,256,256]{2,1,0:T(8,128)(2,1)S(1)}, f32[3,8,128]{2,1,0:T(8,128)S(1)}) custom-call(f32[4]{0:T(128)S(1)} %copy-done.4, bf16[3,256,512]{2,1,0:T(8,128)(2,1)S(1)} %copy-done.2, bf16[4,2,256,256]{3,2,1,0:T(8,128)(2,1)S(1)} %copy-done, bf16[4,2,256,256]{3,2,1,0:T(8,128)(2,1)S(1)} %copy-done.1, ...), custom_call_target="tpu_custom_call" | custom-call | flops 750000000 | bytes 1048576 | tf_op jit(solution)/shard_map/surfaces_early/pallas_call | solution.py:165
  43.5 9.9 %collective-permute-done.6.turn_b = bf16[2,2,256,256]{3,2,1,0:T(8,128)(2,1)S(1)} collective-permute-done((bf16[2,2,256,256]{3,2,1,0:T(8,128)(2,1)S(1)}, bf16[2,2,256,256]{3,2,1,0:T(8,128)(2,1)S(1)}, u32[]{:S(2)}, u32[]{:S(2)}) %collective-permute-start.6) | collective-permute-done | bytes 524320 | tf_op jit(solution)/shard_map/ppermute | solution.py:454
  53.4 5.2 %surfaces_late.1 = (bf16[2,272,256]{2,1,0:T(8,128)(2,1)S(1)}, bf16[2,272,256]{2,1,0:T(8,128)(2,1)S(1)}, bf16[2,272,256]{2,1,0:T(8,128)(2,1)S(1)}, bf16[2,272,256]{2,1,0:T(8,128)(2,1)S(1)}) custom-call(f32[4]{0:T(128)S(1)} %copy-done.4, bf16[3,256,512]{2,1,0:T(8,128)(2,1)S(1)} %copy-done.2, bf16[3,256,256]{2,1,0:T(8,128)(2,1)S(1)} %get-tuple-element.28.early, ...), custom_call_target="tpu_custom_call" | custom-call | flops 1250000000 | bytes 1048576 | tf_op jit(solution)/shard_map/surfaces_late/pallas_call | solution.py:165
  58.7 1.6 %collective-permute-start.7 = (bf16[2,272,256]{2,1,0:T(8,128)(2,1)S(1)}, bf16[2,272,256]{2,1,0:T(8,128)(2,1)S(1)}, u32[]{:S(2)}, u32[]{:S(2)}) collective-permute-start(bf16[2,272,256]{2,1,0:T(8,128)(2,1)S(1)} %get-tuple-element.34), channel_id=1, source_target_pairs={{0,1},{1,2},{2,3},{3,0},{4,5},{5,6},{6,7},{7,4},{8,9},{9,10},{10,1... | collective-permute-start | bytes 835592 | tf_op jit(solution)/shard_map/ppermute | solution.py:429
  60.2 1.1 %collective-permute-start.8 = (bf16[2,272,256]{2,1,0:T(8,128)(2,1)S(1)}, bf16[2,272,256]{2,1,0:T(8,128)(2,1)S(1)}, u32[]{:S(2)}, u32[]{:S(2)}) collective-permute-start(bf16[2,272,256]{2,1,0:T(8,128)(2,1)S(1)} %get-tuple-element.35), channel_id=1, source_target_pairs={{0,2},{1,3},{2,0},{3,1},{4,6},{5,7},{6,4},{7,5},{8,10},{9,11},{10,... | collective-permute-start | bytes 835592 | tf_op jit(solution)/shard_map/ppermute | solution.py:429
  61.4 2.2 %collective-permute-start.9 = (bf16[2,272,256]{2,1,0:T(8,128)(2,1)S(1)}, bf16[2,272,256]{2,1,0:T(8,128)(2,1)S(1)}, u32[]{:S(2)}, u32[]{:S(2)}) collective-permute-start(bf16[2,272,256]{2,1,0:T(8,128)(2,1)S(1)} %get-tuple-element.36), channel_id=1, source_target_pairs={{0,3},{1,0},{2,1},{3,2},{4,7},{5,4},{6,5},{7,6},{8,11},{9,8},{10,9... | collective-permute-start | bytes 835592 | tf_op jit(solution)/shard_map/ppermute | solution.py:429
  63.5 1.8 %collective-permute-done.7.b = bf16[2,272,256]{2,1,0:T(8,128)(2,1)S(1)} collective-permute-done((bf16[2,272,256]{2,1,0:T(8,128)(2,1)S(1)}, bf16[2,272,256]{2,1,0:T(8,128)(2,1)S(1)}, u32[]{:S(2)}, u32[]{:S(2)}) %collective-permute-start.7) | collective-permute-done | bytes 278560 | tf_op jit(solution)/shard_map/ppermute | solution.py:429
  65.3 3.1 %collective-permute-done.8.c = bf16[2,272,256]{2,1,0:T(8,128)(2,1)S(1)} collective-permute-done((bf16[2,272,256]{2,1,0:T(8,128)(2,1)S(1)}, bf16[2,272,256]{2,1,0:T(8,128)(2,1)S(1)}, u32[]{:S(2)}, u32[]{:S(2)}) %collective-permute-start.8) | collective-permute-done | bytes 278560 | tf_op jit(solution)/shard_map/ppermute | solution.py:429
  68.4 2.5 %collective-permute-done.9.d = bf16[2,272,256]{2,1,0:T(8,128)(2,1)S(1)} collective-permute-done((bf16[2,272,256]{2,1,0:T(8,128)(2,1)S(1)}, bf16[2,272,256]{2,1,0:T(8,128)(2,1)S(1)}, u32[]{:S(2)}, u32[]{:S(2)}) %collective-permute-start.9) | collective-permute-done | bytes 278560 | tf_op jit(solution)/shard_map/ppermute | solution.py:429
  70.9 0.2 gather.1
  71.0 2.8 %collective-permute-start.10 = (bf16[144,256]{1,0:T(8,128)(2,1)S(1)}, bf16[144,256]{1,0:T(8,128)(2,1)S(1)}, u32[]{:S(2)}, u32[]{:S(2)}) collective-permute-start(bf16[144,256]{1,0:T(8,128)(2,1)S(1)} %get-tuple-element.38), channel_id=1, source_target_pairs={{0,4},{1,5},{2,6},{3,7},{4,0},{5,1},{6,2},{7,3},{8,12},{9,13},{10,... | collective-permute-start | bytes 221192 | tf_op jit(solution)/shard_map/ppermute | solution.py:438
  73.9 1.8 %collective-permute-start.11 = (bf16[112,256]{1,0:T(8,128)(2,1)S(1)}, bf16[112,256]{1,0:T(8,128)(2,1)S(1)}, u32[]{:S(2)}, u32[]{:S(2)}) collective-permute-start(bf16[112,256]{1,0:T(8,128)(2,1)S(1)} %get-tuple-element.39), channel_id=1, source_target_pairs={{0,248},{1,249},{2,250},{3,251},{4,252},{5,253},{6,254},{7,255},{8... | collective-permute-start | bytes 172040 | tf_op jit(solution)/shard_map/ppermute | solution.py:438
  75.6 0.3 collective-permute-start.12
  76.0 1.2 %collective-permute-start.13 = (bf16[48,256]{1,0:T(8,128)(2,1)S(1)}, bf16[48,256]{1,0:T(8,128)(2,1)S(1)}, u32[]{:S(2)}, u32[]{:S(2)}) collective-permute-start(bf16[48,256]{1,0:T(8,128)(2,1)S(1)} %get-tuple-element.41), channel_id=1, source_target_pairs={{0,128},{1,129},{2,130},{3,131},{4,132},{5,133},{6,134},{7,135},{8... | collective-permute-start | bytes 73736 | tf_op jit(solution)/shard_map/ppermute | solution.py:438
  77.2 1.2 %collective-permute-start.14 = (bf16[48,256]{1,0:T(8,128)(2,1)S(1)}, bf16[48,256]{1,0:T(8,128)(2,1)S(1)}, u32[]{:S(2)}, u32[]{:S(2)}) collective-permute-start(bf16[48,256]{1,0:T(8,128)(2,1)S(1)} %get-tuple-element.42), channel_id=1, source_target_pairs={{0,132},{1,133},{2,134},{3,135},{4,128},{5,129},{6,130},{7,131},{8... | collective-permute-start | bytes 73736 | tf_op jit(solution)/shard_map/ppermute | solution.py:438
  78.4 1.4 %collective-permute-done.13.opp_a = bf16[48,256]{1,0:T(8,128)(2,1)S(1)} collective-permute-done((bf16[48,256]{1,0:T(8,128)(2,1)S(1)}, bf16[48,256]{1,0:T(8,128)(2,1)S(1)}, u32[]{:S(2)}, u32[]{:S(2)}) %collective-permute-start.13) | collective-permute-done | bytes 24608 | tf_op jit(solution)/shard_map/ppermute | solution.py:438
  79.8 2.5 %collective-permute-done.14.opp_b = bf16[48,256]{1,0:T(8,128)(2,1)S(1)} collective-permute-done((bf16[48,256]{1,0:T(8,128)(2,1)S(1)}, bf16[48,256]{1,0:T(8,128)(2,1)S(1)}, u32[]{:S(2)}, u32[]{:S(2)}) %collective-permute-start.14) | collective-permute-done | bytes 24608 | tf_op jit(solution)/shard_map/ppermute | solution.py:438
  82.3 1.3 %final.1 = f32[2,4,32,256]{3,2,1,0:T(8,128)} custom-call(s32[2,4]{1,0:T(2,128)S(1)} %copy-done.5, f32[144,256]{1,0:T(8,128)S(1)} %get-tuple-element.37.keep, bf16[144,256]{1,0:T(8,128)(2,1)S(1)} %collective-permute-done.10.near, bf16[112,256]{1,0:T(8,128)(2,1)S(1)} %collective-permute-done.11.back_a, bf16[112,256]{1,0:T(8,128)(2,1)S(1)} %collective-permute-done.12.back_b, ...), custom_call_target="tpu_custom_call" | custom-call | flops 10000000 | bytes 1048576 | tf_op jit(solution)/shard_map/final/pallas_call | solution.py:165
  (16 shorter events, 0.0 us)
Async XLA Ops:
  3.7 34.1 %copy-start.2 = (bf16[3,256,512]{2,1,0:T(8,128)(2,1)S(1)}, bf16[3,256,512]{2,1,0:T(8,128)(2,1)}, u32[]{:S(2)}) copy-start(bf16[3,256,512]{2,1,0:T(8,128)(2,1)} %constant.5.clone.tab) | copy-start | bytes 2359300
  3.7 14.0 %collective-permute-start = (bf16[2,2,256,256]{3,2,1,0:T(8,128)(2,1)}, bf16[2,2,256,256]{3,2,1,0:T(8,128)(2,1)S(1)}, u32[]{:S(2)}, u32[]{:S(2)}) collective-permute-start(bf16[2,2,256,256]{3,2,1,0:T(8,128)(2,1)} %forward_send.1.sent_a), channel_id=1, source_target_pairs={{0,128},{8,136},{16,144},{24,152},{32,160},{40,168},{48,176},{56,1... | collective-permute-start | bytes 1572872 | tf_op jit(solution)/shard_map/ppermute | solution.py:423
  5.4 1.1 %copy-start.3 = (bf16[2,2,256,256]{3,2,1,0:T(8,128)(2,1)S(1)}, bf16[2,2,256,256]{3,2,1,0:T(8,128)(2,1)}, u32[]{:S(2)}) copy-start(bf16[2,2,256,256]{3,2,1,0:T(8,128)(2,1)} %forward_send.1.sent_a) | copy-start | bytes 1572868
  6.4 31.3 %copy-start.4 = (f32[4]{0:T(128)S(1)}, f32[4]{0:T(128)}, u32[]{:S(2)}) copy-start(f32[4]{0:T(128)} %weight.3) | copy-start | bytes 52
  13.3 69.0 %copy-start.5 = (s32[2,4]{1,0:T(2,128)S(1)}, s32[2,4]{1,0:T(2,128)}, u32[]{:S(2)}) copy-start(s32[2,4]{1,0:T(2,128)} %mask.1) | copy-start | bytes 100
  13.3 17.3 %collective-permute-start.2 = (bf16[4,2,256,256]{3,2,1,0:T(8,128)(2,1)}, bf16[4,2,256,256]{3,2,1,0:T(8,128)(2,1)S(1)}, u32[]{:S(2)}, u32[]{:S(2)}) collective-permute-start(bf16[4,2,256,256]{3,2,1,0:T(8,128)(2,1)} %get-tuple-element.24.e0), channel_id=1, source_target_pairs={{8,0},{16,8},{24,16},{32,24},{40,32},{48,40},{56,48},{64,56},{72,6... | collective-permute-start | bytes 3145736 | tf_op jit(solution)/shard_map/ppermute | solution.py:450
  14.6 14.7 %collective-permute-start.1 = (bf16[2,2,256,256]{3,2,1,0:T(8,128)(2,1)S(1)}, bf16[2,2,256,256]{3,2,1,0:T(8,128)(2,1)S(1)}, u32[]{:S(2)}, u32[]{:S(2)}) collective-permute-start(bf16[2,2,256,256]{3,2,1,0:T(8,128)(2,1)S(1)} %get-tuple-element.26), channel_id=1, source_target_pairs={{0,128},{8,136},{16,144},{24,152},{32,160},{40,168},{48,176},{56,1... | collective-permute-start | bytes 1572872 | tf_op jit(solution)/shard_map/ppermute | solution.py:423
  17.7 13.0 %collective-permute-start.3 = (bf16[2,2,256,256]{3,2,1,0:T(8,128)(2,1)S(1)}, bf16[2,2,256,256]{3,2,1,0:T(8,128)(2,1)S(1)}, u32[]{:S(2)}, u32[]{:S(2)}) collective-permute-start(bf16[2,2,256,256]{3,2,1,0:T(8,128)(2,1)S(1)} %collective-permute-done.op_a), channel_id=1, source_target_pairs={{0,120},{128,248},{1,121},{129,249},{2,122},{130,250},{3,123},{131... | collective-permute-start | bytes 1572872 | tf_op jit(solution)/shard_map/ppermute | solution.py:452
  30.7 22.8 %collective-permute-start.4 = (bf16[4,2,256,256]{3,2,1,0:T(8,128)(2,1)}, bf16[4,2,256,256]{3,2,1,0:T(8,128)(2,1)S(1)}, u32[]{:S(2)}, u32[]{:S(2)}) collective-permute-start(bf16[4,2,256,256]{3,2,1,0:T(8,128)(2,1)} %get-tuple-element.30.e1), channel_id=1, source_target_pairs={{0,8},{8,16},{16,24},{24,32},{32,40},{40,48},{48,56},{56,64},{64,7... | collective-permute-start | bytes 3145736 | tf_op jit(solution)/shard_map/ppermute | solution.py:423
  30.7 22.8 %collective-permute-start.5 = (bf16[4,2,256,256]{3,2,1,0:T(8,128)(2,1)}, bf16[4,2,256,256]{3,2,1,0:T(8,128)(2,1)S(1)}, u32[]{:S(2)}, u32[]{:S(2)}) collective-permute-start(bf16[4,2,256,256]{3,2,1,0:T(8,128)(2,1)} %get-tuple-element.32), channel_id=1, source_target_pairs={{0,248},{8,0},{16,8},{24,16},{32,24},{40,32},{48,40},{56,48},{64,5... | collective-permute-start | bytes 3145736 | tf_op jit(solution)/shard_map/ppermute | solution.py:423
  35.3 18.1 %collective-permute-start.6 = (bf16[2,2,256,256]{3,2,1,0:T(8,128)(2,1)S(1)}, bf16[2,2,256,256]{3,2,1,0:T(8,128)(2,1)S(1)}, u32[]{:S(2)}, u32[]{:S(2)}) collective-permute-start(bf16[2,2,256,256]{3,2,1,0:T(8,128)(2,1)S(1)} %collective-permute-done.1.op_b), channel_id=1, source_target_pairs={{0,120},{128,248},{1,121},{129,249},{2,122},{130,250},{3,123},{131... | collective-permute-start | bytes 1572872 | tf_op jit(solution)/shard_map/ppermute | solution.py:454
  37.8 1.2 %copy-start = (bf16[4,2,256,256]{3,2,1,0:T(8,128)(2,1)S(1)}, bf16[4,2,256,256]{3,2,1,0:T(8,128)(2,1)}, u32[]{:S(2)}) copy-start(bf16[4,2,256,256]{3,2,1,0:T(8,128)(2,1)} %get-tuple-element.24.e0) | copy-start | bytes 3145732
  39.0 1.2 %copy-start.1 = (bf16[4,2,256,256]{3,2,1,0:T(8,128)(2,1)S(1)}, bf16[4,2,256,256]{3,2,1,0:T(8,128)(2,1)}, u32[]{:S(2)}) copy-start(bf16[4,2,256,256]{3,2,1,0:T(8,128)(2,1)} %get-tuple-element.30.e1) | copy-start | bytes 3145732
  58.7 6.6 %collective-permute-start.7 = (bf16[2,272,256]{2,1,0:T(8,128)(2,1)S(1)}, bf16[2,272,256]{2,1,0:T(8,128)(2,1)S(1)}, u32[]{:S(2)}, u32[]{:S(2)}) collective-permute-start(bf16[2,272,256]{2,1,0:T(8,128)(2,1)S(1)} %get-tuple-element.34), channel_id=1, source_target_pairs={{0,1},{1,2},{2,3},{3,0},{4,5},{5,6},{6,7},{7,4},{8,9},{9,10},{10,1... | collective-permute-start | bytes 835592 | tf_op jit(solution)/shard_map/ppermute | solution.py:429
  60.2 8.2 %collective-permute-start.8 = (bf16[2,272,256]{2,1,0:T(8,128)(2,1)S(1)}, bf16[2,272,256]{2,1,0:T(8,128)(2,1)S(1)}, u32[]{:S(2)}, u32[]{:S(2)}) collective-permute-start(bf16[2,272,256]{2,1,0:T(8,128)(2,1)S(1)} %get-tuple-element.35), channel_id=1, source_target_pairs={{0,2},{1,3},{2,0},{3,1},{4,6},{5,7},{6,4},{7,5},{8,10},{9,11},{10,... | collective-permute-start | bytes 835592 | tf_op jit(solution)/shard_map/ppermute | solution.py:429
  61.4 9.5 %collective-permute-start.9 = (bf16[2,272,256]{2,1,0:T(8,128)(2,1)S(1)}, bf16[2,272,256]{2,1,0:T(8,128)(2,1)S(1)}, u32[]{:S(2)}, u32[]{:S(2)}) collective-permute-start(bf16[2,272,256]{2,1,0:T(8,128)(2,1)S(1)} %get-tuple-element.36), channel_id=1, source_target_pairs={{0,3},{1,0},{2,1},{3,2},{4,7},{5,4},{6,5},{7,6},{8,11},{9,8},{10,9... | collective-permute-start | bytes 835592 | tf_op jit(solution)/shard_map/ppermute | solution.py:429
  71.0 11.2 %collective-permute-start.10 = (bf16[144,256]{1,0:T(8,128)(2,1)S(1)}, bf16[144,256]{1,0:T(8,128)(2,1)S(1)}, u32[]{:S(2)}, u32[]{:S(2)}) collective-permute-start(bf16[144,256]{1,0:T(8,128)(2,1)S(1)} %get-tuple-element.38), channel_id=1, source_target_pairs={{0,4},{1,5},{2,6},{3,7},{4,0},{5,1},{6,2},{7,3},{8,12},{9,13},{10,... | collective-permute-start | bytes 221192 | tf_op jit(solution)/shard_map/ppermute | solution.py:438
  73.9 8.4 %collective-permute-start.11 = (bf16[112,256]{1,0:T(8,128)(2,1)S(1)}, bf16[112,256]{1,0:T(8,128)(2,1)S(1)}, u32[]{:S(2)}, u32[]{:S(2)}) collective-permute-start(bf16[112,256]{1,0:T(8,128)(2,1)S(1)} %get-tuple-element.39), channel_id=1, source_target_pairs={{0,248},{1,249},{2,250},{3,251},{4,252},{5,253},{6,254},{7,255},{8... | collective-permute-start | bytes 172040 | tf_op jit(solution)/shard_map/ppermute | solution.py:438
  75.6 6.6 %collective-permute-start.12 = (bf16[112,256]{1,0:T(8,128)(2,1)S(1)}, bf16[112,256]{1,0:T(8,128)(2,1)S(1)}, u32[]{:S(2)}, u32[]{:S(2)}) collective-permute-start(bf16[112,256]{1,0:T(8,128)(2,1)S(1)} %get-tuple-element.40), channel_id=1, source_target_pairs={{0,252},{1,253},{2,254},{3,255},{4,248},{5,249},{6,250},{7,251},{8... | collective-permute-start | bytes 172040 | tf_op jit(solution)/shard_map/ppermute | solution.py:438
  76.0 3.8 %collective-permute-start.13 = (bf16[48,256]{1,0:T(8,128)(2,1)S(1)}, bf16[48,256]{1,0:T(8,128)(2,1)S(1)}, u32[]{:S(2)}, u32[]{:S(2)}) collective-permute-start(bf16[48,256]{1,0:T(8,128)(2,1)S(1)} %get-tuple-element.41), channel_id=1, source_target_pairs={{0,128},{1,129},{2,130},{3,131},{4,132},{5,133},{6,134},{7,135},{8... | collective-permute-start | bytes 73736 | tf_op jit(solution)/shard_map/ppermute | solution.py:438
  77.2 5.0 %collective-permute-start.14 = (bf16[48,256]{1,0:T(8,128)(2,1)S(1)}, bf16[48,256]{1,0:T(8,128)(2,1)S(1)}, u32[]{:S(2)}, u32[]{:S(2)}) collective-permute-start(bf16[48,256]{1,0:T(8,128)(2,1)S(1)} %get-tuple-element.42), channel_id=1, source_target_pairs={{0,132},{1,133},{2,134},{3,135},{4,128},{5,129},{6,130},{7,131},{8... | collective-permute-start | bytes 73736 | tf_op jit(solution)/shard_map/ppermute | solution.py:438

commit v2 on v1

--- a/solution.py
+++ b/solution.py
@@ -452,8 +452,8 @@
     turn_a = lax.ppermute(op_a, "look", edges)
     op_b = after(op_b, pl0, turn_a)
     turn_b = lax.ppermute(op_b, "look", edges)
-    pl1 = over_look(after(wrapped, op_b), behind)
-    q1 = over_look(after(e1, op_b), ahead)
+    pl1 = over_look(after(wrapped, op_a), behind)
+    q1 = over_look(after(e1, op_a), ahead)
 
     vm = lambda *arrays: [("v", a) for a in arrays]
     common = [("s", patch_weight), ("v", inverse_tables)]

time: 83.9 us -> 86.7 us (1.033)
  starting transfers between devices: 29.2 us -> 36.4 us
  waiting for transfers between devices: 30.2 us -> 25.1 us
    ppermute x1, waiting for transfers between devices: 9.9 us -> 4.95 us  [per_device(): turn_b = lax.ppermute(op_b, 'look', edges)]
    ppermute x5, starting transfers between devices: 7.4 us -> 11.7 us  [over_both(): return lax.ppermute(array, ('look', 'swath'), perm)]
    ppermute x3, waiting for transfers between devices: 7.36 us -> 11.6 us  [over_x(): moved.append(lax.ppermute(parts[by], 'swath', perm))]
    ppermute x4, waiting for transfers between devices: 7.84 us -> 3.9 us  [over_look(): return lax.ppermute(array, 'look', [(i, to(i)) for i in range(nlook)])]
    ppermute x1, starting transfers between devices: 2.45 us -> 6.13 us  [per_device(): turn_b = lax.ppermute(op_b, 'look', edges)]
where the time goes in v2:
time: 86.7 us; the launch traced here: 85.8 us
  starting transfers between devices  36.4 us (42%)
  waiting for transfers between devices  25.1 us (29%)
  Pallas kernels  20.6 us (24%)
  local copies, waits for them, and re-layouts  3.53 us (4%)
    pallas_call x6, Pallas kernels, call(): pl.pallas_call(kernel, out_shape=[jax.ShapeDtypeStruct(s, t) for s, t in...  20.6 us
    ppermute x5, starting transfers between devices, over_both(): return lax.ppermute(array, ('look', 'swath'), perm)  11.7 us
    ppermute x3, waiting for transfers between devices, over_x(): moved.append(lax.ppermute(parts[by], 'swath', perm))  11.6 us
    ppermute x1, starting transfers between devices, per_device(): turn_a = lax.ppermute(op_a, 'look', edges)  6.35 us
    ppermute x1, starting transfers between devices, per_device(): turn_b = lax.ppermute(op_b, 'look', edges)  6.13 us
    ppermute x4, starting transfers between devices, over_look(): return lax.ppermute(array, 'look', [(i, to(i)) for i in range(nlook)])  6.12 us
    ppermute x1, waiting for transfers between devices, per_device(): turn_b = lax.ppermute(op_b, 'look', edges)  4.95 us
    ppermute x3, starting transfers between devices, over_x(): moved.append(lax.ppermute(parts[by], 'swath', perm))  4.83 us
  transfers between devices with their start and end apart: 15, of which 9 were waited for; matrix products, arithmetic and copies ran while one was open for 0% of the time, Pallas kernels for 12%

profile of v2, /device:TPU:2, one launch (start us, length us, event | category | flops | bytes accessed | tf_op | source)
XLA Modules:
  0.0 85.8 jit_solution(7146746805335733813)
XLA Ops:
  0.0 3.7 %forward_send.1.sent_a = bf16[2,2,256,256]{3,2,1,0:T(8,128)(2,1)} custom-call(bf16[2,4,2,512,512]{4,3,2,1,0:T(8,128)(2,1)} %img.3, bf16[32,256,512]{2,1,0:T(8,128)(2,1)} %constant.4.clone.tables), custom_call_target="tpu_custom_call" | custom-call | flops 1200000000 | bytes 1048576 | tf_op jit(solution)/shard_map/forward_send/pallas_call | solution.py:165
  3.7 1.7 %collective-permute-start = (bf16[2,2,256,256]{3,2,1,0:T(8,128)(2,1)}, bf16[2,2,256,256]{3,2,1,0:T(8,128)(2,1)S(1)}, u32[]{:S(2)}, u32[]{:S(2)}) collective-permute-start(bf16[2,2,256,256]{3,2,1,0:T(8,128)(2,1)} %forward_send.1.sent_a), channel_id=1, source_target_pairs={{0,128},{8,136},{16,144},{24,152},{32,160},{40,168},{48,176},{56,1... | collective-permute-start | bytes 1572872 | tf_op jit(solution)/shard_map/ppermute | solution.py:423
  5.4 1.1 %copy-done.3 = bf16[2,2,256,256]{3,2,1,0:T(8,128)(2,1)S(1)} copy-done((bf16[2,2,256,256]{3,2,1,0:T(8,128)(2,1)S(1)}, bf16[2,2,256,256]{3,2,1,0:T(8,128)(2,1)}, u32[]{:S(2)}) %copy-start.3) | copy-done | bytes 524312
  6.4 6.9 %forward_rest.1 = (bf16[4,2,256,256]{3,2,1,0:T(8,128)(2,1)}, bf16[4,2,256,256]{3,2,1,0:T(8,128)(2,1)}, bf16[4,2,256,256]{3,2,1,0:T(8,128)(2,1)}, bf16[2,2,256,256]{3,2,1,0:T(8,128)(2,1)S(1)}) custom-call(bf16[2,4,2,512,512]{4,3,2,1,0:T(8,128)(2,1)} %img.3, bf16[32,256,512]{2,1,0:T(8,128)(2,1)} %constant.4.clone.tables, bf16[2,2,256,256]{3,2,1,0:T(8,128)(2,1)S(1)} %copy-done.3), custom_call_target="tpu_custom_call" | custom-call | flops 3600000000 | bytes 1048576 | tf_op jit(solution)/shard_map/forward_rest/pallas_call | solution.py:165
  13.3 1.3 %collective-permute-start.2 = (bf16[4,2,256,256]{3,2,1,0:T(8,128)(2,1)}, bf16[4,2,256,256]{3,2,1,0:T(8,128)(2,1)S(1)}, u32[]{:S(2)}, u32[]{:S(2)}) collective-permute-start(bf16[4,2,256,256]{3,2,1,0:T(8,128)(2,1)} %get-tuple-element.24.e0), channel_id=1, source_target_pairs={{8,0},{16,8},{24,16},{32,24},{40,32},{48,40},{56,48},{64,56},{72,6... | collective-permute-start | bytes 3145736 | tf_op jit(solution)/shard_map/ppermute | solution.py:450
  14.6 0.5 collective-permute-start.1
  15.2 2.5 %collective-permute-done.op_a = bf16[2,2,256,256]{3,2,1,0:T(8,128)(2,1)S(1)} collective-permute-done((bf16[2,2,256,256]{3,2,1,0:T(8,128)(2,1)}, bf16[2,2,256,256]{3,2,1,0:T(8,128)(2,1)S(1)}, u32[]{:S(2)}, u32[]{:S(2)}) %collective-permute-start) | collective-permute-done | bytes 524320 | tf_op jit(solution)/shard_map/ppermute | solution.py:423
  17.7 6.4 %collective-permute-start.3 = (bf16[2,2,256,256]{3,2,1,0:T(8,128)(2,1)S(1)}, bf16[2,2,256,256]{3,2,1,0:T(8,128)(2,1)S(1)}, u32[]{:S(2)}, u32[]{:S(2)}) collective-permute-start(bf16[2,2,256,256]{3,2,1,0:T(8,128)(2,1)S(1)} %collective-permute-done.op_a), channel_id=1, source_target_pairs={{0,120},{128,248},{1,121},{129,249},{2,122},{130,250},{3,123},{131... | collective-permute-start | bytes 1572872 | tf_op jit(solution)/shard_map/ppermute | solution.py:452
  24.0 0.1 collective-permute-start.4
  24.1 3.8 %collective-permute-start.5 = (bf16[4,2,256,256]{3,2,1,0:T(8,128)(2,1)}, bf16[4,2,256,256]{3,2,1,0:T(8,128)(2,1)S(1)}, u32[]{:S(2)}, u32[]{:S(2)}) collective-permute-start(bf16[4,2,256,256]{3,2,1,0:T(8,128)(2,1)} %get-tuple-element.32), channel_id=1, source_target_pairs={{0,248},{8,0},{16,8},{24,16},{32,24},{40,32},{48,40},{56,48},{64,5... | collective-permute-start | bytes 3145736 | tf_op jit(solution)/shard_map/ppermute | solution.py:423
  27.9 1.4 %collective-permute-done.1.op_b = bf16[2,2,256,256]{3,2,1,0:T(8,128)(2,1)S(1)} collective-permute-done((bf16[2,2,256,256]{3,2,1,0:T(8,128)(2,1)S(1)}, bf16[2,2,256,256]{3,2,1,0:T(8,128)(2,1)S(1)}, u32[]{:S(2)}, u32[]{:S(2)}) %collective-permute-start.1) | collective-permute-done | bytes 524320 | tf_op jit(solution)/shard_map/ppermute | solution.py:423
  29.4 1.3 %collective-permute-done.3.turn_a = bf16[2,2,256,256]{3,2,1,0:T(8,128)(2,1)S(1)} collective-permute-done((bf16[2,2,256,256]{3,2,1,0:T(8,128)(2,1)S(1)}, bf16[2,2,256,256]{3,2,1,0:T(8,128)(2,1)S(1)}, u32[]{:S(2)}, u32[]{:S(2)}) %collective-permute-start.3) | collective-permute-done | bytes 524320 | tf_op jit(solution)/shard_map/ppermute | solution.py:452
  30.7 6.1 %collective-permute-start.6 = (bf16[2,2,256,256]{3,2,1,0:T(8,128)(2,1)S(1)}, bf16[2,2,256,256]{3,2,1,0:T(8,128)(2,1)S(1)}, u32[]{:S(2)}, u32[]{:S(2)}) collective-permute-start(bf16[2,2,256,256]{3,2,1,0:T(8,128)(2,1)S(1)} %collective-permute-done.1.op_b), channel_id=1, source_target_pairs={{0,120},{128,248},{1,121},{129,249},{2,122},{130,250},{3,123},{131... | collective-permute-start | bytes 1572872 | tf_op jit(solution)/shard_map/ppermute | solution.py:454
  36.8 1.2 %copy-done = bf16[4,2,256,256]{3,2,1,0:T(8,128)(2,1)S(1)} copy-done((bf16[4,2,256,256]{3,2,1,0:T(8,128)(2,1)S(1)}, bf16[4,2,256,256]{3,2,1,0:T(8,128)(2,1)}, u32[]{:S(2)}) %copy-start) | copy-done | bytes 1048600
  38.0 1.2 %copy-done.1 = bf16[4,2,256,256]{3,2,1,0:T(8,128)(2,1)S(1)} copy-done((bf16[4,2,256,256]{3,2,1,0:T(8,128)(2,1)S(1)}, bf16[4,2,256,256]{3,2,1,0:T(8,128)(2,1)}, u32[]{:S(2)}) %copy-start.1) | copy-done | bytes 1048600
  39.3 3.3 %surfaces_early.1 = (bf16[3,256,256]{2,1,0:T(8,128)(2,1)S(1)}, f32[3,8,128]{2,1,0:T(8,128)S(1)}) custom-call(f32[4]{0:T(128)S(1)} %copy-done.4, bf16[3,256,512]{2,1,0:T(8,128)(2,1)S(1)} %copy-done.2, bf16[4,2,256,256]{3,2,1,0:T(8,128)(2,1)S(1)} %copy-done, bf16[4,2,256,256]{3,2,1,0:T(8,128)(2,1)S(1)} %copy-done.1, ...), custom_call_target="tpu_custom_call" | custom-call | flops 750000000 | bytes 1048576 | tf_op jit(solution)/shard_map/surfaces_early/pallas_call | solution.py:165
  42.6 5.0 %collective-permute-done.6.turn_b = bf16[2,2,256,256]{3,2,1,0:T(8,128)(2,1)S(1)} collective-permute-done((bf16[2,2,256,256]{3,2,1,0:T(8,128)(2,1)S(1)}, bf16[2,2,256,256]{3,2,1,0:T(8,128)(2,1)S(1)}, u32[]{:S(2)}, u32[]{:S(2)}) %collective-permute-start.6) | collective-permute-done | bytes 524320 | tf_op jit(solution)/shard_map/ppermute | solution.py:454
  47.6 5.2 %surfaces_late.1 = (bf16[2,272,256]{2,1,0:T(8,128)(2,1)S(1)}, bf16[2,272,256]{2,1,0:T(8,128)(2,1)S(1)}, bf16[2,272,256]{2,1,0:T(8,128)(2,1)S(1)}, bf16[2,272,256]{2,1,0:T(8,128)(2,1)S(1)}) custom-call(f32[4]{0:T(128)S(1)} %copy-done.4, bf16[3,256,512]{2,1,0:T(8,128)(2,1)S(1)} %copy-done.2, bf16[3,256,256]{2,1,0:T(8,128)(2,1)S(1)} %get-tuple-element.28.early, ...), custom_call_target="tpu_custom_call" | custom-call | flops 1250000000 | bytes 1048576 | tf_op jit(solution)/shard_map/surfaces_late/pallas_call | solution.py:165
  52.8 1.6 %collective-permute-start.7 = (bf16[2,272,256]{2,1,0:T(8,128)(2,1)S(1)}, bf16[2,272,256]{2,1,0:T(8,128)(2,1)S(1)}, u32[]{:S(2)}, u32[]{:S(2)}) collective-permute-start(bf16[2,272,256]{2,1,0:T(8,128)(2,1)S(1)} %get-tuple-element.34), channel_id=1, source_target_pairs={{0,1},{1,2},{2,3},{3,0},{4,5},{5,6},{6,7},{7,4},{8,9},{9,10},{10,1... | collective-permute-start | bytes 835592 | tf_op jit(solution)/shard_map/ppermute | solution.py:429
  54.4 1.7 %collective-permute-start.8 = (bf16[2,272,256]{2,1,0:T(8,128)(2,1)S(1)}, bf16[2,272,256]{2,1,0:T(8,128)(2,1)S(1)}, u32[]{:S(2)}, u32[]{:S(2)}) collective-permute-start(bf16[2,272,256]{2,1,0:T(8,128)(2,1)S(1)} %get-tuple-element.35), channel_id=1, source_target_pairs={{0,2},{1,3},{2,0},{3,1},{4,6},{5,7},{6,4},{7,5},{8,10},{9,11},{10,... | collective-permute-start | bytes 835592 | tf_op jit(solution)/shard_map/ppermute | solution.py:429
  56.0 1.6 %collective-permute-start.9 = (bf16[2,272,256]{2,1,0:T(8,128)(2,1)S(1)}, bf16[2,272,256]{2,1,0:T(8,128)(2,1)S(1)}, u32[]{:S(2)}, u32[]{:S(2)}) collective-permute-start(bf16[2,272,256]{2,1,0:T(8,128)(2,1)S(1)} %get-tuple-element.36), channel_id=1, source_target_pairs={{0,3},{1,0},{2,1},{3,2},{4,7},{5,4},{6,5},{7,6},{8,11},{9,8},{10,9... | collective-permute-start | bytes 835592 | tf_op jit(solution)/shard_map/ppermute | solution.py:429
  57.6 4.8 %collective-permute-done.7.b = bf16[2,272,256]{2,1,0:T(8,128)(2,1)S(1)} collective-permute-done((bf16[2,272,256]{2,1,0:T(8,128)(2,1)S(1)}, bf16[2,272,256]{2,1,0:T(8,128)(2,1)S(1)}, u32[]{:S(2)}, u32[]{:S(2)}) %collective-permute-start.7) | collective-permute-done | bytes 278560 | tf_op jit(solution)/shard_map/ppermute | solution.py:429
  62.4 3.0 %collective-permute-done.8.c = bf16[2,272,256]{2,1,0:T(8,128)(2,1)S(1)} collective-permute-done((bf16[2,272,256]{2,1,0:T(8,128)(2,1)S(1)}, bf16[2,272,256]{2,1,0:T(8,128)(2,1)S(1)}, u32[]{:S(2)}, u32[]{:S(2)}) %collective-permute-start.8) | collective-permute-done | bytes 278560 | tf_op jit(solution)/shard_map/ppermute | solution.py:429
  65.5 3.7 %collective-permute-done.9.d = bf16[2,272,256]{2,1,0:T(8,128)(2,1)S(1)} collective-permute-done((bf16[2,272,256]{2,1,0:T(8,128)(2,1)S(1)}, bf16[2,272,256]{2,1,0:T(8,128)(2,1)S(1)}, u32[]{:S(2)}, u32[]{:S(2)}) %collective-permute-start.9) | collective-permute-done | bytes 278560 | tf_op jit(solution)/shard_map/ppermute | solution.py:429
  69.2 0.2 gather.1
  69.3 0.1 collective-permute-start.10
  69.4 7.2 %collective-permute-start.11 = (bf16[112,256]{1,0:T(8,128)(2,1)S(1)}, bf16[112,256]{1,0:T(8,128)(2,1)S(1)}, u32[]{:S(2)}, u32[]{:S(2)}) collective-permute-start(bf16[112,256]{1,0:T(8,128)(2,1)S(1)} %get-tuple-element.39), channel_id=1, source_target_pairs={{0,248},{1,249},{2,250},{3,251},{4,252},{5,253},{6,254},{7,255},{8... | collective-permute-start | bytes 172040 | tf_op jit(solution)/shard_map/ppermute | solution.py:438
  76.7 2.7 %collective-permute-start.12 = (bf16[112,256]{1,0:T(8,128)(2,1)S(1)}, bf16[112,256]{1,0:T(8,128)(2,1)S(1)}, u32[]{:S(2)}, u32[]{:S(2)}) collective-permute-start(bf16[112,256]{1,0:T(8,128)(2,1)S(1)} %get-tuple-element.40), channel_id=1, source_target_pairs={{0,252},{1,253},{2,254},{3,255},{4,248},{5,249},{6,250},{7,251},{8... | collective-permute-start | bytes 172040 | tf_op jit(solution)/shard_map/ppermute | solution.py:438
  79.4 1.7 %collective-permute-start.14 = (bf16[48,256]{1,0:T(8,128)(2,1)S(1)}, bf16[48,256]{1,0:T(8,128)(2,1)S(1)}, u32[]{:S(2)}, u32[]{:S(2)}) collective-permute-start(bf16[48,256]{1,0:T(8,128)(2,1)S(1)} %get-tuple-element.42), channel_id=1, source_target_pairs={{0,132},{1,133},{2,134},{3,135},{4,128},{5,129},{6,130},{7,131},{8... | collective-permute-start | bytes 73736 | tf_op jit(solution)/shard_map/ppermute | solution.py:438
  81.0 2.2 %collective-permute-done.13.opp_a = bf16[48,256]{1,0:T(8,128)(2,1)S(1)} collective-permute-done((bf16[48,256]{1,0:T(8,128)(2,1)S(1)}, bf16[48,256]{1,0:T(8,128)(2,1)S(1)}, u32[]{:S(2)}, u32[]{:S(2)}) %collective-permute-start.13) | collective-permute-done | bytes 24608 | tf_op jit(solution)/shard_map/ppermute | solution.py:438
  83.2 1.2 %collective-permute-done.14.opp_b = bf16[48,256]{1,0:T(8,128)(2,1)S(1)} collective-permute-done((bf16[48,256]{1,0:T(8,128)(2,1)S(1)}, bf16[48,256]{1,0:T(8,128)(2,1)S(1)}, u32[]{:S(2)}, u32[]{:S(2)}) %collective-permute-start.14) | collective-permute-done | bytes 24608 | tf_op jit(solution)/shard_map/ppermute | solution.py:438
  84.5 1.3 %final.1 = f32[2,4,32,256]{3,2,1,0:T(8,128)} custom-call(s32[2,4]{1,0:T(2,128)S(1)} %copy-done.5, f32[144,256]{1,0:T(8,128)S(1)} %get-tuple-element.37.keep, bf16[144,256]{1,0:T(8,128)(2,1)S(1)} %collective-permute-done.10.near, bf16[112,256]{1,0:T(8,128)(2,1)S(1)} %collective-permute-done.11.back_a, bf16[112,256]{1,0:T(8,128)(2,1)S(1)} %collective-permute-done.12.back_b, ...), custom_call_target="tpu_custom_call" | custom-call | flops 10000000 | bytes 1048576 | tf_op jit(solution)/shard_map/final/pallas_call | solution.py:165
  (16 shorter events, 0.0 us)
Async XLA Ops:
  3.7 33.1 %copy-start.2 = (bf16[3,256,512]{2,1,0:T(8,128)(2,1)S(1)}, bf16[3,256,512]{2,1,0:T(8,128)(2,1)}, u32[]{:S(2)}) copy-start(bf16[3,256,512]{2,1,0:T(8,128)(2,1)} %constant.5.clone.tab) | copy-start | bytes 2359300
  3.7 14.0 %collective-permute-start = (bf16[2,2,256,256]{3,2,1,0:T(8,128)(2,1)}, bf16[2,2,256,256]{3,2,1,0:T(8,128)(2,1)S(1)}, u32[]{:S(2)}, u32[]{:S(2)}) collective-permute-start(bf16[2,2,256,256]{3,2,1,0:T(8,128)(2,1)} %forward_send.1.sent_a), channel_id=1, source_target_pairs={{0,128},{8,136},{16,144},{24,152},{32,160},{40,168},{48,176},{56,1... | collective-permute-start | bytes 1572872 | tf_op jit(solution)/shard_map/ppermute | solution.py:423
  5.4 1.1 %copy-start.3 = (bf16[2,2,256,256]{3,2,1,0:T(8,128)(2,1)S(1)}, bf16[2,2,256,256]{3,2,1,0:T(8,128)(2,1)}, u32[]{:S(2)}) copy-start(bf16[2,2,256,256]{3,2,1,0:T(8,128)(2,1)} %forward_send.1.sent_a) | copy-start | bytes 1572868
  6.4 30.4 %copy-start.4 = (f32[4]{0:T(128)S(1)}, f32[4]{0:T(128)}, u32[]{:S(2)}) copy-start(f32[4]{0:T(128)} %weight.3) | copy-start | bytes 52
  13.3 71.1 %copy-start.5 = (s32[2,4]{1,0:T(2,128)S(1)}, s32[2,4]{1,0:T(2,128)}, u32[]{:S(2)}) copy-start(s32[2,4]{1,0:T(2,128)} %mask.1) | copy-start | bytes 100
  13.3 17.3 %collective-permute-start.2 = (bf16[4,2,256,256]{3,2,1,0:T(8,128)(2,1)}, bf16[4,2,256,256]{3,2,1,0:T(8,128)(2,1)S(1)}, u32[]{:S(2)}, u32[]{:S(2)}) collective-permute-start(bf16[4,2,256,256]{3,2,1,0:T(8,128)(2,1)} %get-tuple-element.24.e0), channel_id=1, source_target_pairs={{8,0},{16,8},{24,16},{32,24},{40,32},{48,40},{56,48},{64,56},{72,6... | collective-permute-start | bytes 3145736 | tf_op jit(solution)/shard_map/ppermute | solution.py:450
  14.6 14.7 %collective-permute-start.1 = (bf16[2,2,256,256]{3,2,1,0:T(8,128)(2,1)S(1)}, bf16[2,2,256,256]{3,2,1,0:T(8,128)(2,1)S(1)}, u32[]{:S(2)}, u32[]{:S(2)}) collective-permute-start(bf16[2,2,256,256]{3,2,1,0:T(8,128)(2,1)S(1)} %get-tuple-element.26), channel_id=1, source_target_pairs={{0,128},{8,136},{16,144},{24,152},{32,160},{40,168},{48,176},{56,1... | collective-permute-start | bytes 1572872 | tf_op jit(solution)/shard_map/ppermute | solution.py:423
  17.7 13.0 %collective-permute-start.3 = (bf16[2,2,256,256]{3,2,1,0:T(8,128)(2,1)S(1)}, bf16[2,2,256,256]{3,2,1,0:T(8,128)(2,1)S(1)}, u32[]{:S(2)}, u32[]{:S(2)}) collective-permute-start(bf16[2,2,256,256]{3,2,1,0:T(8,128)(2,1)S(1)} %collective-permute-done.op_a), channel_id=1, source_target_pairs={{0,120},{128,248},{1,121},{129,249},{2,122},{130,250},{3,123},{131... | collective-permute-start | bytes 1572872 | tf_op jit(solution)/shard_map/ppermute | solution.py:452
  24.0 18.6 %collective-permute-start.4 = (bf16[4,2,256,256]{3,2,1,0:T(8,128)(2,1)}, bf16[4,2,256,256]{3,2,1,0:T(8,128)(2,1)S(1)}, u32[]{:S(2)}, u32[]{:S(2)}) collective-permute-start(bf16[4,2,256,256]{3,2,1,0:T(8,128)(2,1)} %get-tuple-element.30.e1), channel_id=1, source_target_pairs={{0,8},{8,16},{16,24},{24,32},{32,40},{40,48},{48,56},{56,64},{64,7... | collective-permute-start | bytes 3145736 | tf_op jit(solution)/shard_map/ppermute | solution.py:423
  24.1 18.5 %collective-permute-start.5 = (bf16[4,2,256,256]{3,2,1,0:T(8,128)(2,1)}, bf16[4,2,256,256]{3,2,1,0:T(8,128)(2,1)S(1)}, u32[]{:S(2)}, u32[]{:S(2)}) collective-permute-start(bf16[4,2,256,256]{3,2,1,0:T(8,128)(2,1)} %get-tuple-element.32), channel_id=1, source_target_pairs={{0,248},{8,0},{16,8},{24,16},{32,24},{40,32},{48,40},{56,48},{64,5... | collective-permute-start | bytes 3145736 | tf_op jit(solution)/shard_map/ppermute | solution.py:423
  30.7 16.9 %collective-permute-start.6 = (bf16[2,2,256,256]{3,2,1,0:T(8,128)(2,1)S(1)}, bf16[2,2,256,256]{3,2,1,0:T(8,128)(2,1)S(1)}, u32[]{:S(2)}, u32[]{:S(2)}) collective-permute-start(bf16[2,2,256,256]{3,2,1,0:T(8,128)(2,1)S(1)} %collective-permute-done.1.op_b), channel_id=1, source_target_pairs={{0,120},{128,248},{1,121},{129,249},{2,122},{130,250},{3,123},{131... | collective-permute-start | bytes 1572872 | tf_op jit(solution)/shard_map/ppermute | solution.py:454
  36.8 1.2 %copy-start = (bf16[4,2,256,256]{3,2,1,0:T(8,128)(2,1)S(1)}, bf16[4,2,256,256]{3,2,1,0:T(8,128)(2,1)}, u32[]{:S(2)}) copy-start(bf16[4,2,256,256]{3,2,1,0:T(8,128)(2,1)} %get-tuple-element.24.e0) | copy-start | bytes 3145732
  38.0 1.2 %copy-start.1 = (bf16[4,2,256,256]{3,2,1,0:T(8,128)(2,1)S(1)}, bf16[4,2,256,256]{3,2,1,0:T(8,128)(2,1)}, u32[]{:S(2)}) copy-start(bf16[4,2,256,256]{3,2,1,0:T(8,128)(2,1)} %get-tuple-element.30.e1) | copy-start | bytes 3145732
  52.8 9.6 %collective-permute-start.7 = (bf16[2,272,256]{2,1,0:T(8,128)(2,1)S(1)}, bf16[2,272,256]{2,1,0:T(8,128)(2,1)S(1)}, u32[]{:S(2)}, u32[]{:S(2)}) collective-permute-start(bf16[2,272,256]{2,1,0:T(8,128)(2,1)S(1)} %get-tuple-element.34), channel_id=1, source_target_pairs={{0,1},{1,2},{2,3},{3,0},{4,5},{5,6},{6,7},{7,4},{8,9},{9,10},{10,1... | collective-permute-start | bytes 835592 | tf_op jit(solution)/shard_map/ppermute | solution.py:429
  54.4 11.1 %collective-permute-start.8 = (bf16[2,272,256]{2,1,0:T(8,128)(2,1)S(1)}, bf16[2,272,256]{2,1,0:T(8,128)(2,1)S(1)}, u32[]{:S(2)}, u32[]{:S(2)}) collective-permute-start(bf16[2,272,256]{2,1,0:T(8,128)(2,1)S(1)} %get-tuple-element.35), channel_id=1, source_target_pairs={{0,2},{1,3},{2,0},{3,1},{4,6},{5,7},{6,4},{7,5},{8,10},{9,11},{10,... | collective-permute-start | bytes 835592 | tf_op jit(solution)/shard_map/ppermute | solution.py:429
  56.0 13.2 %collective-permute-start.9 = (bf16[2,272,256]{2,1,0:T(8,128)(2,1)S(1)}, bf16[2,272,256]{2,1,0:T(8,128)(2,1)S(1)}, u32[]{:S(2)}, u32[]{:S(2)}) collective-permute-start(bf16[2,272,256]{2,1,0:T(8,128)(2,1)S(1)} %get-tuple-element.36), channel_id=1, source_target_pairs={{0,3},{1,0},{2,1},{3,2},{4,7},{5,4},{6,5},{7,6},{8,11},{9,8},{10,9... | collective-permute-start | bytes 835592 | tf_op jit(solution)/shard_map/ppermute | solution.py:429
  69.3 15.1 %collective-permute-start.10 = (bf16[144,256]{1,0:T(8,128)(2,1)S(1)}, bf16[144,256]{1,0:T(8,128)(2,1)S(1)}, u32[]{:S(2)}, u32[]{:S(2)}) collective-permute-start(bf16[144,256]{1,0:T(8,128)(2,1)S(1)} %get-tuple-element.38), channel_id=1, source_target_pairs={{0,4},{1,5},{2,6},{3,7},{4,0},{5,1},{6,2},{7,3},{8,12},{9,13},{10,... | collective-permute-start | bytes 221192 | tf_op jit(solution)/shard_map/ppermute | solution.py:438
  69.4 15.0 %collective-permute-start.11 = (bf16[112,256]{1,0:T(8,128)(2,1)S(1)}, bf16[112,256]{1,0:T(8,128)(2,1)S(1)}, u32[]{:S(2)}, u32[]{:S(2)}) collective-permute-start(bf16[112,256]{1,0:T(8,128)(2,1)S(1)} %get-tuple-element.39), channel_id=1, source_target_pairs={{0,248},{1,249},{2,250},{3,251},{4,252},{5,253},{6,254},{7,255},{8... | collective-permute-start | bytes 172040 | tf_op jit(solution)/shard_map/ppermute | solution.py:438
  76.7 7.8 %collective-permute-start.12 = (bf16[112,256]{1,0:T(8,128)(2,1)S(1)}, bf16[112,256]{1,0:T(8,128)(2,1)S(1)}, u32[]{:S(2)}, u32[]{:S(2)}) collective-permute-start(bf16[112,256]{1,0:T(8,128)(2,1)S(1)} %get-tuple-element.40), channel_id=1, source_target_pairs={{0,252},{1,253},{2,254},{3,255},{4,248},{5,249},{6,250},{7,251},{8... | collective-permute-start | bytes 172040 | tf_op jit(solution)/shard_map/ppermute | solution.py:438
  79.4 3.8 %collective-permute-start.13 = (bf16[48,256]{1,0:T(8,128)(2,1)S(1)}, bf16[48,256]{1,0:T(8,128)(2,1)S(1)}, u32[]{:S(2)}, u32[]{:S(2)}) collective-permute-start(bf16[48,256]{1,0:T(8,128)(2,1)S(1)} %get-tuple-element.41), channel_id=1, source_target_pairs={{0,128},{1,129},{2,130},{3,131},{4,132},{5,133},{6,134},{7,135},{8... | collective-permute-start | bytes 73736 | tf_op jit(solution)/shard_map/ppermute | solution.py:438
  79.4 5.1 %collective-permute-start.14 = (bf16[48,256]{1,0:T(8,128)(2,1)S(1)}, bf16[48,256]{1,0:T(8,128)(2,1)S(1)}, u32[]{:S(2)}, u32[]{:S(2)}) collective-permute-start(bf16[48,256]{1,0:T(8,128)(2,1)S(1)} %get-tuple-element.42), channel_id=1, source_target_pairs={{0,132},{1,133},{2,134},{3,135},{4,128},{5,129},{6,130},{7,131},{8... | collective-permute-start | bytes 73736 | tf_op jit(solution)/shard_map/ppermute | solution.py:438

commit v3 on v1

--- a/solution.py
+++ b/solution.py
@@ -277,45 +277,49 @@
     return [jnp.zeros((16, 128), F32)] * count
 
 
-def early_kernel(weight, tab, e0, e1, op_a, op_b, surf, energy_out, cross):
+def early_kernel(weight, tab, e0, e1, q1, op_a, op_b, surf, energy_out, cross):
     lo = place()["lo"] > 0
     energy_out[...] = jnp.zeros_like(energy_out)
 
     def body(row, rowi, lane):
-        acc, energy = zeros(4), zeros(3)
+        acc, energy = zeros(8), zeros(4)
         for p in range(4):
             w = weight[p]
             own0, own1 = load_block(e0, p, row, lane), load_block(e1, p, row, lane)
             opp = load_block((op_a, op_b)[p // 2], p % 2, row, lane)
-            for i, v in enumerate((own0, own1, opp)):
+            prev = load_block(q1, p, row, lane)
+            for i, v in enumerate((own0, own1, opp, prev)):
                 add_energy(energy, i, w, v)
             accumulate(acc, 0, [w * v for v in own0], own1)
             accumulate(acc, 1, [w * v for v in pick(lo, own1, own0)], opp)
-        for i in range(2):
-            cross[i, pl.ds(row, 16), lane] = acc[2 * i].astype(BF)
-            cross[i, pl.ds(rowi, 16), lane] = acc[2 * i + 1].astype(BF)
+            wq = [w * v for v in prev]
+            accumulate(acc, 2, wq, own0)
+            accumulate(acc, 3, wq, own1)
+        for i, at in enumerate((0, 1, 3, 4)):
+            cross[at, pl.ds(row, 16), lane] = acc[2 * i].astype(BF)
+            cross[at, pl.ds(rowi, 16), lane] = acc[2 * i + 1].astype(BF)
         cross[2, pl.ds(row, 16), lane] = acc[2].astype(BF)
         cross[2, pl.ds(rowi, 16), lane] = (-acc[3]).astype(BF)
-        for i in range(3):
+        for i in range(4):
             energy_out[i] += energy[i][:8] + energy[i][8:]
 
     blocks(body)
-    inverse(tab, cross, surf, 3, 0)
+    inverse(tab, cross, surf, 5, 0)
 
 
 def late_kernel(
-    weight, tab, early, energy_in, e0, e1, q1, pl0, pl1, turn_a, turn_b, s0, s1, s2, s3, cross, surf, energy_sum
+    weight, tab, early, energy_in, e0, q1, pl0, pl1, turn_a, turn_b, s0, s1, s2, s3, cross, surf, energy_sum
 ):
     at = place()
     swapped, end = at["last"], at["end"]
-    energy_sum[0:3] = energy_in[...]
-    energy_sum[3:6] = jnp.zeros((3, 8, 128), F32)
+    energy_sum[0:4] = energy_in[...]
+    energy_sum[4:6] = jnp.zeros((2, 8, 128), F32)
 
     def body(row, rowi, lane):
-        acc, energy = zeros(10), zeros(3)
+        acc, energy = zeros(6), zeros(2)
         for p in range(4):
             w = weight[p]
-            own0, own1 = load_block(e0, p, row, lane), load_block(e1, p, row, lane)
+            own0 = load_block(e0, p, row, lane)
             prev = load_block(q1, p, row, lane)
             turned = (turn_a, turn_b)[p // 2]
             a = [
@@ -324,23 +328,23 @@
             ]
             b = load_block(pl1, p, row, lane)
             next0, next1 = pick(swapped, b, a), pick(swapped, a, b)
-            for i, v in enumerate((prev, next0, next1)):
+            for i, v in enumerate((next0, next1)):
                 add_energy(energy, i, w, v)
             w0 = [w * v for v in own0]
             wq = [w * v for v in prev]
             for i, (l, m) in enumerate(
-                ((w0, next0), (w0, next1), (wq, own0), (wq, own1), (wq, next0))
+                ((w0, next0), (w0, next1), (wq, next0))
             ):
                 accumulate(acc, i, l, m)
-        for i in range(5):
+        for i in range(3):
             cross[i, pl.ds(row, 16), lane] = acc[2 * i].astype(BF)
             cross[i, pl.ds(rowi, 16), lane] = acc[2 * i + 1].astype(BF)
-        for i in range(3):
-            energy_sum[3 + i] += energy[i][:8] + energy[i][8:]
+        for i in range(2):
+            energy_sum[4 + i] += energy[i][:8] + energy[i][8:]
 
     blocks(body)
-    surf[0:3] = early[...]
-    inverse(tab, cross, surf, 5, 3)
+    surf[0:5] = early[...]
+    inverse(tab, cross, surf, 3, 5)
     emit(surf, 8, (s0, s1, s2, s3), total_rows(energy_sum, 6))
 
 
@@ -374,9 +378,10 @@
         total = add_parts((a, b, c, d), h)
         erows = energy_rows(sum_energy(total[256:], 6))
         near_out[0:64] = total[0:64].astype(near_out.dtype)
-        near_out[64:128] = total[96:160].astype(near_out.dtype)
+        near_out[64:128] = total[160:224].astype(near_out.dtype)
         near_out[128:] = erows.astype(near_out.dtype)
-        back_out[0:96] = total[160:256].astype(BF)
+        back_out[0:64] = total[96:160].astype(BF)
+        back_out[64:96] = total[224:256].astype(BF)
         back_out[96:] = erows
         opp_out[0:32] = total[64:96].astype(BF)
         opp_out[32:] = erows
@@ -459,17 +464,17 @@
     common = [("s", patch_weight), ("v", inverse_tables)]
     surf, energy = surfaces(
         early_kernel,
-        3,
-        [((3, WIN, WIN), BF), ((3, 8, 128), F32)],
-        common + vm(e0, e1, op_a, op_b),
+        5,
+        [((5, WIN, WIN), BF), ((4, 8, 128), F32)],
+        common + vm(e0, e1, q1, op_a, op_b),
         [],
         "surfaces_early",
     )
     parts = surfaces(
         late_kernel,
-        5,
+        3,
         [((2, 8 * 32 + EROWS, WIN), BF)] * 4,
-        common + vm(surf, energy, e0, e1, q1, pl0, pl1, turn_a, turn_b),
+        common + vm(surf, energy, e0, q1, pl0, pl1, turn_a, turn_b),
         [pltpu.VMEM((8, WIN, WIN), BF), pltpu.VMEM((6, 8, 128), F32)],
         "surfaces_late",
     )

time: 83.9 us -> 87.6 us (1.044)
  starting transfers between devices: 29.2 us -> 33.3 us
    ppermute x4, waiting for transfers between devices: 7.84 us -> 18 us  [over_look(): return lax.ppermute(array, 'look', [(i, to(i)) for i in range(nlook)])]
    ppermute x1, waiting for transfers between devices: 9.9 us -> 0.01 us  [per_device(): turn_b = lax.ppermute(op_b, 'look', edges)]
    ppermute x5, starting transfers between devices: 7.4 us -> 11.5 us  [over_both(): return lax.ppermute(array, ('look', 'swath'), perm)]
    ppermute x5, waiting for transfers between devices: 3.83 us -> 2.79 us  [over_both(): return lax.ppermute(array, ('look', 'swath'), perm)]
  transfers between devices with their start and end apart: 15 -> 15, of which waited for: 9 -> 9; matrix products, arithmetic and copies ran while one was open for 0% -> 0% of each run, Pallas kernels for 12% -> 13%
where the time goes in v3:
time: 87.6 us; the launch traced here: 87.3 us
  starting transfers between devices  33.3 us (38%)
  waiting for transfers between devices  29.8 us (34%)
  Pallas kernels  20.6 us (24%)
  local copies, waits for them, and re-layouts  3.54 us (4%)
    pallas_call x6, Pallas kernels, call(): pl.pallas_call(kernel, out_shape=[jax.ShapeDtypeStruct(s, t) for s, t in...  20.6 us
    ppermute x4, waiting for transfers between devices, over_look(): return lax.ppermute(array, 'look', [(i, to(i)) for i in range(nlook)])  18 us
    ppermute x5, starting transfers between devices, over_both(): return lax.ppermute(array, ('look', 'swath'), perm)  11.5 us
    ppermute x3, waiting for transfers between devices, over_x(): moved.append(lax.ppermute(parts[by], 'swath', perm))  7.66 us
    ppermute x4, starting transfers between devices, over_look(): return lax.ppermute(array, 'look', [(i, to(i)) for i in range(nlook)])  6.83 us
    ppermute x1, starting transfers between devices, per_device(): turn_a = lax.ppermute(op_a, 'look', edges)  6.35 us
    ppermute x3, starting transfers between devices, over_x(): moved.append(lax.ppermute(parts[by], 'swath', perm))  4.86 us
    unnamed x12, local copies, waits for them, and re-layouts  3.54 us
  transfers between devices with their start and end apart: 15, of which 9 were waited for; matrix products, arithmetic and copies ran while one was open for 0% of the time, Pallas kernels for 13%

profile of v3, /device:TPU:2, one launch (start us, length us, event | category | flops | bytes accessed | tf_op | source)
XLA Modules:
  0.0 87.3 jit_solution(2832634041093934378)
XLA Ops:
  0.0 3.7 %forward_send.1.sent_a = bf16[2,2,256,256]{3,2,1,0:T(8,128)(2,1)} custom-call(bf16[2,4,2,512,512]{4,3,2,1,0:T(8,128)(2,1)} %img.3, bf16[32,256,512]{2,1,0:T(8,128)(2,1)} %constant.4.clone.tables), custom_call_target="tpu_custom_call" | custom-call | flops 1200000000 | bytes 1048576 | tf_op jit(solution)/shard_map/forward_send/pallas_call | solution.py:165
  3.7 0.0 copy-start.1
  3.7 1.7 %collective-permute-start.2 = (bf16[2,2,256,256]{3,2,1,0:T(8,128)(2,1)}, bf16[2,2,256,256]{3,2,1,0:T(8,128)(2,1)S(1)}, u32[]{:S(2)}, u32[]{:S(2)}) collective-permute-start(bf16[2,2,256,256]{3,2,1,0:T(8,128)(2,1)} %forward_send.1.sent_a), channel_id=1, source_target_pairs={{0,128},{8,136},{16,144},{24,152},{32,160},{40,168},{48,176},{56,1... | collective-permute-start | bytes 1572872 | tf_op jit(solution)/shard_map/ppermute | solution.py:428
  5.4 1.1 %copy-done.2 = bf16[2,2,256,256]{3,2,1,0:T(8,128)(2,1)S(1)} copy-done((bf16[2,2,256,256]{3,2,1,0:T(8,128)(2,1)S(1)}, bf16[2,2,256,256]{3,2,1,0:T(8,128)(2,1)}, u32[]{:S(2)}) %copy-start.2) | copy-done | bytes 524312
  6.4 6.9 %forward_rest.1 = (bf16[4,2,256,256]{3,2,1,0:T(8,128)(2,1)}, bf16[4,2,256,256]{3,2,1,0:T(8,128)(2,1)}, bf16[4,2,256,256]{3,2,1,0:T(8,128)(2,1)}, bf16[2,2,256,256]{3,2,1,0:T(8,128)(2,1)S(1)}) custom-call(bf16[2,4,2,512,512]{4,3,2,1,0:T(8,128)(2,1)} %img.3, bf16[32,256,512]{2,1,0:T(8,128)(2,1)} %constant.4.clone.tables, bf16[2,2,256,256]{3,2,1,0:T(8,128)(2,1)S(1)} %copy-done.2), custom_call_target="tpu_custom_call" | custom-call | flops 3600000000 | bytes 1048576 | tf_op jit(solution)/shard_map/forward_rest/pallas_call | solution.py:165
  13.3 1.3 %collective-permute-start.1 = (bf16[4,2,256,256]{3,2,1,0:T(8,128)(2,1)}, bf16[4,2,256,256]{3,2,1,0:T(8,128)(2,1)S(1)}, u32[]{:S(2)}, u32[]{:S(2)}) collective-permute-start(bf16[4,2,256,256]{3,2,1,0:T(8,128)(2,1)} %get-tuple-element.24.e0), channel_id=1, source_target_pairs={{8,0},{16,8},{24,16},{32,24},{40,32},{48,40},{56,48},{64,56},{72,6... | collective-permute-start | bytes 3145736 | tf_op jit(solution)/shard_map/ppermute | solution.py:455
  14.6 0.5 collective-permute-start
  15.2 2.5 %collective-permute-done.2.op_a = bf16[2,2,256,256]{3,2,1,0:T(8,128)(2,1)S(1)} collective-permute-done((bf16[2,2,256,256]{3,2,1,0:T(8,128)(2,1)}, bf16[2,2,256,256]{3,2,1,0:T(8,128)(2,1)S(1)}, u32[]{:S(2)}, u32[]{:S(2)}) %collective-permute-start.2) | collective-permute-done | bytes 524320 | tf_op jit(solution)/shard_map/ppermute | solution.py:428
  17.7 6.4 %collective-permute-start.3 = (bf16[2,2,256,256]{3,2,1,0:T(8,128)(2,1)S(1)}, bf16[2,2,256,256]{3,2,1,0:T(8,128)(2,1)S(1)}, u32[]{:S(2)}, u32[]{:S(2)}) collective-permute-start(bf16[2,2,256,256]{3,2,1,0:T(8,128)(2,1)S(1)} %collective-permute-done.2.op_a), channel_id=1, source_target_pairs={{0,120},{128,248},{1,121},{129,249},{2,122},{130,250},{3,123},{131... | collective-permute-start | bytes 1572872 | tf_op jit(solution)/shard_map/ppermute | solution.py:457
  24.0 5.3 %collective-permute-done.op_b = bf16[2,2,256,256]{3,2,1,0:T(8,128)(2,1)S(1)} collective-permute-done((bf16[2,2,256,256]{3,2,1,0:T(8,128)(2,1)S(1)}, bf16[2,2,256,256]{3,2,1,0:T(8,128)(2,1)S(1)}, u32[]{:S(2)}, u32[]{:S(2)}) %collective-permute-start) | collective-permute-done | bytes 524320 | tf_op jit(solution)/shard_map/ppermute | solution.py:428
  29.3 1.3 %collective-permute-done.3.turn_a = bf16[2,2,256,256]{3,2,1,0:T(8,128)(2,1)S(1)} collective-permute-done((bf16[2,2,256,256]{3,2,1,0:T(8,128)(2,1)S(1)}, bf16[2,2,256,256]{3,2,1,0:T(8,128)(2,1)S(1)}, u32[]{:S(2)}, u32[]{:S(2)}) %collective-permute-start.3) | collective-permute-done | bytes 524320 | tf_op jit(solution)/shard_map/ppermute | solution.py:457
  30.7 4.6 %collective-permute-start.5 = (bf16[4,2,256,256]{3,2,1,0:T(8,128)(2,1)}, bf16[4,2,256,256]{3,2,1,0:T(8,128)(2,1)S(1)}, u32[]{:S(2)}, u32[]{:S(2)}) collective-permute-start(bf16[4,2,256,256]{3,2,1,0:T(8,128)(2,1)} %get-tuple-element.32), channel_id=1, source_target_pairs={{0,248},{8,0},{16,8},{24,16},{32,24},{40,32},{48,40},{56,48},{64,5... | collective-permute-start | bytes 3145736 | tf_op jit(solution)/shard_map/ppermute | solution.py:428
  35.3 2.4 %collective-permute-start.6 = (bf16[2,2,256,256]{3,2,1,0:T(8,128)(2,1)S(1)}, bf16[2,2,256,256]{3,2,1,0:T(8,128)(2,1)S(1)}, u32[]{:S(2)}, u32[]{:S(2)}) collective-permute-start(bf16[2,2,256,256]{3,2,1,0:T(8,128)(2,1)S(1)} %collective-permute-done.op_b), channel_id=1, source_target_pairs={{0,120},{128,248},{1,121},{129,249},{2,122},{130,250},{3,123},{131... | collective-permute-start | bytes 1572872 | tf_op jit(solution)/shard_map/ppermute | solution.py:459
  37.7 10.2 %collective-permute-done.4.q1 = bf16[4,2,256,256]{3,2,1,0:T(8,128)(2,1)S(1)} collective-permute-done((bf16[4,2,256,256]{3,2,1,0:T(8,128)(2,1)}, bf16[4,2,256,256]{3,2,1,0:T(8,128)(2,1)S(1)}, u32[]{:S(2)}, u32[]{:S(2)}) %collective-permute-start.4) | collective-permute-done | bytes 1048608 | tf_op jit(solution)/shard_map/ppermute | solution.py:428
  47.9 1.2 %copy-done = bf16[4,2,256,256]{3,2,1,0:T(8,128)(2,1)S(1)} copy-done((bf16[4,2,256,256]{3,2,1,0:T(8,128)(2,1)S(1)}, bf16[4,2,256,256]{3,2,1,0:T(8,128)(2,1)}, u32[]{:S(2)}) %copy-start) | copy-done | bytes 1048600
  49.1 1.2 %copy-done.3 = bf16[4,2,256,256]{3,2,1,0:T(8,128)(2,1)S(1)} copy-done((bf16[4,2,256,256]{3,2,1,0:T(8,128)(2,1)S(1)}, bf16[4,2,256,256]{3,2,1,0:T(8,128)(2,1)}, u32[]{:S(2)}) %copy-start.3) | copy-done | bytes 1048600
  50.4 4.8 %surfaces_early.1 = (bf16[5,256,256]{2,1,0:T(8,128)(2,1)S(1)}, f32[4,8,128]{2,1,0:T(8,128)S(1)}) custom-call(f32[4]{0:T(128)S(1)} %copy-done.4, bf16[3,256,512]{2,1,0:T(8,128)(2,1)S(1)} %copy-done.1, bf16[4,2,256,256]{3,2,1,0:T(8,128)(2,1)S(1)} %copy-done, bf16[4,2,256,256]{3,2,1,0:T(8,128)(2,1)S(1)} %copy-done.3, ...), custom_call_target="tpu_custom_call" | custom-call | flops 1250000000 | bytes 1048576 | tf_op jit(solution)/shard_map/surfaces_early/pallas_call | solution.py:165
  55.2 3.7 %surfaces_late.1 = (bf16[2,272,256]{2,1,0:T(8,128)(2,1)S(1)}, bf16[2,272,256]{2,1,0:T(8,128)(2,1)S(1)}, bf16[2,272,256]{2,1,0:T(8,128)(2,1)S(1)}, bf16[2,272,256]{2,1,0:T(8,128)(2,1)S(1)}) custom-call(f32[4]{0:T(128)S(1)} %copy-done.4, bf16[3,256,512]{2,1,0:T(8,128)(2,1)S(1)} %copy-done.1, bf16[5,256,256]{2,1,0:T(8,128)(2,1)S(1)} %get-tuple-element.29.early, ...), custom_call_target="tpu_custom_call" | custom-call | flops 750000000 | bytes 1048576 | tf_op jit(solution)/shard_map/surfaces_late/pallas_call | solution.py:165
  59.0 1.6 %collective-permute-start.7 = (bf16[2,272,256]{2,1,0:T(8,128)(2,1)S(1)}, bf16[2,272,256]{2,1,0:T(8,128)(2,1)S(1)}, u32[]{:S(2)}, u32[]{:S(2)}) collective-permute-start(bf16[2,272,256]{2,1,0:T(8,128)(2,1)S(1)} %get-tuple-element.34), channel_id=1, source_target_pairs={{0,1},{1,2},{2,3},{3,0},{4,5},{5,6},{6,7},{7,4},{8,9},{9,10},{10,1... | collective-permute-start | bytes 835592 | tf_op jit(solution)/shard_map/ppermute | solution.py:434
  60.5 1.1 %collective-permute-start.8 = (bf16[2,272,256]{2,1,0:T(8,128)(2,1)S(1)}, bf16[2,272,256]{2,1,0:T(8,128)(2,1)S(1)}, u32[]{:S(2)}, u32[]{:S(2)}) collective-permute-start(bf16[2,272,256]{2,1,0:T(8,128)(2,1)S(1)} %get-tuple-element.35), channel_id=1, source_target_pairs={{0,2},{1,3},{2,0},{3,1},{4,6},{5,7},{6,4},{7,5},{8,10},{9,11},{10,... | collective-permute-start | bytes 835592 | tf_op jit(solution)/shard_map/ppermute | solution.py:434
  61.6 2.2 %collective-permute-start.9 = (bf16[2,272,256]{2,1,0:T(8,128)(2,1)S(1)}, bf16[2,272,256]{2,1,0:T(8,128)(2,1)S(1)}, u32[]{:S(2)}, u32[]{:S(2)}) collective-permute-start(bf16[2,272,256]{2,1,0:T(8,128)(2,1)S(1)} %get-tuple-element.36), channel_id=1, source_target_pairs={{0,3},{1,0},{2,1},{3,2},{4,7},{5,4},{6,5},{7,6},{8,11},{9,8},{10,9... | collective-permute-start | bytes 835592 | tf_op jit(solution)/shard_map/ppermute | solution.py:434
  63.8 2.6 %collective-permute-done.7.b = bf16[2,272,256]{2,1,0:T(8,128)(2,1)S(1)} collective-permute-done((bf16[2,272,256]{2,1,0:T(8,128)(2,1)S(1)}, bf16[2,272,256]{2,1,0:T(8,128)(2,1)S(1)}, u32[]{:S(2)}, u32[]{:S(2)}) %collective-permute-start.7) | collective-permute-done | bytes 278560 | tf_op jit(solution)/shard_map/ppermute | solution.py:434
  66.4 2.9 %collective-permute-done.8.c = bf16[2,272,256]{2,1,0:T(8,128)(2,1)S(1)} collective-permute-done((bf16[2,272,256]{2,1,0:T(8,128)(2,1)S(1)}, bf16[2,272,256]{2,1,0:T(8,128)(2,1)S(1)}, u32[]{:S(2)}, u32[]{:S(2)}) %collective-permute-start.8) | collective-permute-done | bytes 278560 | tf_op jit(solution)/shard_map/ppermute | solution.py:434
  69.3 2.2 %collective-permute-done.9.d = bf16[2,272,256]{2,1,0:T(8,128)(2,1)S(1)} collective-permute-done((bf16[2,272,256]{2,1,0:T(8,128)(2,1)S(1)}, bf16[2,272,256]{2,1,0:T(8,128)(2,1)S(1)}, u32[]{:S(2)}, u32[]{:S(2)}) %collective-permute-start.9) | collective-permute-done | bytes 278560 | tf_op jit(solution)/shard_map/ppermute | solution.py:434
  71.5 0.2 gather.1
  71.6 3.0 %collective-permute-start.10 = (bf16[144,256]{1,0:T(8,128)(2,1)S(1)}, bf16[144,256]{1,0:T(8,128)(2,1)S(1)}, u32[]{:S(2)}, u32[]{:S(2)}) collective-permute-start(bf16[144,256]{1,0:T(8,128)(2,1)S(1)} %get-tuple-element.38), channel_id=1, source_target_pairs={{0,4},{1,5},{2,6},{3,7},{4,0},{5,1},{6,2},{7,3},{8,12},{9,13},{10,... | collective-permute-start | bytes 221192 | tf_op jit(solution)/shard_map/ppermute | solution.py:443
  74.6 4.4 %collective-permute-start.11 = (bf16[112,256]{1,0:T(8,128)(2,1)S(1)}, bf16[112,256]{1,0:T(8,128)(2,1)S(1)}, u32[]{:S(2)}, u32[]{:S(2)}) collective-permute-start(bf16[112,256]{1,0:T(8,128)(2,1)S(1)} %get-tuple-element.39), channel_id=1, source_target_pairs={{0,248},{1,249},{2,250},{3,251},{4,252},{5,253},{6,254},{7,255},{8... | collective-permute-start | bytes 172040 | tf_op jit(solution)/shard_map/ppermute | solution.py:443
  79.0 1.9 %collective-permute-start.12 = (bf16[112,256]{1,0:T(8,128)(2,1)S(1)}, bf16[112,256]{1,0:T(8,128)(2,1)S(1)}, u32[]{:S(2)}, u32[]{:S(2)}) collective-permute-start(bf16[112,256]{1,0:T(8,128)(2,1)S(1)} %get-tuple-element.40), channel_id=1, source_target_pairs={{0,252},{1,253},{2,254},{3,255},{4,248},{5,249},{6,250},{7,251},{8... | collective-permute-start | bytes 172040 | tf_op jit(solution)/shard_map/ppermute | solution.py:443
  80.9 2.3 %collective-permute-start.14 = (bf16[48,256]{1,0:T(8,128)(2,1)S(1)}, bf16[48,256]{1,0:T(8,128)(2,1)S(1)}, u32[]{:S(2)}, u32[]{:S(2)}) collective-permute-start(bf16[48,256]{1,0:T(8,128)(2,1)S(1)} %get-tuple-element.42), channel_id=1, source_target_pairs={{0,132},{1,133},{2,134},{3,135},{4,128},{5,129},{6,130},{7,131},{8... | collective-permute-start | bytes 73736 | tf_op jit(solution)/shard_map/ppermute | solution.py:443
  83.2 1.6 %collective-permute-done.13.opp_a = bf16[48,256]{1,0:T(8,128)(2,1)S(1)} collective-permute-done((bf16[48,256]{1,0:T(8,128)(2,1)S(1)}, bf16[48,256]{1,0:T(8,128)(2,1)S(1)}, u32[]{:S(2)}, u32[]{:S(2)}) %collective-permute-start.13) | collective-permute-done | bytes 24608 | tf_op jit(solution)/shard_map/ppermute | solution.py:443
  84.8 1.2 %collective-permute-done.14.opp_b = bf16[48,256]{1,0:T(8,128)(2,1)S(1)} collective-permute-done((bf16[48,256]{1,0:T(8,128)(2,1)S(1)}, bf16[48,256]{1,0:T(8,128)(2,1)S(1)}, u32[]{:S(2)}, u32[]{:S(2)}) %collective-permute-start.14) | collective-permute-done | bytes 24608 | tf_op jit(solution)/shard_map/ppermute | solution.py:443
  86.0 1.3 %final.1 = f32[2,4,32,256]{3,2,1,0:T(8,128)} custom-call(s32[2,4]{1,0:T(2,128)S(1)} %copy-done.5, f32[144,256]{1,0:T(8,128)S(1)} %get-tuple-element.37.keep, bf16[144,256]{1,0:T(8,128)(2,1)S(1)} %collective-permute-done.10.near, bf16[112,256]{1,0:T(8,128)(2,1)S(1)} %collective-permute-done.11.back_a, bf16[112,256]{1,0:T(8,128)(2,1)S(1)} %collective-permute-done.12.back_b, ...), custom_call_target="tpu_custom_call" | custom-call | flops 10000000 | bytes 1048576 | tf_op jit(solution)/shard_map/final/pallas_call | solution.py:165
  (16 shorter events, 0.0 us)
Async XLA Ops:
  3.7 44.2 %copy-start.1 = (bf16[3,256,512]{2,1,0:T(8,128)(2,1)S(1)}, bf16[3,256,512]{2,1,0:T(8,128)(2,1)}, u32[]{:S(2)}) copy-start(bf16[3,256,512]{2,1,0:T(8,128)(2,1)} %constant.5.clone.tab) | copy-start | bytes 2359300
  3.7 14.0 %collective-permute-start.2 = (bf16[2,2,256,256]{3,2,1,0:T(8,128)(2,1)}, bf16[2,2,256,256]{3,2,1,0:T(8,128)(2,1)S(1)}, u32[]{:S(2)}, u32[]{:S(2)}) collective-permute-start(bf16[2,2,256,256]{3,2,1,0:T(8,128)(2,1)} %forward_send.1.sent_a), channel_id=1, source_target_pairs={{0,128},{8,136},{16,144},{24,152},{32,160},{40,168},{48,176},{56,1... | collective-permute-start | bytes 1572872 | tf_op jit(solution)/shard_map/ppermute | solution.py:428
  5.4 1.1 %copy-start.2 = (bf16[2,2,256,256]{3,2,1,0:T(8,128)(2,1)S(1)}, bf16[2,2,256,256]{3,2,1,0:T(8,128)(2,1)}, u32[]{:S(2)}) copy-start(bf16[2,2,256,256]{3,2,1,0:T(8,128)(2,1)} %forward_send.1.sent_a) | copy-start | bytes 1572868
  6.4 41.5 %copy-start.4 = (f32[4]{0:T(128)S(1)}, f32[4]{0:T(128)}, u32[]{:S(2)}) copy-start(f32[4]{0:T(128)} %weight.3) | copy-start | bytes 52
  13.3 72.7 %copy-start.5 = (s32[2,4]{1,0:T(2,128)S(1)}, s32[2,4]{1,0:T(2,128)}, u32[]{:S(2)}) copy-start(s32[2,4]{1,0:T(2,128)} %mask.1) | copy-start | bytes 100
  13.3 16.0 %collective-permute-start.1 = (bf16[4,2,256,256]{3,2,1,0:T(8,128)(2,1)}, bf16[4,2,256,256]{3,2,1,0:T(8,128)(2,1)S(1)}, u32[]{:S(2)}, u32[]{:S(2)}) collective-permute-start(bf16[4,2,256,256]{3,2,1,0:T(8,128)(2,1)} %get-tuple-element.24.e0), channel_id=1, source_target_pairs={{8,0},{16,8},{24,16},{32,24},{40,32},{48,40},{56,48},{64,56},{72,6... | collective-permute-start | bytes 3145736 | tf_op jit(solution)/shard_map/ppermute | solution.py:455
  14.6 14.7 %collective-permute-start = (bf16[2,2,256,256]{3,2,1,0:T(8,128)(2,1)S(1)}, bf16[2,2,256,256]{3,2,1,0:T(8,128)(2,1)S(1)}, u32[]{:S(2)}, u32[]{:S(2)}) collective-permute-start(bf16[2,2,256,256]{3,2,1,0:T(8,128)(2,1)S(1)} %get-tuple-element.26), channel_id=1, source_target_pairs={{0,128},{8,136},{16,144},{24,152},{32,160},{40,168},{48,176},{56,1... | collective-permute-start | bytes 1572872 | tf_op jit(solution)/shard_map/ppermute | solution.py:428
  17.7 13.0 %collective-permute-start.3 = (bf16[2,2,256,256]{3,2,1,0:T(8,128)(2,1)S(1)}, bf16[2,2,256,256]{3,2,1,0:T(8,128)(2,1)S(1)}, u32[]{:S(2)}, u32[]{:S(2)}) collective-permute-start(bf16[2,2,256,256]{3,2,1,0:T(8,128)(2,1)S(1)} %collective-permute-done.2.op_a), channel_id=1, source_target_pairs={{0,120},{128,248},{1,121},{129,249},{2,122},{130,250},{3,123},{131... | collective-permute-start | bytes 1572872 | tf_op jit(solution)/shard_map/ppermute | solution.py:457
  30.7 17.2 %collective-permute-start.4 = (bf16[4,2,256,256]{3,2,1,0:T(8,128)(2,1)}, bf16[4,2,256,256]{3,2,1,0:T(8,128)(2,1)S(1)}, u32[]{:S(2)}, u32[]{:S(2)}) collective-permute-start(bf16[4,2,256,256]{3,2,1,0:T(8,128)(2,1)} %get-tuple-element.28.e1), channel_id=1, source_target_pairs={{0,8},{8,16},{16,24},{24,32},{32,40},{40,48},{48,56},{56,64},{64,7... | collective-permute-start | bytes 3145736 | tf_op jit(solution)/shard_map/ppermute | solution.py:428
  30.7 24.5 %collective-permute-start.5 = (bf16[4,2,256,256]{3,2,1,0:T(8,128)(2,1)}, bf16[4,2,256,256]{3,2,1,0:T(8,128)(2,1)S(1)}, u32[]{:S(2)}, u32[]{:S(2)}) collective-permute-start(bf16[4,2,256,256]{3,2,1,0:T(8,128)(2,1)} %get-tuple-element.32), channel_id=1, source_target_pairs={{0,248},{8,0},{16,8},{24,16},{32,24},{40,32},{48,40},{56,48},{64,5... | collective-permute-start | bytes 3145736 | tf_op jit(solution)/shard_map/ppermute | solution.py:428
  35.3 19.9 %collective-permute-start.6 = (bf16[2,2,256,256]{3,2,1,0:T(8,128)(2,1)S(1)}, bf16[2,2,256,256]{3,2,1,0:T(8,128)(2,1)S(1)}, u32[]{:S(2)}, u32[]{:S(2)}) collective-permute-start(bf16[2,2,256,256]{3,2,1,0:T(8,128)(2,1)S(1)} %collective-permute-done.op_b), channel_id=1, source_target_pairs={{0,120},{128,248},{1,121},{129,249},{2,122},{130,250},{3,123},{131... | collective-permute-start | bytes 1572872 | tf_op jit(solution)/shard_map/ppermute | solution.py:459
  47.9 1.2 %copy-start = (bf16[4,2,256,256]{3,2,1,0:T(8,128)(2,1)S(1)}, bf16[4,2,256,256]{3,2,1,0:T(8,128)(2,1)}, u32[]{:S(2)}) copy-start(bf16[4,2,256,256]{3,2,1,0:T(8,128)(2,1)} %get-tuple-element.24.e0) | copy-start | bytes 3145732
  49.1 1.2 %copy-start.3 = (bf16[4,2,256,256]{3,2,1,0:T(8,128)(2,1)S(1)}, bf16[4,2,256,256]{3,2,1,0:T(8,128)(2,1)}, u32[]{:S(2)}) copy-start(bf16[4,2,256,256]{3,2,1,0:T(8,128)(2,1)} %get-tuple-element.28.e1) | copy-start | bytes 3145732
  59.0 7.5 %collective-permute-start.7 = (bf16[2,272,256]{2,1,0:T(8,128)(2,1)S(1)}, bf16[2,272,256]{2,1,0:T(8,128)(2,1)S(1)}, u32[]{:S(2)}, u32[]{:S(2)}) collective-permute-start(bf16[2,272,256]{2,1,0:T(8,128)(2,1)S(1)} %get-tuple-element.34), channel_id=1, source_target_pairs={{0,1},{1,2},{2,3},{3,0},{4,5},{5,6},{6,7},{7,4},{8,9},{9,10},{10,1... | collective-permute-start | bytes 835592 | tf_op jit(solution)/shard_map/ppermute | solution.py:434
  60.5 8.8 %collective-permute-start.8 = (bf16[2,272,256]{2,1,0:T(8,128)(2,1)S(1)}, bf16[2,272,256]{2,1,0:T(8,128)(2,1)S(1)}, u32[]{:S(2)}, u32[]{:S(2)}) collective-permute-start(bf16[2,272,256]{2,1,0:T(8,128)(2,1)S(1)} %get-tuple-element.35), channel_id=1, source_target_pairs={{0,2},{1,3},{2,0},{3,1},{4,6},{5,7},{6,4},{7,5},{8,10},{9,11},{10,... | collective-permute-start | bytes 835592 | tf_op jit(solution)/shard_map/ppermute | solution.py:434
  61.6 9.8 %collective-permute-start.9 = (bf16[2,272,256]{2,1,0:T(8,128)(2,1)S(1)}, bf16[2,272,256]{2,1,0:T(8,128)(2,1)S(1)}, u32[]{:S(2)}, u32[]{:S(2)}) collective-permute-start(bf16[2,272,256]{2,1,0:T(8,128)(2,1)S(1)} %get-tuple-element.36), channel_id=1, source_target_pairs={{0,3},{1,0},{2,1},{3,2},{4,7},{5,4},{6,5},{7,6},{8,11},{9,8},{10,9... | collective-permute-start | bytes 835592 | tf_op jit(solution)/shard_map/ppermute | solution.py:434
  71.6 14.3 %collective-permute-start.10 = (bf16[144,256]{1,0:T(8,128)(2,1)S(1)}, bf16[144,256]{1,0:T(8,128)(2,1)S(1)}, u32[]{:S(2)}, u32[]{:S(2)}) collective-permute-start(bf16[144,256]{1,0:T(8,128)(2,1)S(1)} %get-tuple-element.38), channel_id=1, source_target_pairs={{0,4},{1,5},{2,6},{3,7},{4,0},{5,1},{6,2},{7,3},{8,12},{9,13},{10,... | collective-permute-start | bytes 221192 | tf_op jit(solution)/shard_map/ppermute | solution.py:443
  74.6 11.4 %collective-permute-start.11 = (bf16[112,256]{1,0:T(8,128)(2,1)S(1)}, bf16[112,256]{1,0:T(8,128)(2,1)S(1)}, u32[]{:S(2)}, u32[]{:S(2)}) collective-permute-start(bf16[112,256]{1,0:T(8,128)(2,1)S(1)} %get-tuple-element.39), channel_id=1, source_target_pairs={{0,248},{1,249},{2,250},{3,251},{4,252},{5,253},{6,254},{7,255},{8... | collective-permute-start | bytes 172040 | tf_op jit(solution)/shard_map/ppermute | solution.py:443
  79.0 6.9 %collective-permute-start.12 = (bf16[112,256]{1,0:T(8,128)(2,1)S(1)}, bf16[112,256]{1,0:T(8,128)(2,1)S(1)}, u32[]{:S(2)}, u32[]{:S(2)}) collective-permute-start(bf16[112,256]{1,0:T(8,128)(2,1)S(1)} %get-tuple-element.40), channel_id=1, source_target_pairs={{0,252},{1,253},{2,254},{3,255},{4,248},{5,249},{6,250},{7,251},{8... | collective-permute-start | bytes 172040 | tf_op jit(solution)/shard_map/ppermute | solution.py:443
  80.9 3.8 %collective-permute-start.13 = (bf16[48,256]{1,0:T(8,128)(2,1)S(1)}, bf16[48,256]{1,0:T(8,128)(2,1)S(1)}, u32[]{:S(2)}, u32[]{:S(2)}) collective-permute-start(bf16[48,256]{1,0:T(8,128)(2,1)S(1)} %get-tuple-element.41), channel_id=1, source_target_pairs={{0,128},{1,129},{2,130},{3,131},{4,132},{5,133},{6,134},{7,135},{8... | collective-permute-start | bytes 73736 | tf_op jit(solution)/shard_map/ppermute | solution.py:443
  80.9 5.0 %collective-permute-start.14 = (bf16[48,256]{1,0:T(8,128)(2,1)S(1)}, bf16[48,256]{1,0:T(8,128)(2,1)S(1)}, u32[]{:S(2)}, u32[]{:S(2)}) collective-permute-start(bf16[48,256]{1,0:T(8,128)(2,1)S(1)} %get-tuple-element.42), channel_id=1, source_target_pairs={{0,132},{1,133},{2,134},{3,135},{4,128},{5,129},{6,130},{7,131},{8... | collective-permute-start | bytes 73736 | tf_op jit(solution)/shard_map/ppermute | solution.py:443

commit v4 on v1

--- a/solution.py
+++ b/solution.py
@@ -16,7 +16,7 @@
 CHUNK = 2
 EROWS = 16
 TABLES = 32
-REST_LIMIT = 52
+REST_LIMIT = 46
 BF = jnp.bfloat16
 F32 = jnp.float32
 

time: 83.9 us -> 83.4 us (level)
  waiting for transfers between devices: 30.2 us -> 35.2 us
  local copies, waits for them, and re-layouts: 3.53 us -> 1.09 us
  Pallas kernels: 20.6 us -> 18.9 us
  starting transfers between devices: 29.2 us -> 27.8 us
    ppermute x1, waiting for transfers between devices: 9.9 us -> 12.5 us  [per_device(): turn_b = lax.ppermute(op_b, 'look', edges)]
    unnamed x12 -> x8, local copies, waits for them, and re-layouts: 3.53 us -> 1.09 us
    ppermute x4, waiting for transfers between devices: 7.84 us -> 9.8 us  [over_look(): return lax.ppermute(array, 'look', [(i, to(i)) for i in range(nlook)])]
    pallas_call x6, Pallas kernels: 20.6 us -> 18.9 us  [call(): pl.pallas_call(kernel, out_shape=[jax.ShapeDtypeStruct(s, t) for s, t in...]
  transfers between devices with their start and end apart: 15 -> 15, of which waited for: 9 -> 9; matrix products, arithmetic and copies ran while one was open for 0% -> 0% of each run, Pallas kernels for 12% -> 10%
where the time goes in v4:
time: 83.4 us; the launch traced here: 83.2 us
  waiting for transfers between devices  35.2 us (42%)
  starting transfers between devices  27.8 us (33%)
  Pallas kernels  18.9 us (23%)
  local copies, waits for them, and re-layouts  1.09 us (1%)
    pallas_call x6, Pallas kernels, call(): pl.pallas_call(kernel, out_shape=[jax.ShapeDtypeStruct(s, t) for s, t in...  18.9 us
    ppermute x1, waiting for transfers between devices, per_device(): turn_b = lax.ppermute(op_b, 'look', edges)  12.5 us
    ppermute x4, waiting for transfers between devices, over_look(): return lax.ppermute(array, 'look', [(i, to(i)) for i in range(nlook)])  9.8 us
    ppermute x5, starting transfers between devices, over_both(): return lax.ppermute(array, ('look', 'swath'), perm)  7.69 us
    ppermute x3, waiting for transfers between devices, over_x(): moved.append(lax.ppermute(parts[by], 'swath', perm))  7.36 us
    ppermute x4, starting transfers between devices, over_look(): return lax.ppermute(array, 'look', [(i, to(i)) for i in range(nlook)])  6.33 us
    ppermute x1, starting transfers between devices, per_device(): turn_a = lax.ppermute(op_a, 'look', edges)  5.56 us
    ppermute x3, starting transfers between devices, over_x(): moved.append(lax.ppermute(parts[by], 'swath', perm))  4.85 us
  transfers between devices with their start and end apart: 15, of which 9 were waited for; matrix products, arithmetic and copies ran while one was open for 0% of the time, Pallas kernels for 10%

profile of v4, /device:TPU:2, one launch (start us, length us, event | category | flops | bytes accessed | tf_op | source)
XLA Modules:
  0.0 83.2 jit_solution(11821883191458327320)
XLA Ops:
  0.0 3.7 %forward_send.1.sent_a = bf16[2,2,256,256]{3,2,1,0:T(8,128)(2,1)} custom-call(bf16[2,4,2,512,512]{4,3,2,1,0:T(8,128)(2,1)} %img.3, bf16[32,256,512]{2,1,0:T(8,128)(2,1)} %constant.4.clone.tables), custom_call_target="tpu_custom_call" | custom-call | flops 1200000000 | bytes 1048576 | tf_op jit(solution)/shard_map/forward_send/pallas_call | solution.py:165
  3.7 0.0 copy-start
  3.7 1.7 %collective-permute-start = (bf16[2,2,256,256]{3,2,1,0:T(8,128)(2,1)}, bf16[2,2,256,256]{3,2,1,0:T(8,128)(2,1)S(1)}, u32[]{:S(2)}, u32[]{:S(2)}) collective-permute-start(bf16[2,2,256,256]{3,2,1,0:T(8,128)(2,1)} %forward_send.1.sent_a), channel_id=1, source_target_pairs={{0,128},{8,136},{16,144},{24,152},{32,160},{40,168},{48,176},{56,1... | collective-permute-start | bytes 1572872 | tf_op jit(solution)/shard_map/ppermute | solution.py:423
  5.4 1.1 %copy-done.1 = bf16[2,2,256,256]{3,2,1,0:T(8,128)(2,1)S(1)} copy-done((bf16[2,2,256,256]{3,2,1,0:T(8,128)(2,1)S(1)}, bf16[2,2,256,256]{3,2,1,0:T(8,128)(2,1)}, u32[]{:S(2)}) %copy-start.1) | copy-done | bytes 524312
  6.4 5.2 %forward_rest.1 = (bf16[4,2,256,256]{3,2,1,0:T(8,128)(2,1)S(1)}, bf16[4,2,256,256]{3,2,1,0:T(8,128)(2,1)S(1)}, bf16[4,2,256,256]{3,2,1,0:T(8,128)(2,1)S(1)}, bf16[2,2,256,256]{3,2,1,0:T(8,128)(2,1)S(1)}) custom-call(bf16[2,4,2,512,512]{4,3,2,1,0:T(8,128)(2,1)} %img.3, bf16[32,256,512]{2,1,0:T(8,128)(2,1)} %constant.4.clone.tables, ...), custom_call_target="tpu_custom_call" | custom-call | flops 3600000000 | bytes 1048576 | tf_op jit(solution)/shard_map/forward_rest/pallas_call | solution.py:165
  11.7 0.0 copy-start.3
  11.7 1.3 %collective-permute-start.2 = (bf16[4,2,256,256]{3,2,1,0:T(8,128)(2,1)S(1)}, bf16[4,2,256,256]{3,2,1,0:T(8,128)(2,1)S(1)}, u32[]{:S(2)}, u32[]{:S(2)}) collective-permute-start(bf16[4,2,256,256]{3,2,1,0:T(8,128)(2,1)S(1)} %get-tuple-element.24.e0), channel_id=1, source_target_pairs={{8,0},{16,8},{24,16},{32,24},{40,32},{48,40},{56,48},{64,56},{72,6... | collective-permute-start | bytes 3145736 | tf_op jit(solution)/shard_map/ppermute | solution.py:450
  13.0 0.5 collective-permute-start.1
  13.5 4.9 %collective-permute-done.op_a = bf16[2,2,256,256]{3,2,1,0:T(8,128)(2,1)S(1)} collective-permute-done((bf16[2,2,256,256]{3,2,1,0:T(8,128)(2,1)}, bf16[2,2,256,256]{3,2,1,0:T(8,128)(2,1)S(1)}, u32[]{:S(2)}, u32[]{:S(2)}) %collective-permute-start) | collective-permute-done | bytes 524320 | tf_op jit(solution)/shard_map/ppermute | solution.py:423
  18.4 5.6 %collective-permute-start.3 = (bf16[2,2,256,256]{3,2,1,0:T(8,128)(2,1)S(1)}, bf16[2,2,256,256]{3,2,1,0:T(8,128)(2,1)S(1)}, u32[]{:S(2)}, u32[]{:S(2)}) collective-permute-start(bf16[2,2,256,256]{3,2,1,0:T(8,128)(2,1)S(1)} %collective-permute-done.op_a), channel_id=1, source_target_pairs={{0,120},{128,248},{1,121},{129,249},{2,122},{130,250},{3,123},{131... | collective-permute-start | bytes 1572872 | tf_op jit(solution)/shard_map/ppermute | solution.py:452
  24.0 4.9 %collective-permute-done.1.op_b = bf16[2,2,256,256]{3,2,1,0:T(8,128)(2,1)S(1)} collective-permute-done((bf16[2,2,256,256]{3,2,1,0:T(8,128)(2,1)S(1)}, bf16[2,2,256,256]{3,2,1,0:T(8,128)(2,1)S(1)}, u32[]{:S(2)}, u32[]{:S(2)}) %collective-permute-start.1) | collective-permute-done | bytes 524320 | tf_op jit(solution)/shard_map/ppermute | solution.py:423
  28.9 1.8 %collective-permute-done.3.turn_a = bf16[2,2,256,256]{3,2,1,0:T(8,128)(2,1)S(1)} collective-permute-done((bf16[2,2,256,256]{3,2,1,0:T(8,128)(2,1)S(1)}, bf16[2,2,256,256]{3,2,1,0:T(8,128)(2,1)S(1)}, u32[]{:S(2)}, u32[]{:S(2)}) %collective-permute-start.3) | collective-permute-done | bytes 524320 | tf_op jit(solution)/shard_map/ppermute | solution.py:452
  30.7 4.1 %collective-permute-start.5 = (bf16[4,2,256,256]{3,2,1,0:T(8,128)(2,1)S(1)}, bf16[4,2,256,256]{3,2,1,0:T(8,128)(2,1)S(1)}, u32[]{:S(2)}, u32[]{:S(2)}) collective-permute-start(bf16[4,2,256,256]{3,2,1,0:T(8,128)(2,1)S(1)} %get-tuple-element.32), channel_id=1, source_target_pairs={{0,248},{8,0},{16,8},{24,16},{32,24},{40,32},{48,40},{56,48},{64,5... | collective-permute-start | bytes 3145736 | tf_op jit(solution)/shard_map/ppermute | solution.py:423
  34.8 2.1 %collective-permute-start.6 = (bf16[2,2,256,256]{3,2,1,0:T(8,128)(2,1)S(1)}, bf16[2,2,256,256]{3,2,1,0:T(8,128)(2,1)S(1)}, u32[]{:S(2)}, u32[]{:S(2)}) collective-permute-start(bf16[2,2,256,256]{3,2,1,0:T(8,128)(2,1)S(1)} %collective-permute-done.1.op_b), channel_id=1, source_target_pairs={{0,120},{128,248},{1,121},{129,249},{2,122},{130,250},{3,123},{131... | collective-permute-start | bytes 1572872 | tf_op jit(solution)/shard_map/ppermute | solution.py:454
  36.9 3.3 %surfaces_early.1 = (bf16[3,256,256]{2,1,0:T(8,128)(2,1)S(1)}, f32[3,8,128]{2,1,0:T(8,128)S(1)}) custom-call(f32[4]{0:T(128)S(1)} %copy-done.2, bf16[3,256,512]{2,1,0:T(8,128)(2,1)S(1)} %copy-done, bf16[4,2,256,256]{3,2,1,0:T(8,128)(2,1)S(1)} %get-tuple-element.24.e0, bf16[4,2,256,256]{3,2,1,0:T(8,128)(2,1)S(1)} %get-tuple-element.30.e1, ...), custom_call_target="tpu_custom_call" | custom-call | flops 750000000 | bytes 1048576 | tf_op jit(solution)/shard_map/surfaces_early/pallas_call | solution.py:165
  40.2 12.5 %collective-permute-done.6.turn_b = bf16[2,2,256,256]{3,2,1,0:T(8,128)(2,1)S(1)} collective-permute-done((bf16[2,2,256,256]{3,2,1,0:T(8,128)(2,1)S(1)}, bf16[2,2,256,256]{3,2,1,0:T(8,128)(2,1)S(1)}, u32[]{:S(2)}, u32[]{:S(2)}) %collective-permute-start.6) | collective-permute-done | bytes 524320 | tf_op jit(solution)/shard_map/ppermute | solution.py:454
  52.7 5.2 %surfaces_late.1 = (bf16[2,272,256]{2,1,0:T(8,128)(2,1)S(1)}, bf16[2,272,256]{2,1,0:T(8,128)(2,1)S(1)}, bf16[2,272,256]{2,1,0:T(8,128)(2,1)S(1)}, bf16[2,272,256]{2,1,0:T(8,128)(2,1)S(1)}) custom-call(f32[4]{0:T(128)S(1)} %copy-done.2, bf16[3,256,512]{2,1,0:T(8,128)(2,1)S(1)} %copy-done, bf16[3,256,256]{2,1,0:T(8,128)(2,1)S(1)} %get-tuple-element.28.early, ...), custom_call_target="tpu_custom_call" | custom-call | flops 1250000000 | bytes 1048576 | tf_op jit(solution)/shard_map/surfaces_late/pallas_call | solution.py:165
  58.0 1.6 %collective-permute-start.7 = (bf16[2,272,256]{2,1,0:T(8,128)(2,1)S(1)}, bf16[2,272,256]{2,1,0:T(8,128)(2,1)S(1)}, u32[]{:S(2)}, u32[]{:S(2)}) collective-permute-start(bf16[2,272,256]{2,1,0:T(8,128)(2,1)S(1)} %get-tuple-element.34), channel_id=1, source_target_pairs={{0,1},{1,2},{2,3},{3,0},{4,5},{5,6},{6,7},{7,4},{8,9},{9,10},{10,1... | collective-permute-start | bytes 835592 | tf_op jit(solution)/shard_map/ppermute | solution.py:429
  59.6 1.1 %collective-permute-start.8 = (bf16[2,272,256]{2,1,0:T(8,128)(2,1)S(1)}, bf16[2,272,256]{2,1,0:T(8,128)(2,1)S(1)}, u32[]{:S(2)}, u32[]{:S(2)}) collective-permute-start(bf16[2,272,256]{2,1,0:T(8,128)(2,1)S(1)} %get-tuple-element.35), channel_id=1, source_target_pairs={{0,2},{1,3},{2,0},{3,1},{4,6},{5,7},{6,4},{7,5},{8,10},{9,11},{10,... | collective-permute-start | bytes 835592 | tf_op jit(solution)/shard_map/ppermute | solution.py:429
  60.7 2.2 %collective-permute-start.9 = (bf16[2,272,256]{2,1,0:T(8,128)(2,1)S(1)}, bf16[2,272,256]{2,1,0:T(8,128)(2,1)S(1)}, u32[]{:S(2)}, u32[]{:S(2)}) collective-permute-start(bf16[2,272,256]{2,1,0:T(8,128)(2,1)S(1)} %get-tuple-element.36), channel_id=1, source_target_pairs={{0,3},{1,0},{2,1},{3,2},{4,7},{5,4},{6,5},{7,6},{8,11},{9,8},{10,9... | collective-permute-start | bytes 835592 | tf_op jit(solution)/shard_map/ppermute | solution.py:429
  62.8 1.8 %collective-permute-done.7.b = bf16[2,272,256]{2,1,0:T(8,128)(2,1)S(1)} collective-permute-done((bf16[2,272,256]{2,1,0:T(8,128)(2,1)S(1)}, bf16[2,272,256]{2,1,0:T(8,128)(2,1)S(1)}, u32[]{:S(2)}, u32[]{:S(2)}) %collective-permute-start.7) | collective-permute-done | bytes 278560 | tf_op jit(solution)/shard_map/ppermute | solution.py:429
  64.6 3.1 %collective-permute-done.8.c = bf16[2,272,256]{2,1,0:T(8,128)(2,1)S(1)} collective-permute-done((bf16[2,272,256]{2,1,0:T(8,128)(2,1)S(1)}, bf16[2,272,256]{2,1,0:T(8,128)(2,1)S(1)}, u32[]{:S(2)}, u32[]{:S(2)}) %collective-permute-start.8) | collective-permute-done | bytes 278560 | tf_op jit(solution)/shard_map/ppermute | solution.py:429
  67.7 2.5 %collective-permute-done.9.d = bf16[2,272,256]{2,1,0:T(8,128)(2,1)S(1)} collective-permute-done((bf16[2,272,256]{2,1,0:T(8,128)(2,1)S(1)}, bf16[2,272,256]{2,1,0:T(8,128)(2,1)S(1)}, u32[]{:S(2)}, u32[]{:S(2)}) %collective-permute-start.9) | collective-permute-done | bytes 278560 | tf_op jit(solution)/shard_map/ppermute | solution.py:429
  70.2 0.2 gather.1
  70.3 3.0 %collective-permute-start.10 = (bf16[144,256]{1,0:T(8,128)(2,1)S(1)}, bf16[144,256]{1,0:T(8,128)(2,1)S(1)}, u32[]{:S(2)}, u32[]{:S(2)}) collective-permute-start(bf16[144,256]{1,0:T(8,128)(2,1)S(1)} %get-tuple-element.38), channel_id=1, source_target_pairs={{0,4},{1,5},{2,6},{3,7},{4,0},{5,1},{6,2},{7,3},{8,12},{9,13},{10,... | collective-permute-start | bytes 221192 | tf_op jit(solution)/shard_map/ppermute | solution.py:438
  73.4 2.0 %collective-permute-start.11 = (bf16[112,256]{1,0:T(8,128)(2,1)S(1)}, bf16[112,256]{1,0:T(8,128)(2,1)S(1)}, u32[]{:S(2)}, u32[]{:S(2)}) collective-permute-start(bf16[112,256]{1,0:T(8,128)(2,1)S(1)} %get-tuple-element.39), channel_id=1, source_target_pairs={{0,248},{1,249},{2,250},{3,251},{4,252},{5,253},{6,254},{7,255},{8... | collective-permute-start | bytes 172040 | tf_op jit(solution)/shard_map/ppermute | solution.py:438
  75.4 0.4 collective-permute-start.12
  75.8 1.0 %collective-permute-start.13 = (bf16[48,256]{1,0:T(8,128)(2,1)S(1)}, bf16[48,256]{1,0:T(8,128)(2,1)S(1)}, u32[]{:S(2)}, u32[]{:S(2)}) collective-permute-start(bf16[48,256]{1,0:T(8,128)(2,1)S(1)} %get-tuple-element.41), channel_id=1, source_target_pairs={{0,128},{1,129},{2,130},{3,131},{4,132},{5,133},{6,134},{7,135},{8... | collective-permute-start | bytes 73736 | tf_op jit(solution)/shard_map/ppermute | solution.py:438
  76.8 1.3 %collective-permute-start.14 = (bf16[48,256]{1,0:T(8,128)(2,1)S(1)}, bf16[48,256]{1,0:T(8,128)(2,1)S(1)}, u32[]{:S(2)}, u32[]{:S(2)}) collective-permute-start(bf16[48,256]{1,0:T(8,128)(2,1)S(1)} %get-tuple-element.42), channel_id=1, source_target_pairs={{0,132},{1,133},{2,134},{3,135},{4,128},{5,129},{6,130},{7,131},{8... | collective-permute-start | bytes 73736 | tf_op jit(solution)/shard_map/ppermute | solution.py:438
  78.0 1.6 %collective-permute-done.13.opp_a = bf16[48,256]{1,0:T(8,128)(2,1)S(1)} collective-permute-done((bf16[48,256]{1,0:T(8,128)(2,1)S(1)}, bf16[48,256]{1,0:T(8,128)(2,1)S(1)}, u32[]{:S(2)}, u32[]{:S(2)}) %collective-permute-start.13) | collective-permute-done | bytes 24608 | tf_op jit(solution)/shard_map/ppermute | solution.py:438
  79.6 2.2 %collective-permute-done.14.opp_b = bf16[48,256]{1,0:T(8,128)(2,1)S(1)} collective-permute-done((bf16[48,256]{1,0:T(8,128)(2,1)S(1)}, bf16[48,256]{1,0:T(8,128)(2,1)S(1)}, u32[]{:S(2)}, u32[]{:S(2)}) %collective-permute-start.14) | collective-permute-done | bytes 24608 | tf_op jit(solution)/shard_map/ppermute | solution.py:438
  81.8 1.3 %final.1 = f32[2,4,32,256]{3,2,1,0:T(8,128)} custom-call(s32[2,4]{1,0:T(2,128)S(1)} %copy-done.3, f32[144,256]{1,0:T(8,128)S(1)} %get-tuple-element.37.keep, bf16[144,256]{1,0:T(8,128)(2,1)S(1)} %collective-permute-done.10.near, bf16[112,256]{1,0:T(8,128)(2,1)S(1)} %collective-permute-done.11.back_a, bf16[112,256]{1,0:T(8,128)(2,1)S(1)} %collective-permute-done.12.back_b, ...), custom_call_target="tpu_custom_call" | custom-call | flops 10000000 | bytes 1048576 | tf_op jit(solution)/shard_map/final/pallas_call | solution.py:165
  (12 shorter events, 0.0 us)
Async XLA Ops:
  3.7 33.2 %copy-start = (bf16[3,256,512]{2,1,0:T(8,128)(2,1)S(1)}, bf16[3,256,512]{2,1,0:T(8,128)(2,1)}, u32[]{:S(2)}) copy-start(bf16[3,256,512]{2,1,0:T(8,128)(2,1)} %constant.5.clone.tab) | copy-start | bytes 2359300
  3.7 14.7 %collective-permute-start = (bf16[2,2,256,256]{3,2,1,0:T(8,128)(2,1)}, bf16[2,2,256,256]{3,2,1,0:T(8,128)(2,1)S(1)}, u32[]{:S(2)}, u32[]{:S(2)}) collective-permute-start(bf16[2,2,256,256]{3,2,1,0:T(8,128)(2,1)} %forward_send.1.sent_a), channel_id=1, source_target_pairs={{0,128},{8,136},{16,144},{24,152},{32,160},{40,168},{48,176},{56,1... | collective-permute-start | bytes 1572872 | tf_op jit(solution)/shard_map/ppermute | solution.py:423
  5.4 1.1 %copy-start.1 = (bf16[2,2,256,256]{3,2,1,0:T(8,128)(2,1)S(1)}, bf16[2,2,256,256]{3,2,1,0:T(8,128)(2,1)}, u32[]{:S(2)}) copy-start(bf16[2,2,256,256]{3,2,1,0:T(8,128)(2,1)} %forward_send.1.sent_a) | copy-start | bytes 1572868
  6.4 30.5 %copy-start.2 = (f32[4]{0:T(128)S(1)}, f32[4]{0:T(128)}, u32[]{:S(2)}) copy-start(f32[4]{0:T(128)} %weight.3) | copy-start | bytes 52
  11.7 70.1 %copy-start.3 = (s32[2,4]{1,0:T(2,128)S(1)}, s32[2,4]{1,0:T(2,128)}, u32[]{:S(2)}) copy-start(s32[2,4]{1,0:T(2,128)} %mask.1) | copy-start | bytes 100
  11.7 19.0 %collective-permute-start.2 = (bf16[4,2,256,256]{3,2,1,0:T(8,128)(2,1)S(1)}, bf16[4,2,256,256]{3,2,1,0:T(8,128)(2,1)S(1)}, u32[]{:S(2)}, u32[]{:S(2)}) collective-permute-start(bf16[4,2,256,256]{3,2,1,0:T(8,128)(2,1)S(1)} %get-tuple-element.24.e0), channel_id=1, source_target_pairs={{8,0},{16,8},{24,16},{32,24},{40,32},{48,40},{56,48},{64,56},{72,6... | collective-permute-start | bytes 3145736 | tf_op jit(solution)/shard_map/ppermute | solution.py:450
  13.0 15.9 %collective-permute-start.1 = (bf16[2,2,256,256]{3,2,1,0:T(8,128)(2,1)S(1)}, bf16[2,2,256,256]{3,2,1,0:T(8,128)(2,1)S(1)}, u32[]{:S(2)}, u32[]{:S(2)}) collective-permute-start(bf16[2,2,256,256]{3,2,1,0:T(8,128)(2,1)S(1)} %get-tuple-element.26), channel_id=1, source_target_pairs={{0,128},{8,136},{16,144},{24,152},{32,160},{40,168},{48,176},{56,1... | collective-permute-start | bytes 1572872 | tf_op jit(solution)/shard_map/ppermute | solution.py:423
  18.4 12.2 %collective-permute-start.3 = (bf16[2,2,256,256]{3,2,1,0:T(8,128)(2,1)S(1)}, bf16[2,2,256,256]{3,2,1,0:T(8,128)(2,1)S(1)}, u32[]{:S(2)}, u32[]{:S(2)}) collective-permute-start(bf16[2,2,256,256]{3,2,1,0:T(8,128)(2,1)S(1)} %collective-permute-done.op_a), channel_id=1, source_target_pairs={{0,120},{128,248},{1,121},{129,249},{2,122},{130,250},{3,123},{131... | collective-permute-start | bytes 1572872 | tf_op jit(solution)/shard_map/ppermute | solution.py:452
  30.7 22.1 %collective-permute-start.4 = (bf16[4,2,256,256]{3,2,1,0:T(8,128)(2,1)S(1)}, bf16[4,2,256,256]{3,2,1,0:T(8,128)(2,1)S(1)}, u32[]{:S(2)}, u32[]{:S(2)}) collective-permute-start(bf16[4,2,256,256]{3,2,1,0:T(8,128)(2,1)S(1)} %get-tuple-element.30.e1), channel_id=1, source_target_pairs={{0,8},{8,16},{16,24},{24,32},{32,40},{40,48},{48,56},{56,64},{64,7... | collective-permute-start | bytes 3145736 | tf_op jit(solution)/shard_map/ppermute | solution.py:423
  30.7 22.1 %collective-permute-start.5 = (bf16[4,2,256,256]{3,2,1,0:T(8,128)(2,1)S(1)}, bf16[4,2,256,256]{3,2,1,0:T(8,128)(2,1)S(1)}, u32[]{:S(2)}, u32[]{:S(2)}) collective-permute-start(bf16[4,2,256,256]{3,2,1,0:T(8,128)(2,1)S(1)} %get-tuple-element.32), channel_id=1, source_target_pairs={{0,248},{8,0},{16,8},{24,16},{32,24},{40,32},{48,40},{56,48},{64,5... | collective-permute-start | bytes 3145736 | tf_op jit(solution)/shard_map/ppermute | solution.py:423
  34.8 17.9 %collective-permute-start.6 = (bf16[2,2,256,256]{3,2,1,0:T(8,128)(2,1)S(1)}, bf16[2,2,256,256]{3,2,1,0:T(8,128)(2,1)S(1)}, u32[]{:S(2)}, u32[]{:S(2)}) collective-permute-start(bf16[2,2,256,256]{3,2,1,0:T(8,128)(2,1)S(1)} %collective-permute-done.1.op_b), channel_id=1, source_target_pairs={{0,120},{128,248},{1,121},{129,249},{2,122},{130,250},{3,123},{131... | collective-permute-start | bytes 1572872 | tf_op jit(solution)/shard_map/ppermute | solution.py:454
  58.0 6.6 %collective-permute-start.7 = (bf16[2,272,256]{2,1,0:T(8,128)(2,1)S(1)}, bf16[2,272,256]{2,1,0:T(8,128)(2,1)S(1)}, u32[]{:S(2)}, u32[]{:S(2)}) collective-permute-start(bf16[2,272,256]{2,1,0:T(8,128)(2,1)S(1)} %get-tuple-element.34), channel_id=1, source_target_pairs={{0,1},{1,2},{2,3},{3,0},{4,5},{5,6},{6,7},{7,4},{8,9},{9,10},{10,1... | collective-permute-start | bytes 835592 | tf_op jit(solution)/shard_map/ppermute | solution.py:429
  59.6 8.2 %collective-permute-start.8 = (bf16[2,272,256]{2,1,0:T(8,128)(2,1)S(1)}, bf16[2,272,256]{2,1,0:T(8,128)(2,1)S(1)}, u32[]{:S(2)}, u32[]{:S(2)}) collective-permute-start(bf16[2,272,256]{2,1,0:T(8,128)(2,1)S(1)} %get-tuple-element.35), channel_id=1, source_target_pairs={{0,2},{1,3},{2,0},{3,1},{4,6},{5,7},{6,4},{7,5},{8,10},{9,11},{10,... | collective-permute-start | bytes 835592 | tf_op jit(solution)/shard_map/ppermute | solution.py:429
  60.7 9.5 %collective-permute-start.9 = (bf16[2,272,256]{2,1,0:T(8,128)(2,1)S(1)}, bf16[2,272,256]{2,1,0:T(8,128)(2,1)S(1)}, u32[]{:S(2)}, u32[]{:S(2)}) collective-permute-start(bf16[2,272,256]{2,1,0:T(8,128)(2,1)S(1)} %get-tuple-element.36), channel_id=1, source_target_pairs={{0,3},{1,0},{2,1},{3,2},{4,7},{5,4},{6,5},{7,6},{8,11},{9,8},{10,9... | collective-permute-start | bytes 835592 | tf_op jit(solution)/shard_map/ppermute | solution.py:429
  70.3 11.5 %collective-permute-start.10 = (bf16[144,256]{1,0:T(8,128)(2,1)S(1)}, bf16[144,256]{1,0:T(8,128)(2,1)S(1)}, u32[]{:S(2)}, u32[]{:S(2)}) collective-permute-start(bf16[144,256]{1,0:T(8,128)(2,1)S(1)} %get-tuple-element.38), channel_id=1, source_target_pairs={{0,4},{1,5},{2,6},{3,7},{4,0},{5,1},{6,2},{7,3},{8,12},{9,13},{10,... | collective-permute-start | bytes 221192 | tf_op jit(solution)/shard_map/ppermute | solution.py:438
  73.4 8.4 %collective-permute-start.11 = (bf16[112,256]{1,0:T(8,128)(2,1)S(1)}, bf16[112,256]{1,0:T(8,128)(2,1)S(1)}, u32[]{:S(2)}, u32[]{:S(2)}) collective-permute-start(bf16[112,256]{1,0:T(8,128)(2,1)S(1)} %get-tuple-element.39), channel_id=1, source_target_pairs={{0,248},{1,249},{2,250},{3,251},{4,252},{5,253},{6,254},{7,255},{8... | collective-permute-start | bytes 172040 | tf_op jit(solution)/shard_map/ppermute | solution.py:438
  75.4 6.4 %collective-permute-start.12 = (bf16[112,256]{1,0:T(8,128)(2,1)S(1)}, bf16[112,256]{1,0:T(8,128)(2,1)S(1)}, u32[]{:S(2)}, u32[]{:S(2)}) collective-permute-start(bf16[112,256]{1,0:T(8,128)(2,1)S(1)} %get-tuple-element.40), channel_id=1, source_target_pairs={{0,252},{1,253},{2,254},{3,255},{4,248},{5,249},{6,250},{7,251},{8... | collective-permute-start | bytes 172040 | tf_op jit(solution)/shard_map/ppermute | solution.py:438
  75.8 3.8 %collective-permute-start.13 = (bf16[48,256]{1,0:T(8,128)(2,1)S(1)}, bf16[48,256]{1,0:T(8,128)(2,1)S(1)}, u32[]{:S(2)}, u32[]{:S(2)}) collective-permute-start(bf16[48,256]{1,0:T(8,128)(2,1)S(1)} %get-tuple-element.41), channel_id=1, source_target_pairs={{0,128},{1,129},{2,130},{3,131},{4,132},{5,133},{6,134},{7,135},{8... | collective-permute-start | bytes 73736 | tf_op jit(solution)/shard_map/ppermute | solution.py:438
  76.8 5.0 %collective-permute-start.14 = (bf16[48,256]{1,0:T(8,128)(2,1)S(1)}, bf16[48,256]{1,0:T(8,128)(2,1)S(1)}, u32[]{:S(2)}, u32[]{:S(2)}) collective-permute-start(bf16[48,256]{1,0:T(8,128)(2,1)S(1)} %get-tuple-element.42), channel_id=1, source_target_pairs={{0,132},{1,133},{2,134},{3,135},{4,128},{5,129},{6,130},{7,131},{8... | collective-permute-start | bytes 73736 | tf_op jit(solution)/shard_map/ppermute | solution.py:438
